TPU v7x, 32 devices: a whole 2x2x4 slice. The times are simulated.
32 devices in a mesh: expert: 4 (over y, x), shard: 8 (over z, core).
Axes of the slice: x: 2, y: 2, z: 4, core: 2. Of those that a mesh axis runs over, the one named last changes fastest.
Arguments:
- tokens: float32 [4, 2048, 1024], P('expert', 'shard'), may hold values from -6 to 6
- block_ids: int32 [4, 2048], P('expert'), may hold values from 0 to 7, never falling along the last dimension, each value on 1 to 512 neighbouring positions
- routes: int32 [4, 2048, 8], P('expert', 'shard'), may hold values from 0 to 31, all different within a row; in each aligned block of 256 rows (0 to 255, 256 to 511, ..., all dimensions but the last counted through in order) at most 80 rows name the same one
- gates: float32 [4, 2048, 8], P('expert', 'shard'), may hold values from 0.3 to 1
- attn_gain: float32 [1024], P(('expert', 'shard')), may hold values from 0.5 to 1.5
- w_query: float32 [1024, 1024], P(('expert', 'shard')), may hold values from -0.1875 to 0.1875
- w_key: float32 [1024, 512], P(('expert', 'shard')), may hold values from -0.1875 to 0.1875
- w_value: float32 [1024, 512], P(('expert', 'shard')), may hold values from -0.1875 to 0.1875
- w_out: float32 [1024, 1024], P(('expert', 'shard')), may hold values from -6 to 6
- moe_gain: float32 [1024], P(('expert', 'shard')), may hold values from 0.5 to 1.5
- w_gate: float32 [32, 1024, 512], P('expert', 'shard'), may hold values from -0.1875 to 0.1875
- w_up: float32 [32, 1024, 512], P('expert', 'shard'), may hold values from -0.1875 to 0.1875
- w_down: float32 [32, 1024, 512], P('expert', 'shard'), may hold values from -0.25 to 0.25
- cotangent: float32 [4, 2048, 1024], P('expert', 'shard'), may hold values from -6 to 6
Outputs:
- output: float32 [4, 2048, 1024], P('expert', 'shard')
- token_grad: float32 [4, 2048, 1024], P('expert', 'shard')
- gate_grad: float32 [4, 2048, 8], P('expert', 'shard')
- attn_gain_grad: float32 [1024], P(('expert', 'shard'))
- w_query_grad: float32 [1024, 1024], P(('expert', 'shard'))
- w_key_grad: float32 [1024, 512], P(('expert', 'shard'))
- w_value_grad: float32 [1024, 512], P(('expert', 'shard'))
- w_out_grad: float32 [1024, 1024], P(('expert', 'shard'))
- moe_gain_grad: float32 [1024], P(('expert', 'shard'))
- w_gate_grad: float32 [32, 1024, 512], P('expert', 'shard')
- w_up_grad: float32 [32, 1024, 512], P('expert', 'shard')
- w_down_grad: float32 [32, 1024, 512], P('expert', 'shard')
Inputs may be any that keep to these rules, and one draw needn't show every extreme that they name: `routes`: each token names 8 different experts. In the rows of one device no expert is named more than 80 times, and in some device's rows one expert is named exactly 80 times. `block_ids`: along each sequence the numbers start at 0, never fall and rise by at most one; each number covers 1 to 512 positions, one exactly 512.
All inputs are finite; a program needn't handle non-finite values.
Results may differ from a plain program's by a relative error of at most 0.023.
Values may be sent and summed in bfloat16 or wider, within the bound.
No kernel may reach another device: no remote copies, remote signals or barrier semaphores. Data moves between devices by JAX's collectives and lax.ppermute only.
A program may use at most 192 MiB of HBM per device.

v0:
```python
import jax
import jax.numpy as jnp
from jax import lax
from jax.sharding import PartitionSpec as P

H = 16
KVH = 8
HD = 64
EXPERTS = 32
TOP = 8
CAP = 80


EPSILON = 1e-06


def rope_tables(length, offset, width):
    half = width // 2
    freqs = 10000.0 ** (-(jnp.arange(half, dtype=jnp.float32) * 2.0 / width))
    places = offset + jnp.arange(length, dtype=jnp.float32)
    angles = places[:, None] * freqs[None, :]
    return (jnp.cos(angles), jnp.sin(angles))


def rotate(value, cosine, sine):
    half = value.shape[-1] // 2
    first = value[..., :half]
    second = value[..., half:]
    cosine = cosine[:, None, :]
    sine = sine[:, None, :]
    return jnp.concatenate(
        [first * cosine - second * sine, second * cosine + first * sine], axis=-1
    )


def unrotate(value, cosine, sine):
    half = value.shape[-1] // 2
    first = value[..., :half]
    second = value[..., half:]
    cosine = cosine[:, None, :]
    sine = sine[:, None, :]
    return jnp.concatenate(
        [first * cosine + second * sine, second * cosine - first * sine], axis=-1
    )


def norm_parts(values, gain):
    inverse = lax.rsqrt(jnp.mean(values * values, axis=-1, keepdims=True) + EPSILON)
    return (inverse, values * inverse * gain)


def norm_back(values, inverse, gain, d_normed):
    scaled = d_normed * gain
    d_gain = jnp.sum(d_normed * values * inverse, axis=0)
    inner = jnp.mean(scaled * values, axis=-1, keepdims=True)
    return (inverse * scaled - values * inverse * inverse * inverse * inner, d_gain)


def sub_rows():
    return 512


def body(
    tokens,
    block_ids,
    routes,
    gates,
    attn_gain,
    w_query,
    w_key,
    w_value,
    w_out,
    moe_gain,
    w_gate,
    w_up,
    w_down,
    cotangent,
):
    length = tokens.shape[1]
    width = tokens.shape[2]
    groups = H // KVH
    scale = HD ** (-0.5)
    n_expert = lax.axis_size("expert")
    local_experts = w_gate.shape[0]
    offset = lax.axis_index("shard") * length
    gathered = (
        lax.all_gather(attn_gain.astype(jnp.bfloat16), ("expert", "shard"), axis=0, tiled=True),
        lax.all_gather(w_query.astype(jnp.bfloat16), ("expert", "shard"), axis=0, tiled=True),
        lax.all_gather(w_key.astype(jnp.bfloat16), ("expert", "shard"), axis=0, tiled=True),
        lax.all_gather(w_value.astype(jnp.bfloat16), ("expert", "shard"), axis=0, tiled=True),
        lax.all_gather(w_out.astype(jnp.bfloat16), ("expert", "shard"), axis=0, tiled=True),
        lax.all_gather(moe_gain.astype(jnp.bfloat16), ("expert", "shard"), axis=0, tiled=True),
    )
    gain_one, query_w, key_w, value_w, out_w, gain_two = gathered
    gain_one = gain_one.astype(jnp.float32)
    gain_two = gain_two.astype(jnp.float32)
    expert_w = (
        lax.all_gather(w_gate.astype(jnp.bfloat16), "shard", axis=1, tiled=True),
        lax.all_gather(w_up.astype(jnp.bfloat16), "shard", axis=1, tiled=True),
        lax.all_gather(w_down.astype(jnp.bfloat16), "shard", axis=1, tiled=True),
    )
    gate_full, up_full, down_full = expert_w
    every_block = block_ids[0]
    seq_length = every_block.shape[0]
    own_blocks = lax.dynamic_slice_in_dim(every_block, offset, length)
    values_in = tokens[0]
    inverse_one, normed = norm_parts(values_in, gain_one)
    normed = normed.astype(jnp.bfloat16)
    query_pre = jnp.dot(normed, query_w, preferred_element_type=jnp.float32)
    key_pre = jnp.dot(normed, key_w, preferred_element_type=jnp.float32)
    value_low = jnp.dot(normed, value_w, preferred_element_type=jnp.float32).astype(jnp.bfloat16)
    cosine, sine = rope_tables(length, offset.astype(jnp.float32), HD)
    query_flat = (
        rotate(query_pre.reshape(length, H, HD), cosine, sine)
        .astype(jnp.bfloat16)
        .reshape(length, H * HD)
    )
    query_low = query_flat.reshape(length, KVH, groups, HD)
    key_low = (
        rotate(key_pre.reshape(length, KVH, HD), cosine, sine)
        .astype(jnp.bfloat16)
        .reshape(length, KVH * HD)
    )
    start_state = (
        jnp.full((KVH, groups, length), -1e30, jnp.float32),
        jnp.zeros((KVH, groups, length), jnp.float32),
        jnp.zeros((KVH, groups, length, HD), jnp.float32),
    )
    key_part = lax.all_gather(key_low, "shard", axis=0, tiled=True)
    value_part = lax.all_gather(value_low, "shard", axis=0, tiled=True)
    piece_rows = key_part.shape[0]
    sub_span = sub_rows()

    def forward_one_sub(number, status):
        running_max, running_sum, summed = status
        first_row = number * sub_span
        keys_sub = lax.dynamic_slice_in_dim(key_part, first_row, sub_span).reshape(
            sub_span, KVH, HD
        )
        values_sub = lax.dynamic_slice_in_dim(value_part, first_row, sub_span).reshape(
            sub_span, KVH, HD
        )
        blocks_sub = lax.dynamic_slice_in_dim(every_block, first_row, sub_span)
        scores = (
            jnp.einsum("tkgd,skd->kgts", query_low, keys_sub, preferred_element_type=jnp.float32)
            * scale
        )
        allowed = blocks_sub[None, :] <= own_blocks[:, None]
        masked = jnp.where(allowed, scores, -1e30)
        new_max = jnp.maximum(running_max, jnp.max(masked, axis=-1))
        weights = jnp.where(allowed, jnp.exp(masked - new_max[..., None]), 0.0)
        factor = jnp.exp(running_max - new_max)
        new_sum = running_sum * factor + jnp.sum(weights, axis=-1)
        new_summed = summed * factor[..., None] + jnp.einsum(
            "kgts,skd->kgtd",
            weights.astype(jnp.bfloat16),
            values_sub,
            preferred_element_type=jnp.float32,
        )
        return (new_max, new_sum, new_summed)

    def forward_compute(status):
        return lax.fori_loop(0, piece_rows // sub_span, forward_one_sub, status)

    needed = every_block[0] <= own_blocks[length - 1]
    final_max, final_sum, final_summed = lax.cond(
        needed, forward_compute, lambda kept_state: kept_state, start_state
    )
    log_sum = final_max + jnp.log(final_sum)
    mixed_full = (final_summed / final_sum[..., None]).transpose(2, 0, 1, 3).reshape(length, H * HD)
    mixed_low = mixed_full.astype(jnp.bfloat16)
    middle = values_in + jnp.dot(mixed_low, out_w, preferred_element_type=jnp.float32)
    inverse_two, normed_two = norm_parts(middle, gain_two)
    normed_two = normed_two.astype(jnp.bfloat16)
    flat_routes = routes[0].reshape(length * TOP)
    matches = (flat_routes[:, None] == jnp.arange(EXPERTS, dtype=jnp.int32)[None, :]).astype(
        jnp.int32
    )
    earlier = jnp.cumsum(matches, axis=0) - matches
    ranks = jnp.sum(earlier * matches, axis=-1)
    slots = flat_routes * CAP + ranks
    token_of = jnp.arange(length * TOP, dtype=jnp.int32) // TOP
    outgoing = jnp.zeros((EXPERTS * CAP, width), jnp.bfloat16).at[slots].set(normed_two[token_of])
    outgoing = outgoing.reshape(n_expert, local_experts * CAP, width)
    received = lax.all_to_all(outgoing, "expert", split_axis=0, concat_axis=0, tiled=True).reshape(
        n_expert, local_experts, CAP, width
    )
    gate_pre = jnp.einsum("nesd,edf->nesf", received, gate_full, preferred_element_type=jnp.float32)
    up_pre = jnp.einsum("nesd,edf->nesf", received, up_full, preferred_element_type=jnp.float32)
    sigmoid_gate = jax.nn.sigmoid(gate_pre)
    activated = gate_pre * sigmoid_gate
    hidden = (activated * up_pre).astype(jnp.bfloat16)
    expert_out = jnp.einsum(
        "nesf,edf->nesd", hidden, down_full, preferred_element_type=jnp.float32
    ).astype(jnp.bfloat16)
    returned = lax.all_to_all(
        expert_out.reshape(n_expert, local_experts * CAP, width),
        "expert",
        split_axis=0,
        concat_axis=0,
        tiled=True,
    ).reshape(EXPERTS * CAP, width)
    picked = returned[slots].reshape(length, TOP, width)
    local_gates = gates[0]
    mixture = jnp.einsum("tkd,tk->td", picked, local_gates, preferred_element_type=jnp.float32)
    output = middle + mixture
    d_output = cotangent[0]
    gate_grad = jnp.einsum("tkd,td->tk", picked, d_output, preferred_element_type=jnp.float32)
    d_rows = (
        (local_gates[:, :, None] * d_output[:, None, :])
        .astype(jnp.bfloat16)
        .reshape(length * TOP, width)
    )
    d_outgoing = jnp.zeros((EXPERTS * CAP, width), jnp.bfloat16).at[slots].set(d_rows)
    d_received = lax.all_to_all(
        d_outgoing.reshape(n_expert, local_experts * CAP, width),
        "expert",
        split_axis=0,
        concat_axis=0,
        tiled=True,
    ).reshape(n_expert, local_experts, CAP, width)
    d_hidden = jnp.einsum(
        "nesd,edf->nesf", d_received, down_full, preferred_element_type=jnp.float32
    )
    d_down = jnp.einsum("nesd,nesf->edf", d_received, hidden, preferred_element_type=jnp.float32)
    d_gate_pre = (
        d_hidden * up_pre * sigmoid_gate * (1.0 + gate_pre * (1.0 - sigmoid_gate))
    ).astype(jnp.bfloat16)
    d_up_pre = (d_hidden * activated).astype(jnp.bfloat16)
    d_gate = jnp.einsum("nesd,nesf->edf", received, d_gate_pre, preferred_element_type=jnp.float32)
    d_up = jnp.einsum("nesd,nesf->edf", received, d_up_pre, preferred_element_type=jnp.float32)
    d_inputs = (
        jnp.einsum("nesf,edf->nesd", d_gate_pre, gate_full, preferred_element_type=jnp.float32)
        + jnp.einsum("nesf,edf->nesd", d_up_pre, up_full, preferred_element_type=jnp.float32)
    ).astype(jnp.bfloat16)
    d_back = lax.all_to_all(
        d_inputs.reshape(n_expert, local_experts * CAP, width),
        "expert",
        split_axis=0,
        concat_axis=0,
        tiled=True,
    ).reshape(EXPERTS * CAP, width)
    d_normed_two = jnp.sum(d_back[slots].reshape(length, TOP, width).astype(jnp.float32), axis=1)
    expert_grads = (
        lax.psum_scatter(
            d_gate.astype(jnp.bfloat16), "shard", scatter_dimension=1, tiled=True
        ).astype(jnp.float32),
        lax.psum_scatter(
            d_up.astype(jnp.bfloat16), "shard", scatter_dimension=1, tiled=True
        ).astype(jnp.float32),
        lax.psum_scatter(
            d_down.astype(jnp.bfloat16), "shard", scatter_dimension=1, tiled=True
        ).astype(jnp.float32),
    )
    d_middle_norm, d_gain_two = norm_back(middle, inverse_two, gain_two, d_normed_two)
    d_middle = d_output + d_middle_norm
    d_branch = d_middle.astype(jnp.bfloat16)
    d_out_w = jnp.einsum("ti,td->id", mixed_low, d_branch, preferred_element_type=jnp.float32)
    d_mixed = jnp.einsum("td,id->ti", d_branch, out_w, preferred_element_type=jnp.float32)
    grad_low = d_mixed.astype(jnp.bfloat16)
    grad_heads = grad_low.reshape(length, KVH, groups, HD)
    delta = jnp.sum(
        (d_mixed.astype(jnp.bfloat16).astype(jnp.float32) * mixed_full).reshape(
            length, KVH, groups, HD
        ),
        axis=-1,
    ).transpose(1, 2, 0)

    def key_terms(keys_sub, values_sub, blocks_sub):
        scores = (
            jnp.einsum("tkgd,skd->kgts", query_low, keys_sub, preferred_element_type=jnp.float32)
            * scale
        )
        allowed = blocks_sub[None, :] <= own_blocks[:, None]
        probs = jnp.where(allowed, jnp.exp(scores - log_sum[..., None]), 0.0)
        d_probs = jnp.einsum(
            "tkgd,skd->kgts", grad_heads, values_sub, preferred_element_type=jnp.float32
        )
        d_scores = (probs * (d_probs - delta[..., None])).astype(jnp.bfloat16)
        d_query_add = scale * jnp.einsum(
            "kgts,skd->kgtd", d_scores, keys_sub, preferred_element_type=jnp.float32
        )
        d_key_sub = scale * jnp.einsum(
            "kgts,tkgd->skd", d_scores, query_low, preferred_element_type=jnp.float32
        )
        d_value_sub = jnp.einsum(
            "kgts,tkgd->skd",
            probs.astype(jnp.bfloat16),
            grad_heads,
            preferred_element_type=jnp.float32,
        )
        return (d_query_add, d_key_sub, d_value_sub)

    zero_query = jnp.zeros((KVH, groups, length, HD), jnp.float32)
    start_back = (
        zero_query,
        jnp.zeros((seq_length, KVH * HD), jnp.float32),
        jnp.zeros((seq_length, KVH * HD), jnp.float32),
    )
    backward_key_part = lax.all_gather(key_low, "shard", axis=0, tiled=True)
    backward_value_part = lax.all_gather(value_low, "shard", axis=0, tiled=True)
    backward_piece_rows = backward_key_part.shape[0]
    backward_sub_span = sub_rows()

    def backward_one_sub(number, status):
        d_query, d_keys, d_values = status
        first_row = number * backward_sub_span
        keys_sub = lax.dynamic_slice_in_dim(
            backward_key_part, first_row, backward_sub_span
        ).reshape(backward_sub_span, KVH, HD)
        values_sub = lax.dynamic_slice_in_dim(
            backward_value_part, first_row, backward_sub_span
        ).reshape(backward_sub_span, KVH, HD)
        blocks_sub = lax.dynamic_slice_in_dim(every_block, first_row, backward_sub_span)
        d_query_add, d_key_sub, d_value_sub = key_terms(keys_sub, values_sub, blocks_sub)
        d_keys = lax.dynamic_update_slice_in_dim(
            d_keys, d_key_sub.reshape(backward_sub_span, KVH * HD), first_row, 0
        )
        d_values = lax.dynamic_update_slice_in_dim(
            d_values, d_value_sub.reshape(backward_sub_span, KVH * HD), first_row, 0
        )
        return (d_query + d_query_add, d_keys, d_values)

    def backward_compute(status):
        return lax.fori_loop(0, backward_piece_rows // backward_sub_span, backward_one_sub, status)

    needed = every_block[0] <= own_blocks[length - 1]
    folded = lax.cond(needed, backward_compute, lambda kept_state: kept_state, start_back)
    d_query = folded[0]
    d_keys, d_values = (
        lax.psum_scatter(
            folded[1].astype(jnp.bfloat16), "shard", scatter_dimension=0, tiled=True
        ).astype(jnp.float32),
        lax.psum_scatter(
            folded[2].astype(jnp.bfloat16), "shard", scatter_dimension=0, tiled=True
        ).astype(jnp.float32),
    )
    d_query_rot = d_query.transpose(2, 0, 1, 3).reshape(length, H, HD)
    d_query_pre = unrotate(d_query_rot, cosine, sine).astype(jnp.bfloat16).reshape(length, H * HD)
    d_key_pre = (
        unrotate(d_keys.reshape(length, KVH, HD), cosine, sine)
        .astype(jnp.bfloat16)
        .reshape(length, KVH * HD)
    )
    d_value_pre = d_values.astype(jnp.bfloat16)
    d_query_w = jnp.einsum("td,ti->di", normed, d_query_pre, preferred_element_type=jnp.float32)
    d_key_w = jnp.einsum("td,ti->di", normed, d_key_pre, preferred_element_type=jnp.float32)
    d_value_w = jnp.einsum("td,ti->di", normed, d_value_pre, preferred_element_type=jnp.float32)
    d_normed = jnp.einsum("ti,di->td", d_query_pre, query_w, preferred_element_type=jnp.float32)
    d_normed = d_normed + jnp.einsum(
        "ti,di->td", d_key_pre, key_w, preferred_element_type=jnp.float32
    )
    d_normed = d_normed + jnp.einsum(
        "ti,di->td", d_value_pre, value_w, preferred_element_type=jnp.float32
    )
    d_input_norm, d_gain_one = norm_back(values_in, inverse_one, gain_one, d_normed)
    token_grad = d_middle + d_input_norm
    attn_grads = (
        lax.psum_scatter(d_gain_one, ("expert", "shard"), scatter_dimension=0, tiled=True),
        lax.psum_scatter(d_query_w, ("expert", "shard"), scatter_dimension=0, tiled=True),
        lax.psum_scatter(d_key_w, ("expert", "shard"), scatter_dimension=0, tiled=True),
        lax.psum_scatter(d_value_w, ("expert", "shard"), scatter_dimension=0, tiled=True),
        lax.psum_scatter(d_out_w, ("expert", "shard"), scatter_dimension=0, tiled=True),
        lax.psum_scatter(d_gain_two, ("expert", "shard"), scatter_dimension=0, tiled=True),
    )
    return (
        output[None],
        token_grad[None],
        gate_grad[None],
        attn_grads[0],
        attn_grads[1],
        attn_grads[2],
        attn_grads[3],
        attn_grads[4],
        attn_grads[5],
        expert_grads[0],
        expert_grads[1],
        expert_grads[2],
    )


def solution(mesh):
    in_specs = (
        P("expert", "shard", None),
        P("expert", None),
        P("expert", "shard", None),
        P("expert", "shard", None),
        P(("expert", "shard")),
        P(("expert", "shard"), None),
        P(("expert", "shard"), None),
        P(("expert", "shard"), None),
        P(("expert", "shard"), None),
        P(("expert", "shard")),
        P("expert", "shard", None),
        P("expert", "shard", None),
        P("expert", "shard", None),
        P("expert", "shard", None),
    )
    out_specs = (
        P("expert", "shard", None),
        P("expert", "shard", None),
        P("expert", "shard", None),
        P(("expert", "shard")),
        P(("expert", "shard"), None),
        P(("expert", "shard"), None),
        P(("expert", "shard"), None),
        P(("expert", "shard"), None),
        P(("expert", "shard")),
        P("expert", "shard", None),
        P("expert", "shard", None),
        P("expert", "shard", None),
    )
    return jax.shard_map(body, mesh=mesh, in_specs=in_specs, out_specs=out_specs, check_vma=False)
```

profile of v0, /device:TPU:0, one launch (start us, length us, event | category | flops | bytes accessed | tf_op | source)
XLA Modules:
  0.0 1758.2 jit_solution(15780797821311640370)
XLA Ops:
  13.7 42.1 %all-reduce.5 = (bf16[1024]{0:T(1024)(128)(2,1)S(1)}, bf16[1024]{0:T(1024)(128)(2,1)S(1)}) all-reduce(bf16[1024]{0:T(1024)(128)(2,1)S(1)} %dynamic-update-slice, bf16[1024]{0:T(1024)(128)(2,1)S(1)} %dynamic-update-slice.1), channel_id=1, replica_groups=mesh['expert'=4,'shard'=8] {'expert','shard'}, use_global_device_ids=true, to_apply=%add | all-reduce | flops 2048 | bytes 8192
  71.1 53.5 %all-gather.16.cloned.1.call-done = bf16[1024,512]{1,0:T(8,128)(2,1)} async-done(((bf16[32,512]{1,0:T(8,128)(2,1)}), bf16[1024,512]{1,0:T(8,128)(2,1)}) %all-gather.16.cloned.1.call-update) | async-done | bytes 1048592 | tf_op jit(solution)/shard_map/all_gather | solution.py:90
  148.6 35.0 %all-gather.14.cloned.1.call-done = bf16[1024,1024]{1,0:T(8,128)(2,1)} async-done(((bf16[32,1024]{1,0:T(8,128)(2,1)}), bf16[1024,1024]{1,0:T(8,128)(2,1)}) %all-gather.14.cloned.1.call-update) | async-done | bytes 2097168 | tf_op jit(solution)/shard_map/all_gather | solution.py:88
  190.1 25.2 %all-gather.12.cloned.1.call-done = bf16[2048,512]{0,1:T(8,128)(2,1)} async-done(((bf16[256,512]{0,1:T(8,128)(2,1)}), bf16[2048,512]{0,1:T(8,128)(2,1)}) %all-gather.12.cloned.1.call-update) | async-done | bytes 2097168 | tf_op jit(solution)/shard_map/all_gather | solution.py:129
  215.4 30.2 %all-gather.18.cloned.1.call-done = bf16[2048,512]{1,0:T(8,128)(2,1)} async-done(((bf16[256,512]{1,0:T(8,128)(2,1)}), bf16[2048,512]{1,0:T(8,128)(2,1)}) %all-gather.18.cloned.1.call-update) | async-done | bytes 2097168 | tf_op jit(solution)/shard_map/all_gather | solution.py:130
  245.6 85.3 %conditional.2 = (f32[8,2,256]{2,1,0:T(2,128)}, f32[8,2,256]{2,1,0:T(2,128)}, f32[8,2,256,64]{2,3,1,0:T(8,128)}, f32[8,2,256]{2,1,0:T(2,128)S(1)}) conditional(s32[]{:T(128)} %bitcast.2, () %tuple.54, (s32[2048]{0:T(1024)S(1)}, s32[256]{0:T(256)S(1)}, bf16[2048,512]{0,1:T(8,128)(2,1)}, bf16[256,8,2,64]{0,3,2,1:T(8,128)(2,1)S(1)}, ...), branch_computations={%region_1.0_spmd, %region_2.7_spmd} | conditional | flops 565071872 | bytes 32808272 | solution.py:166
  245.6 84.1 %while.34 = (s32[]{:T(128)}, f32[8,2,256]{2,1,0:T(2,128)}, f32[8,2,256]{2,1,0:T(2,128)}, f32[8,2,256,64]{2,3,1,0:T(8,128)}, s32[2048]{0:T(1024)S(1)}, /*index=5*...) while((s32[]{:T(128)}, f32[8,2,256]{2,1,0:T(2,128)}, ...), condition=%wide.region_6.6_spmd.clone, body=%wide.region_3.5_spmd.clone.sunk | while | flops 565071872 | bytes 32775360 | solution.py:163
  336.2 27.7 %scatter_custom_fusion = bf16[2560,1024]{1,0:T(8,128)(2,1)} fusion(s32[2048]{0:T(1024)S(1)} %bitcast.373, bf16[256,1024]{1,0:T(8,128)(2,1)S(1)} %multiply_convert_fusion, s32[2048]{0:T(1024)S(1)} %broadcast_clamp_fusion.1, bf16[]{:T(256)} %constant.167.clone.1), kind=kCustom, calls=%fused_computation.89 | custom fusion | bytes 5242882 | tf_op jit(solution)/shard_map/scatter | solution.py:183
  383.1 45.3 %all-to-all-done = bf16[4,640,1024]{2,1,0:T(8,128)(2,1)} async-done(((bf16[4,640,1024]{2,1,0:T(8,128)(2,1)}), bf16[4,640,1024]{2,1,0:T(8,128)(2,1)}, u32[]{:S(2)}, u32[]{:S(2)}) %all-to-all-start) | async-done | bytes 5242912 | tf_op jit(solution)/shard_map/all_to_all | solution.py:185
  444.0 27.0 %all-gather.24.cloned.1.call-done = bf16[8,1024,512]{2,1,0:T(8,128)(2,1)} async-done(((bf16[8,128,512]{2,1,0:T(8,128)(2,1)}), bf16[8,1024,512]{2,1,0:T(8,128)(2,1)}) %all-gather.24.cloned.1.call-update) | async-done | bytes 8388624 | tf_op jit(solution)/shard_map/all_gather | solution.py:99
  492.0 61.2 %all-gather.26.cloned.1.call-done = bf16[8,1024,512]{2,1,0:T(8,128)(2,1)} async-done(((bf16[8,128,512]{2,1,0:T(8,128)(2,1)}), bf16[8,1024,512]{2,1,0:T(8,128)(2,1)}) %all-gather.26.cloned.1.call-update) | async-done | bytes 8388624 | tf_op jit(solution)/shard_map/all_gather | solution.py:100
  604.4 49.2 %all-to-all-done.3 = bf16[4,640,1024]{2,1,0:T(8,128)(2,1)} async-done(((bf16[4,640,1024]{2,1,0:T(8,128)(2,1)}), bf16[4,640,1024]{2,1,0:T(8,128)(2,1)}, u32[]{:S(2)}, u32[]{:S(2)}) %all-to-all-start.3) | async-done | bytes 5242912 | tf_op jit(solution)/shard_map/all_to_all | solution.py:236
  680.4 37.0 %all-to-all-done.1 = bf16[4,640,1024]{2,1,0:T(8,128)(2,1)} async-done(((bf16[4,640,1024]{2,1,0:T(8,128)(2,1)}), bf16[4,640,1024]{2,1,0:T(8,128)(2,1)}, u32[]{:S(2)}, u32[]{:S(2)}) %all-to-all-start.1) | async-done | bytes 5242912 | tf_op jit(solution)/shard_map/all_to_all | solution.py:196
  739.9 109.5 %conditional.3 = (f32[8,2,256,64]{2,3,1,0:T(8,128)}, bf16[2048,512]{0,1:T(8,128)(2,1)}, bf16[2048,512]{0,1:T(8,128)(2,1)}) conditional(s32[]{:T(128)} %bitcast.2, () %tuple.56, (f32[8,2,256]{2,1,0:T(2,128)}, f32[8,2,256]{2,1,0:T(2,128)S(1)}, bf16[256,1024]{1,0:T(8,128)(2,1)S(1)}, s32[2048]{0:T(1024)S(1)}, s32[256]{0:T(256)S(1)}, ...), branch_computations={%region_16.17_spmd, %region_17.20_spmd} | conditional | flops 1364594688 | bytes 74423736 | solution.py:328
  745.3 104.2 %while.35 = (s32[]{:T(128)}, f32[8,2,256,64]{2,3,1,0:T(8,128)}, bf16[2048,512]{0,1:T(8,128)(2,1)}, bf16[2048,512]{0,1:T(8,128)(2,1)}, s32[2048]{0:T(1024)S(1)}, ...) while((s32[]{:T(128)}, f32[8,2,256,64]{2,3,1,0:T(8,128)}, ...), condition=%wide.region_19.19_spmd.clone, body=%wide.region_18.18_spmd.clone.sunk | while | flops 1364590592 | bytes 69131536 | solution.py:325
  895.8 24.6 %reduce-scatter.12.cloned.1.call-done = bf16[256,512]{0,1:T(8,128)(2,1)} async-done(((bf16[2048,512]{0,1:T(8,128)(2,1)}), bf16[256,512]{0,1:T(8,128)(2,1)}) %reduce-scatter.12.cloned.1.call-update) | async-done | bytes 262160 | tf_op jit(solution)/shard_map/reduce_scatter | solution.py:334
  934.6 39.6 %all-reduce.4 = (f32[1024]{0:T(1024)S(1)}, f32[1024]{0:T(1024)S(1)}) all-reduce(f32[1024]{0:T(1024)S(1)} %get-tuple-element.541, f32[1024]{0:T(1024)S(1)} %get-tuple-element.539), channel_id=4, replica_groups=mesh['expert'=4,'shard'=8] {'expert','shard'}, use_global_device_ids=true, to_apply=%region_24.25.clone | all-reduce | flops 2048 | bytes 16384
  978.0 34.0 %reduce-scatter.22.cloned.1.call-done = bf16[8,128,512]{2,1,0:T(8,128)(2,1)} async-done(((bf16[8,1024,512]{2,1,0:T(8,128)(2,1)}), bf16[8,128,512]{2,1,0:T(8,128)(2,1)}) %reduce-scatter.22.cloned.1.call-update) | async-done | bytes 1048592 | tf_op jit(solution)/shard_map/reduce_scatter | solution.py:245
  1014.8 87.5 %reduce-scatter.24.cloned.1.call-done = bf16[8,128,512]{2,1,0:T(8,128)(2,1)} async-done(((bf16[8,1024,512]{2,1,0:T(8,128)(2,1)}), bf16[8,128,512]{2,1,0:T(8,128)(2,1)}) %reduce-scatter.24.cloned.1.call-update) | async-done | bytes 1048592 | tf_op jit(solution)/shard_map/reduce_scatter | solution.py:248
  1105.1 87.3 %reduce-scatter.26.cloned.1.call-done = bf16[8,128,512]{2,1,0:T(8,128)(2,1)} async-done(((bf16[8,1024,512]{2,1,0:T(8,128)(2,1)}), bf16[8,128,512]{2,1,0:T(8,128)(2,1)}) %reduce-scatter.26.cloned.1.call-update) | async-done | bytes 1048592 | tf_op jit(solution)/shard_map/reduce_scatter | solution.py:251
  1195.2 141.0 %reduce-scatter.20.cloned.1.call-done = f32[32,1024]{1,0:T(8,128)} async-done(((f32[1024,1024]{1,0:T(8,128)}), f32[32,1024]{1,0:T(8,128)}) %reduce-scatter.20.cloned.1.call-update) | async-done | bytes 131088 | tf_op jit(solution)/shard_map/reduce_scatter | solution.py:363
  1336.2 136.4 %reduce-scatter.16.cloned.1.call-done = f32[32,512]{1,0:T(8,128)} async-done(((f32[1024,512]{1,0:T(8,128)}), f32[32,512]{1,0:T(8,128)}) %reduce-scatter.16.cloned.1.call-update) | async-done | bytes 65552 | tf_op jit(solution)/shard_map/reduce_scatter | solution.py:361
  1472.6 141.4 %reduce-scatter.14.cloned.1.call-done = f32[32,1024]{1,0:T(8,128)} async-done(((f32[1024,1024]{1,0:T(8,128)}), f32[32,1024]{1,0:T(8,128)}) %reduce-scatter.14.cloned.1.call-update) | async-done | bytes 131088 | tf_op jit(solution)/shard_map/reduce_scatter | solution.py:360
  1614.1 137.0 %reduce-scatter.18.cloned.1.call-done = f32[32,512]{1,0:T(8,128)} async-done(((f32[1024,512]{1,0:T(8,128)}), f32[32,512]{1,0:T(8,128)}) %reduce-scatter.18.cloned.1.call-update) | async-done | bytes 65552 | tf_op jit(solution)/shard_map/reduce_scatter | solution.py:362
  (318 shorter events, 478.1 us)
Async XLA Ops:
  7.2 61.0 %all-gather.10.cloned.1.call-start = ((), (), s32[]{:S(2)}) async-start(), calls=%async_computation.13 | async-start | bytes 1081344 | tf_op jit(solution)/shard_map/all_gather | solution.py:89
  8.8 115.8 %all-gather.16.cloned.1.call-start = ((), (), s32[]{:S(2)}) async-start(), calls=%async_computation.16 | async-start | bytes 1081344 | tf_op jit(solution)/shard_map/all_gather | solution.py:90
  10.3 173.3 %all-gather.14.cloned.1.call-start = ((), (), s32[]{:S(2)}) async-start(), calls=%async_computation.15 | async-start | bytes 2162688 | tf_op jit(solution)/shard_map/all_gather | solution.py:88
  12.0 203.4 %all-gather.12.cloned.1.call-start = ((), (), s32[]{:S(2)}) async-start(), calls=%async_computation.14 | async-start | bytes 2359296 | tf_op jit(solution)/shard_map/all_gather | solution.py:129
  57.4 132.5 %copy-start.19 = (f32[256,32]{0,1:T(8,128)}, f32[256,32]{0,1:T(8,128)S(1)}, u32[]{:S(2)}) copy-start(f32[256,32]{0,1:T(8,128)S(1)} %get-tuple-element.610) | copy-start | bytes 98308
  71.0 174.6 %all-gather.18.cloned.1.call-start = ((), (), s32[]{:S(2)}) async-start(), calls=%async_computation.17 | async-start | bytes 2359296 | tf_op jit(solution)/shard_map/all_gather | solution.py:130
  127.0 206.3 %all-gather.20.cloned.1.call-start = ((), (), s32[]{:S(2)}) async-start(), calls=%async_computation.18 | async-start | bytes 2162688 | tf_op jit(solution)/shard_map/all_gather | solution.py:91
  127.7 305.9 %all-gather.22.cloned.1.call-start = ((), (), s32[]{:S(2)}) async-start(), calls=%async_computation.19 | async-start | bytes 9437184 | tf_op jit(solution)/shard_map/all_gather | solution.py:98
  130.5 340.5 %all-gather.24.cloned.1.call-start = ((), (), s32[]{:S(2)}) async-start(), calls=%async_computation.20 | async-start | bytes 9437184 | tf_op jit(solution)/shard_map/all_gather | solution.py:99
  133.3 420.0 %all-gather.26.cloned.1.call-start = ((), (), s32[]{:S(2)}) async-start(), calls=%async_computation.21 | async-start | bytes 9437184 | tf_op jit(solution)/shard_map/all_gather | solution.py:100
  336.0 344.0 %copy-start.4 = (f32[256,1024]{1,0:T(8,128)}, f32[256,1024]{1,0:T(8,128)S(1)}, u32[]{:S(2)}) copy-start(f32[256,1024]{1,0:T(8,128)S(1)} %get-tuple-element.613) | copy-start | bytes 3145732
  363.9 64.5 %all-to-all-start = ((bf16[4,640,1024]{2,1,0:T(8,128)(2,1)}), bf16[4,640,1024]{2,1,0:T(8,128)(2,1)}, u32[]{:S(2)}, u32[]{:S(2)}) async-start(bf16[4,640,1024]{2,1,0:T(8,128)(2,1)} %bitcast.341), calls=%async_computation | async-start | bytes 10485760 | tf_op jit(solution)/shard_map/all_to_all | solution.py:185
  428.4 63.6 %all-to-all-start.2 = ((bf16[4,640,1024]{2,1,0:T(8,128)(2,1)}), bf16[4,640,1024]{2,1,0:T(8,128)(2,1)}, u32[]{:S(2)}, u32[]{:S(2)}) async-start(bf16[4,640,1024]{2,1,0:T(8,128)(2,1)} %bitcast.340), calls=%async_computation.2 | async-start | bytes 10485760 | tf_op jit(solution)/shard_map/all_to_all | solution.py:215
  589.1 64.6 %all-to-all-start.3 = ((bf16[4,640,1024]{2,1,0:T(8,128)(2,1)}), bf16[4,640,1024]{2,1,0:T(8,128)(2,1)}, u32[]{:S(2)}, u32[]{:S(2)}) async-start(bf16[4,640,1024]{2,1,0:T(8,128)(2,1)} %bitcast.342), calls=%async_computation.3 | async-start | bytes 10485760 | tf_op jit(solution)/shard_map/all_to_all | solution.py:236
  653.7 63.7 %all-to-all-start.1 = ((bf16[4,640,1024]{2,1,0:T(8,128)(2,1)}), bf16[4,640,1024]{2,1,0:T(8,128)(2,1)}, u32[]{:S(2)}, u32[]{:S(2)}) async-start(bf16[4,640,1024]{2,1,0:T(8,128)(2,1)} %bitcast.339), calls=%async_computation.1 | async-start | bytes 10485760 | tf_op jit(solution)/shard_map/all_to_all | solution.py:196
  658.9 229.4 %reduce-scatter.10.cloned.1.call-start = ((), (), s32[]{:S(2)}) async-start(), calls=%async_computation.22 | async-start | bytes 2359296 | tf_op jit(solution)/shard_map/reduce_scatter | solution.py:331
  849.5 71.0 %reduce-scatter.12.cloned.1.call-start = ((), (), s32[]{:S(2)}) async-start(), calls=%async_computation.23 | async-start | bytes 2359296 | tf_op jit(solution)/shard_map/reduce_scatter | solution.py:334
  850.2 161.8 %reduce-scatter.22.cloned.1.call-start = ((), (), s32[]{:S(2)}) async-start(), calls=%async_computation.28 | async-start | bytes 9437184 | tf_op jit(solution)/shard_map/reduce_scatter | solution.py:245
  861.6 240.7 %reduce-scatter.24.cloned.1.call-start = ((), (), s32[]{:S(2)}) async-start(), calls=%async_computation.29 | async-start | bytes 9437184 | tf_op jit(solution)/shard_map/reduce_scatter | solution.py:248
  873.0 319.4 %reduce-scatter.26.cloned.1.call-start = ((), (), s32[]{:S(2)}) async-start(), calls=%async_computation.30 | async-start | bytes 9437184 | tf_op jit(solution)/shard_map/reduce_scatter | solution.py:251
  884.3 451.9 %reduce-scatter.20.cloned.1.call-start = ((), (), s32[]{:S(2)}) async-start(), calls=%async_computation.27 | async-start | bytes 4325376 | tf_op jit(solution)/shard_map/reduce_scatter | solution.py:363
  888.2 584.4 %reduce-scatter.16.cloned.1.call-start = ((), (), s32[]{:S(2)}) async-start(), calls=%async_computation.25 | async-start | bytes 2162688 | tf_op jit(solution)/shard_map/reduce_scatter | solution.py:361
  891.3 722.8 %reduce-scatter.14.cloned.1.call-start = ((), (), s32[]{:S(2)}) async-start(), calls=%async_computation.24 | async-start | bytes 4325376 | tf_op jit(solution)/shard_map/reduce_scatter | solution.py:360
  895.6 855.6 %reduce-scatter.18.cloned.1.call-start = ((), (), s32[]{:S(2)}) async-start(), calls=%async_computation.26 | async-start | bytes 2162688 | tf_op jit(solution)/shard_map/reduce_scatter | solution.py:362
  (36 other events, 814.9 us)
Sparse Core Ops, SparseCore 0:
  11.6 56.5 all-gather.9
  71.8 52.7 all-gather.15
  128.1 55.4 all-gather.13
  185.7 29.6 all-gather.11
  217.4 28.1 all-gather.17
  249.0 56.0 all-gather.19
  307.2 80.8 all-gather.21
  390.4 80.5 all-gather.23
  472.6 80.5 all-gather.25
  849.6 33.4 reduce-scatter.9
  885.9 34.4 reduce-scatter.11
  922.6 89.3 reduce-scatter.21
  1014.3 87.9 reduce-scatter.23
  1104.4 87.9 reduce-scatter.25
  1195.1 141.0 reduce-scatter.19
  1338.9 133.7 reduce-scatter.15
  1475.4 138.5 reduce-scatter.13
  1616.8 134.2 reduce-scatter.17
where the time goes:
time: 1770 us; the launch traced here: 1760 us
  waiting for transfers between devices  1170 us (66%)
  matrix products  253 us (14%)
  local copies, waits for them, and re-layouts  117 us (7%)
  other arithmetic  92.8 us (5%)
  blocking collectives  81.7 us (5%)
  starting transfers between devices  22.1 us (1%)
    reduce_scatter x1, waiting for transfers between devices, body(): lax.psum_scatter(d_query_w, ('expert', 'shard'), scatter_dimension=0, til...  141 us
    reduce_scatter x1, waiting for transfers between devices, body(): lax.psum_scatter(d_out_w, ('expert', 'shard'), scatter_dimension=0, tiled...  141 us
    reduce_scatter x1, waiting for transfers between devices, body(): lax.psum_scatter(d_value_w, ('expert', 'shard'), scatter_dimension=0, til...  137 us
    reduce_scatter x1, waiting for transfers between devices, body(): lax.psum_scatter(d_key_w, ('expert', 'shard'), scatter_dimension=0, tiled...  136 us
    reduce_scatter x1, waiting for transfers between devices, body(): lax.psum_scatter(d_up.astype(jnp.bfloat16), 'shard', scatter_dimension=1,...  87.5 us
    reduce_scatter x1, waiting for transfers between devices, body(): lax.psum_scatter(d_down.astype(jnp.bfloat16), 'shard', scatter_dimension=...  87.3 us
    unnamed x2, blocking collectives  81.7 us
    all_gather x1, waiting for transfers between devices, body(): lax.all_gather(w_down.astype(jnp.bfloat16), 'shard', axis=1, tiled=True)  61.2 us
  transfers between devices with their start and end apart: 22, of which 19 were waited for; matrix products, arithmetic and copies ran while one was open for 17% of the time, Pallas kernels for 0%

commit v1 on v0

v1 whole, which is shorter than its diff:
```python
import functools

import jax
import jax.numpy as jnp
from jax import lax
from jax.experimental import pallas as pl
from jax.experimental.pallas import tpu as pltpu
from jax.sharding import PartitionSpec as P

H = 16
KVH = 8
HD = 64
EXPERTS = 32
TOP = 8
CAP = 80
EPSILON = 1e-06
LANES = 128
PAIRS = KVH // 2
GATE_ROWS = 16

BF = jnp.bfloat16
F32 = jnp.float32
VMEM_BYTES = 56 * 1024 * 1024


def dot(left, right):
    return lax.dot_general(left, right, (((1,), (0,)), ((), ())), preferred_element_type=F32)


def dot_nt(left, right):
    return lax.dot_general(left, right, (((1,), (1,)), ((), ())), preferred_element_type=F32)


def dot_tn(left, right):
    return lax.dot_general(left, right, (((0,), (0,)), ((), ())), preferred_element_type=F32)


def call(kernel, grid, scalars, inputs, in_specs, out_shapes, out_specs, scratch=(), flops=0):
    moved = sum(x.size * x.dtype.itemsize for x in inputs)
    moved += sum(x.size * x.dtype.itemsize for x in jax.tree.leaves(out_shapes))
    return pl.pallas_call(
        kernel,
        grid_spec=pltpu.PrefetchScalarGridSpec(
            num_scalar_prefetch=1,
            grid=grid,
            in_specs=in_specs,
            out_specs=out_specs,
            scratch_shapes=list(scratch),
        ),
        out_shape=out_shapes,
        compiler_params=pltpu.CompilerParams(vmem_limit_bytes=VMEM_BYTES),
        cost_estimate=pl.CostEstimate(flops=int(flops), bytes_accessed=int(moved), transcendentals=0),
    )(scalars, *inputs)


def whole_spec(shape):
    return pl.BlockSpec(tuple(shape), lambda *_: (0,) * len(shape))


def lane_ids(rows):
    return lax.broadcasted_iota(jnp.int32, (rows, LANES), 1)


def swap_halves(tile):
    first = lane_ids(tile.shape[0]) % HD < HD // 2
    return jnp.where(first, pltpu.roll(tile, LANES - HD // 2, 1), pltpu.roll(tile, HD // 2, 1))


def turn(value, cosine, signed_sine, direction):
    tiles = []
    for i in range(value.shape[1] // LANES):
        tile = value[:, i * LANES : (i + 1) * LANES]
        tiles.append(tile * cosine + direction * (swap_halves(tile) * signed_sine))
    return tiles[0] if len(tiles) == 1 else jnp.concatenate(tiles, axis=1)


def row_chunk(ids, r, count):
    return ids[0] ^ r if count > 1 else 0


def z_chunk(ids, r, count):
    return ids[1] ^ r if count > 1 else 0


def half_chunk(ids, h, count):
    return ids[2] ^ h if count > 1 else 0


def span(index, size):
    return pl.ds(pl.multiple_of(index * size, size), size)


def qkv_kernel(nr, nh, ids, rows_ref, gain_ref, cos_ref, sin_ref, *rest):
    weights = rest[: nr * nh]
    q_ref, k_ref, v_ref, normed_ref = rest[nr * nh :]
    width = rows_ref.shape[-1]
    chunk = width // nr
    qn, kn = H * HD // nh, KVH * HD // nh
    normed_ref[...] = (rows_ref[0].astype(F32) * gain_ref[...]).astype(BF)
    cosine, sine = cos_ref[...], sin_ref[...]
    for h in range(nh):
        total = None
        for r in range(nr):
            part = dot(
                normed_ref[:, span(row_chunk(ids, r, nr), chunk)],
                weights[r * nh + h][:, qn : qn + 2 * kn],
            )
            total = part if total is None else total + part
        here = span(half_chunk(ids, h, nh), kn)
        k_ref[:, here] = turn(total[:, :kn], cosine, sine, 1.0).astype(BF)
        v_ref[:, here] = total[:, kn:].astype(BF)

    @pl.when(pl.program_id(0) == 0)
    def _():
        for h in range(nh):
            total = None
            for r in range(nr):
                part = dot(
                    normed_ref[:, span(row_chunk(ids, r, nr), chunk)], weights[r * nh + h][:, :qn]
                )
                total = part if total is None else total + part
            turned = turn(total, cosine, sine, 1.0).astype(BF).astype(F32) * HD**-0.5
            q_ref[:, span(half_chunk(ids, h, nh), qn)] = turned.astype(BF)


def project(ids, rows, gain, cosine, sine, weights):
    slots, length, width = rows.shape
    nr, nh = len(weights), len(weights[0])
    flat = [w for row in weights for w in row]
    return call(
        functools.partial(qkv_kernel, nr, nh),
        (slots,),
        ids,
        [rows, gain, cosine, sine, *flat],
        [
            pl.BlockSpec((1, length, width), lambda i, _: (i, 0, 0)),
            whole_spec(gain.shape),
            pl.BlockSpec((length, LANES), lambda i, _: (i, 0)),
            pl.BlockSpec((length, LANES), lambda i, _: (i, 0)),
            *[whole_spec(w.shape) for w in flat],
        ],
        [
            jax.ShapeDtypeStruct((length, H * HD), BF),
            jax.ShapeDtypeStruct((slots * length, KVH * HD), BF),
            jax.ShapeDtypeStruct((slots * length, KVH * HD), BF),
        ],
        [
            whole_spec((length, H * HD)),
            pl.BlockSpec((length, KVH * HD), lambda i, _: (i, 0)),
            pl.BlockSpec((length, KVH * HD), lambda i, _: (i, 0)),
        ],
        [pltpu.VMEM((length, width), BF)],
        2 * slots * length * width * 2 * KVH * HD,
    )


def to_half(tile, which, wanted):
    if which != wanted:
        tile = pltpu.roll(tile, HD, 1)
    return jnp.where(lane_ids(tile.shape[0]) // HD == wanted, tile, 0.0)


def attend_kernel(ids, q_ref, k_ref, v_ref, kx_ref, qx_ref, o_ref, low_ref, lse_ref):
    keys = jnp.concatenate([k_ref[...], kx_ref[...]], axis=1)
    values = v_ref[...]
    extra = qx_ref[...]
    rows = q_ref.shape[0]
    lanes = lane_ids(rows)
    sums = jnp.zeros((rows, LANES), F32)
    for t in range(2):
        tile = q_ref[:, t * LANES : (t + 1) * LANES].astype(F32)
        mixed = jnp.zeros((rows, LANES), F32)
        for w in range(2):
            query = jnp.concatenate([to_half(tile, w, t).astype(BF), extra], axis=1)
            scores = dot_nt(query, keys)
            highest = jnp.max(scores, axis=1, keepdims=True)
            weights = jnp.exp(scores - highest)
            total = jnp.sum(weights, axis=1, keepdims=True)
            out = dot(weights.astype(BF), values) / total
            mixed = mixed + to_half(out, t, w)
            sums = jnp.where(lanes == 2 * t + w, highest + jnp.log(total), sums)
        o_ref[:, t * LANES : (t + 1) * LANES] = mixed
        low_ref[:, t * LANES : (t + 1) * LANES] = mixed.astype(BF)
    lse_ref[0] = sums


def attend(ids, q, k, v, key_extra, query_extra):
    length, keys = q.shape[0], k.shape[0]
    quad = pl.BlockSpec((length, 2 * LANES), lambda p, _: (0, p))
    pair = pl.BlockSpec((keys, LANES), lambda p, _: (0, p))
    return call(
        attend_kernel,
        (PAIRS,),
        ids,
        [q, k, v, key_extra, query_extra],
        [quad, pair, pair, whole_spec(key_extra.shape), whole_spec(query_extra.shape)],
        [
            jax.ShapeDtypeStruct((length, H * HD), F32),
            jax.ShapeDtypeStruct((length, H * HD), BF),
            jax.ShapeDtypeStruct((PAIRS, length, LANES), F32),
        ],
        [quad, quad, pl.BlockSpec((1, length, LANES), lambda p, _: (p, 0, 0))],
        (),
        H * length * keys * (2 * LANES + LANES) * 2,
    )


def three_parts(value):
    high = value.astype(BF)
    rest = value - high.astype(F32)
    middle = rest.astype(BF)
    return high.astype(F32), middle.astype(F32), (rest - middle.astype(F32))


def with_parts(base, value, lanes):
    high, middle, low = three_parts(value)
    base = jnp.where(lanes == 16, high, base)
    base = jnp.where(lanes == 17, middle, base)
    return jnp.where(lanes == 18, low, base).astype(BF)


def attend_back_kernel(
    span_rows, ids, q_ref, do_ref, o_ref, lse_ref, k_ref, v_ref, kx_ref, qx_ref, cos_ref, sin_ref,
    dq_ref, dk_ref, dv_ref, sum_ref,
):
    rows = q_ref.shape[0]
    lanes = lane_ids(rows)
    extra = qx_ref[...].astype(F32)
    nothing = jnp.zeros((rows, LANES), F32)
    sums = lse_ref[0]
    queries, outs, pads_q, pads_o = [], [], [], []
    for t in range(2):
        at = slice(t * LANES, (t + 1) * LANES)
        tile, grad = q_ref[:, at].astype(F32), do_ref[:, at].astype(F32)
        product = grad * o_ref[:, at]
        for w in range(2):
            here = lanes // HD == w
            delta = jnp.sum(jnp.where(here, product, 0.0), axis=1, keepdims=True)
            log_sum = jnp.sum(jnp.where(lanes == 2 * t + w, sums, 0.0), axis=1, keepdims=True)
            q_pad = to_half(tile, w, t).astype(BF)
            o_pad = to_half(grad, w, t).astype(BF)
            queries.append(jnp.concatenate([q_pad, with_parts(extra, -log_sum, lanes)], axis=1))
            outs.append(jnp.concatenate([o_pad, with_parts(nothing, -delta, lanes)], axis=1))
            pads_q.append(q_pad)
            pads_o.append(o_pad)
    all_q = jnp.concatenate(pads_q, axis=0)
    all_o = jnp.concatenate(pads_o, axis=0)
    sum_ref[...] = jnp.zeros_like(sum_ref)

    def one_span(i, _):
        at = pl.ds(pl.multiple_of(i * span_rows, span_rows), span_rows)
        k_here, x_here = k_ref[at, :], kx_ref[at, :]
        keys = jnp.concatenate([k_here, x_here], axis=1)
        values = jnp.concatenate([v_ref[at, :], x_here], axis=1)
        probs, d_scores = [], []
        for n in range(4):
            prob = jnp.exp(dot_nt(keys, queries[n]))
            d_score = (prob * dot_nt(values, outs[n])).astype(BF)
            probs.append(prob.astype(BF))
            d_scores.append(d_score)
            sum_ref[n] += dot_tn(d_score, k_here)
        dv_ref[at, :] = dot(jnp.concatenate(probs, axis=1), all_o).astype(BF)
        d_key = dot(jnp.concatenate(d_scores, axis=1), all_q)
        dk_ref[at, :] = turn(d_key, cos_ref[at, :], sin_ref[at, :], -1.0).astype(BF)
        return 0

    lax.fori_loop(0, k_ref.shape[0] // span_rows, one_span, 0)
    cosine, sine = cos_ref[:rows, :], sin_ref[:rows, :]
    for t in range(2):
        tile = to_half(sum_ref[2 * t], t, 0) + to_half(sum_ref[2 * t + 1], t, 1)
        turned = turn(tile * HD**-0.5, cosine, sine, -1.0)
        dq_ref[:, t * LANES : (t + 1) * LANES] = turned.astype(BF)


def attend_back(ids, q, d_out, out, lse, k, v, key_extra, query_extra, cosine, sine):
    length, keys = q.shape[0], k.shape[0]
    quad = pl.BlockSpec((length, 2 * LANES), lambda p, _: (0, p))
    pair = pl.BlockSpec((keys, LANES), lambda p, _: (0, p))
    return call(
        functools.partial(attend_back_kernel, 512),
        (PAIRS,),
        ids,
        [q, d_out, out, lse, k, v, key_extra, query_extra, cosine, sine],
        [
            quad,
            quad,
            quad,
            pl.BlockSpec((1, length, LANES), lambda p, _: (p, 0, 0)),
            pair,
            pair,
            whole_spec(key_extra.shape),
            whole_spec(query_extra.shape),
            whole_spec(cosine.shape),
            whole_spec(sine.shape),
        ],
        [
            jax.ShapeDtypeStruct((length, H * HD), BF),
            jax.ShapeDtypeStruct((keys, KVH * HD), BF),
            jax.ShapeDtypeStruct((keys, KVH * HD), BF),
        ],
        [quad, pair, pair],
        [pltpu.VMEM((4, length, LANES), F32)],
        H * length * keys * 2 * (4 * LANES + 3 * LANES),
    )


def out_kernel(nr, nh, ids, x_ref, o_ref, gain_ref, *rest):
    weights = rest[: nr * nh]
    x2_ref, n2_ref = rest[nr * nh :]
    width = x_ref.shape[1]
    chunk, cols = H * HD // nr, width // nh
    for h in range(nh):
        at = span(half_chunk(ids, h, nh), cols)
        total = x_ref[:, at]
        for r in range(nr):
            total = total + dot(
                o_ref[:, span(row_chunk(ids, r, nr), chunk)], weights[r * nh + h][:, :cols]
            )
        x2_ref[:, at] = total
    middle = x2_ref[...]
    inverse = lax.rsqrt(jnp.mean(middle * middle, axis=1, keepdims=True) + EPSILON)
    n2_ref[...] = (middle * inverse * gain_ref[...]).astype(BF)


def project_out(ids, x, low, gain, weights):
    nr, nh = len(weights), len(weights[0])
    flat = [w for row in weights for w in row]
    ins = [x, low, gain, *flat]
    outs = [jax.ShapeDtypeStruct(x.shape, F32), jax.ShapeDtypeStruct(x.shape, BF)]
    return call(
        functools.partial(out_kernel, nr, nh),
        (1,),
        ids,
        ins,
        [whole_spec(i.shape) for i in ins],
        outs,
        [whole_spec(o.shape) for o in outs],
        (),
        2 * x.shape[0] * x.shape[1] * H * HD,
    )


def out_back_kernel(nr, nh, ids, c_ref, x2_ref, gain_ref, dn2_ref, low_ref, *rest):
    weights = rest[: nr * nh]
    dx2_ref, do_ref = rest[nr * nh : nr * nh + 2]
    grads = rest[nr * nh + 2 : 2 * nr * nh + 2]
    dr_ref, term_ref = rest[2 * nr * nh + 2 :]
    width = c_ref.shape[1]
    chunk, cols = H * HD // nr, width // nh
    middle, d_normed = x2_ref[...], dn2_ref[...]
    inverse = lax.rsqrt(jnp.mean(middle * middle, axis=1, keepdims=True) + EPSILON)
    scaled = d_normed * gain_ref[...]
    inner = jnp.mean(scaled * middle, axis=1, keepdims=True)
    d_middle = c_ref[...] + inverse * scaled - middle * (inverse * inverse * inverse * inner)
    dx2_ref[...] = d_middle
    dr_ref[...] = d_middle.astype(BF)
    term_ref[...] = (d_normed * middle * inverse).astype(BF)
    ones = jnp.ones((middle.shape[0], LANES), BF)
    for r in range(nr):
        at = span(row_chunk(ids, r, nr), chunk)
        low = low_ref[:, at]
        gain_grad = dot_tn(term_ref[:, at], ones).astype(BF)
        total = None
        for h in range(nh):
            branch = dr_ref[:, span(half_chunk(ids, h, nh), cols)]
            part = dot_nt(branch, weights[r * nh + h][:, :cols])
            total = part if total is None else total + part
            grads[r * nh + h][:, :cols] = dot_tn(low, branch).astype(BF)
            grads[r * nh + h][:, cols:] = gain_grad
        do_ref[:, at] = total.astype(BF)


def project_out_back(ids, c, x2, gain, dn2, low, weights):
    nr, nh = len(weights), len(weights[0])
    flat = [w for row in weights for w in row]
    ins = [c, x2, gain, dn2, low, *flat]
    rows, cols = H * HD // nr, c.shape[1] // nh
    outs = [jax.ShapeDtypeStruct(c.shape, F32), jax.ShapeDtypeStruct((c.shape[0], H * HD), BF)]
    outs += [jax.ShapeDtypeStruct((rows, cols + LANES), BF)] * (nr * nh)
    got = call(
        functools.partial(out_back_kernel, nr, nh),
        (1,),
        ids,
        ins,
        [whole_spec(i.shape) for i in ins],
        outs,
        [whole_spec(o.shape) for o in outs],
        [pltpu.VMEM(c.shape, BF), pltpu.VMEM(c.shape, BF)],
        4 * c.shape[0] * c.shape[1] * H * HD,
    )
    return got[0], got[1], [[got[2 + r * nh + h] for h in range(nh)] for r in range(nr)]


def picks(slot_ref, experts):
    tokens = slot_ref.shape[-1]
    places = lax.broadcasted_iota(jnp.int32, (CAP, tokens), 0).astype(F32)
    rows = [places == slot_ref[0, j : j + 1, :] for j in range(experts)]
    return rows[0] if experts == 1 else jnp.concatenate(rows, axis=0)


def gather_kernel(groups, per, experts, with_gates, ids, slot_ref, *rest):
    if with_gates:
        gate_ref, rest = rest[0], rest[1:]
    tokens, out_ref = rest[:groups], rest[groups]
    chosen = picks(slot_ref, experts)
    low = chosen.astype(F32).astype(BF)
    for g in range(groups):

        @pl.when(pl.program_id(0) // per == g)
        def _(g=g):
            rows = dot(low, tokens[g][0]).astype(BF)
            for j in range(experts):
                out_ref[j, 0] = rows[j * CAP : (j + 1) * CAP]

    if with_gates:
        for j in range(experts):
            mine = chosen[j * CAP : (j + 1) * CAP]
            gates = jnp.sum(jnp.where(mine, gate_ref[0, j : j + 1, :], 0.0), axis=1, keepdims=True)
            rest[groups + 1][j, 0] = jnp.broadcast_to(gates, (CAP, LANES))


def gather_rows(ids, slots, groups, gates=None):
    blocks, experts, length = slots.shape
    per, width = groups[0].shape[0], groups[0].shape[-1]
    ins, specs = [slots], [pl.BlockSpec((1, experts, length), lambda i, _: (i, 0, 0))]
    if gates is not None:
        ins.append(gates)
        specs.append(specs[0])
    for g, tokens in enumerate(groups):
        ins.append(tokens)
        specs.append(
            pl.BlockSpec(
                (1, length, width), lambda i, _, g=g: (jnp.clip(i - g * per, 0, per - 1), 0, 0)
            )
        )
    outs = [jax.ShapeDtypeStruct((experts, blocks, CAP, width), BF)]
    out_specs = [pl.BlockSpec((experts, 1, CAP, width), lambda i, _: (0, i, 0, 0))]
    if gates is not None:
        outs.append(jax.ShapeDtypeStruct((experts, blocks, CAP, LANES), F32))
        out_specs.append(pl.BlockSpec((experts, 1, CAP, LANES), lambda i, _: (0, i, 0, 0)))
    return call(
        functools.partial(gather_kernel, len(groups), per, experts, gates is not None),
        (blocks,),
        ids,
        ins,
        specs,
        outs,
        out_specs,
        (),
        2 * blocks * experts * CAP * length * width,
    )


def expert_kernel(nz, ids, x_ref, c_ref, gate_ref, *rest):
    weights, rest = rest[:nz], rest[nz:]
    y_ref, dx_ref, gg_ref = rest[:3]
    grads, acc_ref = rest[3 : 3 + nz], rest[3 + nz]
    chunk = x_ref.shape[-1] // nz
    step, last = pl.program_id(1), pl.num_programs(1) - 1
    a = b = ch = None
    for r in range(nz):
        at = span(z_chunk(ids, r, nz), chunk)
        x, c = x_ref[0, :, at], c_ref[0, :, at]
        parts = (
            dot(x, weights[r][0, 0]),
            dot(x, weights[r][0, 1]),
            dot(c, weights[r][0, 2]),
        )
        a, b, ch = parts if a is None else (a + parts[0], b + parts[1], ch + parts[2])
    gate = gate_ref[0][:, :1]
    sig = 1.0 / (1.0 + jnp.exp(-a))
    act = a * sig
    hidden = (act * b).astype(BF).astype(F32)
    gg_ref[0] = jnp.broadcast_to(jnp.sum(hidden * ch, axis=1, keepdims=True), gg_ref.shape[1:])
    hg = (hidden * gate).astype(BF)
    dh = ch * gate
    da = (dh * b * sig * (1.0 + a * (1.0 - sig))).astype(BF)
    db = (dh * act).astype(BF)

    @pl.when(step == 0)
    def _():
        acc_ref[...] = jnp.zeros_like(acc_ref)

    for r in range(nz):
        at = span(z_chunk(ids, r, nz), chunk)
        x, c = x_ref[0, :, at], c_ref[0, :, at]
        y_ref[0, :, at] = dot_nt(hg, weights[r][0, 2]).astype(BF)
        dx_ref[0, :, at] = (dot_nt(da, weights[r][0, 0]) + dot_nt(db, weights[r][0, 1])).astype(BF)
        acc_ref[r, 0] += dot_tn(x, da)
        acc_ref[r, 1] += dot_tn(x, db)
        acc_ref[r, 2] += dot_tn(c, hg)

    @pl.when(step == last)
    def _():
        for r in range(nz):
            grads[r][0] = acc_ref[r].astype(BF)


def run_experts(ids, x_rows, c_rows, gate_rows, weights):
    experts, rows, width = x_rows.shape
    nz = len(weights)
    hidden = weights[0].shape[-1]
    tile = 256
    block = pl.BlockSpec((1, tile, width), lambda j, i, _: (j, i, 0))
    narrow = pl.BlockSpec((1, tile, LANES), lambda j, i, _: (j, i, 0))
    matrix = pl.BlockSpec((1,) + weights[0].shape[1:], lambda j, i, _: (j, 0, 0, 0))
    got = call(
        functools.partial(expert_kernel, nz),
        (experts, rows // tile),
        ids,
        [x_rows, c_rows, gate_rows, *weights],
        [block, block, narrow] + [matrix] * nz,
        [
            jax.ShapeDtypeStruct(x_rows.shape, BF),
            jax.ShapeDtypeStruct(x_rows.shape, BF),
            jax.ShapeDtypeStruct((experts, rows, LANES), F32),
        ]
        + [jax.ShapeDtypeStruct(w.shape, BF) for w in weights],
        [block, block, narrow] + [matrix] * nz,
        [pltpu.VMEM((nz,) + weights[0].shape[1:], F32)],
        2 * 9 * experts * rows * width * hidden,
    )
    return got[0], got[1], got[2], got[3:]


def spread_kernel(groups, per, experts, with_grads, ids, slot_ref, rows_ref, *rest):
    if with_grads:
        grad_ref, rest = rest[0], rest[1:]
    chosen = picks(slot_ref, experts)
    low = chosen.astype(F32).astype(BF)
    rows = [rows_ref[j, 0] for j in range(experts)]
    rows = rows[0] if experts == 1 else jnp.concatenate(rows, axis=0)
    total = dot_tn(low, rows).astype(BF)
    length, width = total.shape
    tail = None
    if with_grads:
        fit = width // length
        line = lax.broadcasted_iota(jnp.int32, (GATE_ROWS, width), 0)
        place = lax.broadcasted_iota(jnp.int32, (GATE_ROWS, width), 1) // length
        tail = jnp.zeros((GATE_ROWS, width), F32)
        for j in range(experts):
            mine = chosen[j * CAP : (j + 1) * CAP]
            sums = jnp.sum(jnp.where(mine, grad_ref[j, 0][:, :1], 0.0), axis=0, keepdims=True)
            wide = jnp.concatenate([sums] * fit, axis=1)
            number = ids[3] + j
            tail = tail + jnp.where((line == number // fit) & (place == number % fit), wide, 0.0)
    for g in range(groups):

        @pl.when(pl.program_id(0) // per == g)
        def _(g=g):
            rest[g][0, :length] = total
            if with_grads:
                rest[g][0, length:] = tail.astype(BF)


def spread_rows(ids, slots, rows, groups, grads=None):
    blocks, experts, length = slots.shape
    per, width = blocks // groups, rows.shape[-1]
    high = length + (GATE_ROWS if grads is not None else 0)
    ins = [slots, rows]
    specs = [
        pl.BlockSpec((1, experts, length), lambda i, _: (i, 0, 0)),
        pl.BlockSpec((experts, 1, CAP, width), lambda i, _: (0, i, 0, 0)),
    ]
    if grads is not None:
        ins.append(grads)
        specs.append(pl.BlockSpec((experts, 1, CAP, LANES), lambda i, _: (0, i, 0, 0)))
    return call(
        functools.partial(spread_kernel, groups, per, experts, grads is not None),
        (blocks,),
        ids,
        ins,
        specs,
        [jax.ShapeDtypeStruct((per, high, width), BF)] * groups,
        [
            pl.BlockSpec(
                (1, high, width), lambda i, _, g=g: (jnp.clip(i - g * per, 0, per - 1), 0, 0)
            )
            for g in range(groups)
        ],
        (),
        2 * blocks * experts * CAP * length * width,
    )


def qkv_grad_kernel(nr, nh, ids, rows_ref, gain_ref, dq_ref, dk_ref, dv_ref, *rest):
    grads, (normed_ref, acc_ref) = rest[: nr * nh], rest[nr * nh :]
    width = rows_ref.shape[-1]
    chunk = width // nr
    qn, kn = H * HD // nh, KVH * HD // nh
    step, last = pl.program_id(0), pl.num_programs(0) - 1
    normed_ref[...] = (rows_ref[0].astype(F32) * gain_ref[...]).astype(BF)

    @pl.when(step == 0)
    def _():
        for r in range(nr):
            x = normed_ref[:, span(row_chunk(ids, r, nr), chunk)]
            for h in range(nh):
                n = r * nh + h
                d_query = dq_ref[:, span(half_chunk(ids, h, nh), qn)]
                grads[n][:, :qn] = dot_tn(x, d_query).astype(BF)
        acc_ref[...] = jnp.zeros_like(acc_ref)

    for r in range(nr):
        x = normed_ref[:, span(row_chunk(ids, r, nr), chunk)]
        for h in range(nh):
            here = span(half_chunk(ids, h, nh), kn)
            acc_ref[r * nh + h, :, :kn] += dot_tn(x, dk_ref[:, here])
            acc_ref[r * nh + h, :, kn:] += dot_tn(x, dv_ref[:, here])

    @pl.when(step == last)
    def _():
        for n in range(nr * nh):
            grads[n][:, qn:] = acc_ref[n].astype(BF)


def project_grads(ids, rows, gain, dq, dk, dv, nr, nh):
    slots, length, width = rows.shape
    cols = (H + 2 * KVH) * HD // nh
    outs = [jax.ShapeDtypeStruct((width // nr, cols), BF)] * (nr * nh)
    keys = pl.BlockSpec((length, KVH * HD), lambda i, _: (i, 0))
    got = call(
        functools.partial(qkv_grad_kernel, nr, nh),
        (slots,),
        ids,
        [rows, gain, dq, dk, dv],
        [
            pl.BlockSpec((1, length, width), lambda i, _: (i, 0, 0)),
            whole_spec(gain.shape),
            whole_spec(dq.shape),
            keys,
            keys,
        ],
        outs,
        [whole_spec(o.shape) for o in outs],
        [
            pltpu.VMEM((length, width), BF),
            pltpu.VMEM((nr * nh, width // nr, 2 * KVH * HD // nh), F32),
        ],
        2 * slots * length * width * 2 * KVH * HD,
    )
    return [[got[r * nh + h] for h in range(nh)] for r in range(nr)]


def rows_back_kernel(nr, nh, ids, dq_ref, dkv_ref, x_ref, dx2_ref, gain_ref, *rest):
    weights = rest[: nr * nh]
    out_ref, grad_ref, low_ref = rest[nr * nh :]
    width = x_ref.shape[1]
    chunk = width // nr
    qn, kn = H * HD // nh, KVH * HD // nh
    low_ref[...] = dkv_ref[...].astype(BF)
    for r in range(nr):
        total = None
        for h in range(nh):
            at = half_chunk(ids, h, nh)
            weight = weights[r * nh + h]
            part = dot_nt(dq_ref[:, span(at, qn)], weight[:, :qn])
            part = part + dot_nt(low_ref[:, span(at, kn)], weight[:, qn : qn + kn])
            values = pl.ds(pl.multiple_of(KVH * HD + at * kn, kn), kn)
            part = part + dot_nt(low_ref[:, values], weight[:, qn + kn : qn + 2 * kn])
            total = part if total is None else total + part
        grad_ref[:, span(row_chunk(ids, r, nr), chunk)] = total
    x = x_ref[...]
    scaled = grad_ref[...] * gain_ref[...]
    inverse = lax.rsqrt(jnp.mean(x * x, axis=1, keepdims=True) + EPSILON)
    inner = jnp.mean(scaled * x, axis=1, keepdims=True)
    out_ref[...] = dx2_ref[...] + inverse * scaled - x * (inverse * inverse * inverse * inner)


def rows_back(ids, dq, dkv, x, dx2, gain, weights):
    nr, nh = len(weights), len(weights[0])
    ins = [dq, dkv, x, dx2, gain, *[w for row in weights for w in row]]
    return call(
        functools.partial(rows_back_kernel, nr, nh),
        (1,),
        ids,
        ins,
        [whole_spec(i.shape) for i in ins],
        jax.ShapeDtypeStruct(x.shape, F32),
        whole_spec(x.shape),
        [pltpu.VMEM(x.shape, F32), pltpu.VMEM(dkv.shape, BF)],
        2 * x.shape[0] * x.shape[1] * 2048,
    )


def swap(value, axis, distance):
    count = lax.axis_size(axis)
    return lax.ppermute(value, axis, [(i, i ^ distance) for i in range(count)])


def pick(array, index):
    return lax.dynamic_index_in_dim(array, index, 0, keepdims=False)


def gather_z(value):
    chips = lax.axis_size("shard") // 2
    if chips != 4:
        return [value] + [swap(value, "shard", 2 * r) for r in range(1, chips)]
    near, far = swap(value, "shard", 2), swap(value, "shard", 4)
    return [value, near, far, swap(far, "shard", 2)]


def scatter_z(parts):
    chips = len(parts)
    if chips != 4:
        got = [swap(parts[r], "shard", 2 * r) for r in range(1, chips)]
    else:
        step = swap(parts[3], "shard", 2)
        near = swap(parts[1], "shard", 2)
        far = (parts[2].astype(F32) + step.astype(F32)).astype(BF)
        got = [near, swap(far, "shard", 4)]
    total = parts[0].astype(F32)
    for one in got:
        total = total + one.astype(F32)
    return total


def in_order(mine, other, core, axis):
    return jnp.where(
        core == 0,
        jnp.concatenate([mine, other], axis=axis),
        jnp.concatenate([other, mine], axis=axis),
    )


def gather_matrix(halves, z, core, fast):
    if not fast:
        joined = jnp.concatenate([halves[0], halves[1]], axis=1)
        return [[lax.all_gather(joined, ("expert", "shard"), axis=0, tiled=True)]]
    mine, other = pick(halves, core), pick(halves, 1 - core)
    chip = in_order(mine, swap(other, "shard", 1), core, 0)
    stacked = jnp.stack(gather_z(chip))
    rows = jnp.concatenate([pick(stacked, z ^ i) for i in range(stacked.shape[0])], axis=0)
    blocks = [rows] + [swap(rows, "expert", r) for r in range(1, lax.axis_size("expert"))]
    return [[block, swap(block, "shard", 1)] for block in blocks]


def scatter_matrix(blocks, z, core, fast):
    if not fast:
        total = lax.psum_scatter(blocks[0][0], ("expert", "shard"), scatter_dimension=0, tiled=True)
        return total.astype(F32)
    sums = [
        (block[0].astype(F32) + swap(block[1], "shard", 1).astype(F32)).astype(BF)
        for block in blocks
    ]
    total = sums[0].astype(F32)
    for r in range(1, len(sums)):
        total = total + swap(sums[r], "expert", r).astype(F32)
    chips = lax.axis_size("shard") // 2
    parts = total.astype(BF).reshape(chips, total.shape[0] // chips, total.shape[1])
    rows = scatter_z([pick(parts, z ^ r) for r in range(chips)])
    rows = rows.reshape(2, rows.shape[0] // 2, rows.shape[1])
    mine = pick(rows, core)
    other = swap(pick(rows, 1 - core).astype(BF), "shard", 1).astype(F32)
    return jnp.where(core == 0, mine, other), jnp.where(core == 0, other, mine)


def gather_tokens(value, paired):
    bases = [value] + ([swap(value, "shard", 4)] if paired else [])
    groups = []
    for base in bases:
        count = lax.axis_size("expert")
        own = jnp.stack([base] + [swap(base, "expert", r) for r in range(1, count)])
        groups += [own, swap(own, "shard", 1)]
    return groups


def scatter_tokens(groups, paired):
    totals = []
    for n in range(len(groups) // 2):
        own, other = groups[2 * n], swap(groups[2 * n + 1], "shard", 1)
        sums = [
            (own[r].astype(F32) + other[r].astype(F32)).astype(BF) for r in range(own.shape[0])
        ]
        total = sums[0].astype(F32)
        for r in range(1, len(sums)):
            total = total + swap(sums[r], "expert", r).astype(F32)
        totals.append(total)
    if paired:
        return totals[0] + swap(totals[1].astype(BF), "shard", 4).astype(F32)
    return totals[0]


def body(
    tokens,
    block_ids,
    routes,
    gates,
    attn_gain,
    w_query,
    w_key,
    w_value,
    w_out,
    moe_gain,
    w_gate,
    w_up,
    w_down,
    cotangent,
):
    length, width = tokens.shape[1], tokens.shape[2]
    n_expert, n_shard = lax.axis_size("expert"), lax.axis_size("shard")
    chips = n_shard // 2
    local = w_gate.shape[0]
    fast = n_expert == 4 and n_shard == 8
    paired = chips == 4 and local % 4 == 0
    sides = 2 if paired else 1
    experts = local // (2 * sides)
    e, s = lax.axis_index("expert"), lax.axis_index("shard")
    z, core = s // 2, s % 2
    side = z // 2 if paired else 0
    first_expert = e * local + core * (local // 2) + side * experts
    ids = jnp.stack([e, z, core, first_expert]).astype(jnp.int32)

    x = tokens[0]
    c = cotangent[0]

    inverse_one = lax.rsqrt(jnp.mean(x * x, axis=-1, keepdims=True) + EPSILON)
    scaled_rows = (x * inverse_one).astype(BF)
    own_core = jnp.stack(gather_z(scaled_rows))
    rows = jnp.concatenate([own_core, swap(own_core, "shard", 1)], axis=0)

    def halves(matrix):
        low = matrix.astype(BF)
        return low.reshape(low.shape[0], 2, low.shape[1] // 2).transpose(1, 0, 2)

    def column(gain):
        return jnp.broadcast_to(gain.astype(BF)[None, :, None], (1, gain.shape[0], LANES // 2))

    if fast:
        gain_cols = jnp.concatenate([column(attn_gain), column(moe_gain)], axis=2)
        gain_cols = jnp.concatenate([gain_cols, gain_cols], axis=0)
        packed = jnp.concatenate([halves(w_query), halves(w_key), halves(w_value), gain_cols], axis=2)
        qkv_w = gather_matrix(packed, z, core, fast)
        blocks = jnp.stack([w[0][:, (H + 2 * KVH) * HD // 2 :] for w in qkv_w])
        blocks = jnp.concatenate([pick(blocks, e ^ i) for i in range(n_expert)], axis=0)
        gain_one = blocks[:, 0].astype(F32)[None]
        gain_two = blocks[:, LANES // 2].astype(F32)[None]
    else:
        packed = jnp.concatenate(
            [w_query.astype(BF), w_key.astype(BF), w_value.astype(BF)], axis=1
        )
        packed = lax.all_gather(packed, ("expert", "shard"), axis=0, tiled=True)
        qkv_w = [[packed]]
        both = jnp.stack([attn_gain.astype(BF), moe_gain.astype(BF)], axis=1)
        both = lax.all_gather(both, ("expert", "shard"), axis=0, tiled=True).astype(F32)
        gain_one, gain_two = both[:, 0][None], both[:, 1][None]
    nr, nh = len(qkv_w), len(qkv_w[0])
    out_w = gather_matrix(halves(w_out), z, core, fast)

    numbers = jnp.arange(EXPERTS, dtype=jnp.int32)
    named = routes[0][None, :, :] == numbers[:, None, None]
    dense = jnp.sum(jnp.where(named, gates[0][None, :, :], 0.0), axis=-1)
    dense = jnp.concatenate(gather_tokens(dense, paired), axis=0)
    gate_here = lax.dynamic_slice_in_dim(dense, first_expert, experts, 1)
    chosen = gate_here > 0.0
    before = jnp.triu(jnp.ones((length, length), BF), 1)
    ranks = jnp.einsum("net,tu->neu", chosen.astype(BF), before, preferred_element_type=F32)
    slots = jnp.where(chosen, ranks, -1.0)

    low = jnp.stack([w_gate.astype(BF), w_up.astype(BF), w_down.astype(BF)], axis=1)
    low = low.reshape((2, local // 2) + low.shape[1:])
    chip_w = in_order(pick(low, core), swap(pick(low, 1 - core), "shard", 1), core, 2)
    if paired:
        chip_w = chip_w.reshape((2, experts) + chip_w.shape[1:])
        here, there = pick(chip_w, side), pick(chip_w, 1 - side)
        far = swap(there, "shard", 4)
        expert_w = [here, swap(here, "shard", 2), far, swap(far, "shard", 2)]
    else:
        expert_w = gather_z(chip_w)

    c_groups = gather_tokens(c.astype(BF), paired)
    c_rows, gate_rows = gather_rows(ids, slots, c_groups, gate_here)

    owners = jnp.stack([s ^ (2 * r + k) for k in range(2) for r in range(chips)])
    places = (owners[:, None] * length + jnp.arange(length)[None, :]).reshape(n_shard * length)
    freqs = 10000.0 ** (-(jnp.arange(HD // 2, dtype=F32) * 2.0 / HD))
    angles = places.astype(F32)[:, None] * freqs[None, :]
    cosine, sine = jnp.cos(angles), jnp.sin(angles)
    cosine = jnp.concatenate([cosine] * 4, axis=1)
    sine = jnp.concatenate([-sine, sine] * 2, axis=1)
    every = block_ids[0].reshape(n_shard, length)
    key_blocks = jnp.concatenate([pick(every, s ^ (2 * r + k)) for k in range(2) for r in range(chips)])
    own_blocks = pick(every, s)
    lanes = jnp.arange(LANES, dtype=jnp.int32)[None, :]
    key_extra = ((lanes == key_blocks[:, None]) | ((lanes >= 16) & (lanes < 19))).astype(BF)
    query_extra = jnp.where((lanes < 16) & (lanes > own_blocks[:, None]), -1e30, 0.0).astype(BF)

    q, k, v = project(ids, rows, gain_one, cosine, sine, qkv_w)
    mixed, mixed_low, lse = attend(ids, q, k, v, key_extra, query_extra)
    x2, n2 = project_out(ids, x, mixed_low, gain_two, out_w)

    n2_groups = gather_tokens(n2, paired)
    (x_rows,) = gather_rows(ids, slots, n2_groups)
    flat = (experts, slots.shape[0] * CAP)
    y_rows, dx_rows, grad_rows, d_experts = run_experts(
        ids,
        x_rows.reshape(flat + (width,)),
        c_rows.reshape(flat + (width,)),
        gate_rows.reshape(flat + (LANES,)),
        expert_w,
    )
    split = (experts, slots.shape[0], CAP)
    count = len(n2_groups)
    dn2_parts = spread_rows(ids, slots, dx_rows.reshape(split + (width,)), count)
    dn2 = scatter_tokens(dn2_parts, paired)
    out_parts = spread_rows(
        ids, slots, y_rows.reshape(split + (width,)), count, grad_rows.reshape(split + (LANES,))
    )
    out_sum = scatter_tokens(out_parts, paired)
    output = x2 + out_sum[:length]
    gate_sums = out_sum[length : length + EXPERTS * length // width].reshape(EXPERTS, length)
    gate_grad = jnp.sum(jnp.where(named, gate_sums[:, :, None], 0.0), axis=0)

    if paired:
        step = swap(d_experts[3], "shard", 2)
        near = swap(d_experts[1], "shard", 2)
        far = (d_experts[2].astype(F32) + step.astype(F32)).astype(BF)
        there = swap(far, "shard", 4).astype(F32)
        here = d_experts[0].astype(F32) + near.astype(F32)
        d_chip = jnp.where(
            side == 0, jnp.concatenate([here, there], axis=0), jnp.concatenate([there, here], axis=0)
        )
    else:
        d_chip = scatter_z(d_experts)
    half = d_chip.shape[2] // 2
    d_chip = d_chip.astype(BF)
    mine = lax.dynamic_slice_in_dim(d_chip, core * half, half, 2)
    other = swap(lax.dynamic_slice_in_dim(d_chip, (1 - core) * half, half, 2), "shard", 1)
    d_expert = in_order(mine, other, core, 0).astype(F32)

    dx2, d_mixed, d_out_w = project_out_back(ids, c, x2, gain_two, dn2, mixed_low, out_w)
    dq, dk, dv = attend_back(
        ids, q, d_mixed, mixed, lse, k, v, key_extra, query_extra, cosine, sine
    )
    d_qkv_w = project_grads(ids, rows, gain_one, dq, dk, dv, nr, nh)
    dkv = jnp.concatenate([dk, dv], axis=1).reshape(2, chips, length, 2 * KVH * HD)
    dkv_core = swap(dkv[1], "shard", 1)
    dkv_sums = (dkv[0].astype(F32) + dkv_core.astype(F32)).astype(BF)
    dkv_own = scatter_z([dkv_sums[r] for r in range(chips)])
    token_grad = rows_back(ids, dq, dkv_own, x, dx2, gain_one, qkv_w)

    d_out = scatter_matrix(d_out_w, z, core, fast)
    d_qkv = scatter_matrix(d_qkv_w, z, core, fast)
    if fast:
        cols = width // 2
        d_out_full = jnp.concatenate([d_out[0][:, :cols], d_out[1][:, :cols]], axis=1)
        d_gain_two = d_out[0][:, cols]
        qn, kn = H * HD // 2, KVH * HD // 2
        d_query_w = jnp.concatenate([d[:, :qn] for d in d_qkv], axis=1)
        d_key_w = jnp.concatenate([d[:, qn : qn + kn] for d in d_qkv], axis=1)
        d_value_w = jnp.concatenate([d[:, qn + kn :] for d in d_qkv], axis=1)
    else:
        d_out_full, d_gain_two = d_out[:, :width], d_out[:, width]
        qn, kn = H * HD, KVH * HD
        d_query_w, d_key_w, d_value_w = d_qkv[:, :qn], d_qkv[:, qn : qn + kn], d_qkv[:, qn + kn :]
    row_sums = (
        jnp.sum(w_query.astype(BF).astype(F32) * d_query_w, axis=1)
        + jnp.sum(w_key.astype(BF).astype(F32) * d_key_w, axis=1)
        + jnp.sum(w_value.astype(BF).astype(F32) * d_value_w, axis=1)
    )
    d_gain_one = row_sums / attn_gain.astype(BF).astype(F32)

    return (
        output[None],
        token_grad[None],
        gate_grad[None],
        d_gain_one,
        d_query_w,
        d_key_w,
        d_value_w,
        d_out_full,
        d_gain_two,
        d_expert[:, 0],
        d_expert[:, 1],
        d_expert[:, 2],
    )


def solution(mesh):
    rows = P("expert", "shard", None)
    split = P(("expert", "shard"), None)
    gain = P(("expert", "shard"))
    in_specs = (
        rows, P("expert", None), rows, rows, gain, split, split, split, split, gain, rows, rows, rows, rows,
    )
    out_specs = (rows, rows, rows, gain, split, split, split, split, gain, rows, rows, rows)
    return jax.shard_map(body, mesh=mesh, in_specs=in_specs, out_specs=out_specs, check_vma=False)
```

time: 1770 us -> 763 us (0.43)
  waiting for transfers between devices: 1170 us -> 368 us
  matrix products: 253 us -> 0.14 us
  Pallas kernels: 0 us -> 206 us
  local copies, waits for them, and re-layouts: 117 us -> 24.7 us
  blocking collectives: 81.7 us -> 0 us
  starting transfers between devices: 22.1 us -> 83.2 us
  other arithmetic: 92.8 us -> 66.6 us
    reduce_scatter x9 -> x0, waiting for transfers between devices: 789 us -> none  [the longest x1 141 us: body(): lax.psum_scatter(d_query_w, ('expert', 'shard'), scatter_dimension=0, til...]
    ppermute x0 -> x105, waiting for transfers between devices: none -> 368 us  [swap(): return lax.ppermute(value, axis, [(i, i ^ distance) for i in range(count)])]
    dot_general x51 -> x1, matrix products: 253 us -> 0.14 us  [body(): jnp.einsum('net,tu->neu', chosen.astype(BF), before, preferred_element_ty...]
    all_gather x9 -> x0, waiting for transfers between devices: 242 us -> none  [the longest x1 61.2 us: body(): lax.all_gather(w_down.astype(jnp.bfloat16), 'shard', axis=1, tiled=True)]
    pallas_call x0 -> x12, Pallas kernels: none -> 206 us  [call(): pl.pallas_call(kernel, grid_spec=pltpu.PrefetchScalarGridSpec(num_scalar_...]
    all_to_all x4 -> x0, waiting for transfers between devices: 142 us -> none  [the longest x1 49.2 us: body(): lax.all_to_all(d_inputs.reshape(n_expert, local_experts * CAP, width), 'e...]
    ppermute x0 -> x105, starting transfers between devices: none -> 83.2 us  [swap(): return lax.ppermute(value, axis, [(i, i ^ distance) for i in range(count)])]
    unnamed x2 -> x0, blocking collectives: 81.7 us -> none
  transfers between devices with their start and end apart: 22 -> 105, of which waited for: 19 -> 44; matrix products, arithmetic and copies ran while one was open for 17% -> 11% of each run, Pallas kernels for 0% -> 21%
where the time goes in v1:
time: 763 us; the launch traced here: 752 us
  waiting for transfers between devices  368 us (48%)
  Pallas kernels  206 us (27%)
  starting transfers between devices  83.2 us (11%)
  other arithmetic  66.6 us (9%)
  local copies, waits for them, and re-layouts  24.7 us (3%)
    ppermute x105, waiting for transfers between devices, swap(): return lax.ppermute(value, axis, [(i, i ^ distance) for i in range(count)])  368 us
    pallas_call x12, Pallas kernels, call(): pl.pallas_call(kernel, grid_spec=pltpu.PrefetchScalarGridSpec(num_scalar_...  206 us
    ppermute x105, starting transfers between devices, swap(): return lax.ppermute(value, axis, [(i, i ^ distance) for i in range(count)])  83.2 us
  transfers between devices with their start and end apart: 105, of which 44 were waited for; matrix products, arithmetic and copies ran while one was open for 11% of the time, Pallas kernels for 21%

profile of v1, /device:TPU:0, one launch (start us, length us, event | category | flops | bytes accessed | tf_op | source)
XLA Modules:
  0.0 751.7 jit_solution(16030385898130129636)
XLA Ops:
  39.3 9.2 %collective-permute-done.17 = bf16[64,512]{1,0:T(8,128)(2,1)S(1)} collective-permute-done((bf16[64,512]{1,0:T(8,128)(2,1)S(1)}, bf16[64,512]{1,0:T(8,128)(2,1)S(1)}, u32[]{:S(2)}, u32[]{:S(2)}) %collective-permute-start.17) | collective-permute-done | bytes 65568 | tf_op jit(solution)/shard_map/ppermute | solution.py:688
  64.1 10.0 %collective-permute-done = bf16[256,1024]{1,0:T(8,128)(2,1)S(1)} collective-permute-done((bf16[256,1024]{1,0:T(8,128)(2,1)}, bf16[256,1024]{1,0:T(8,128)(2,1)S(1)}, u32[]{:S(2)}, u32[]{:S(2)}) %collective-permute-start) | collective-permute-done | bytes 524320 | tf_op jit(solution)/shard_map/ppermute | solution.py:688
  89.3 13.5 %collective-permute-done.31 = f32[32,256]{1,0:T(8,128)} collective-permute-done((f32[32,256]{1,0:T(8,128)S(1)}, f32[32,256]{1,0:T(8,128)}, u32[]{:S(2)}, u32[]{:S(2)}) %collective-permute-start.31) | collective-permute-done | bytes 32800 | tf_op jit(solution)/shard_map/ppermute | solution.py:688
  106.3 13.6 %collective-permute-done.22.rest_4_ = bf16[256,512]{1,0:T(8,128)(2,1)S(1)} collective-permute-done((bf16[256,512]{1,0:T(8,128)(2,1)S(1)}, bf16[256,512]{1,0:T(8,128)(2,1)S(1)}, u32[]{:S(2)}, u32[]{:S(2)}) %collective-permute-start.22) | collective-permute-done | bytes 262176 | tf_op jit(solution)/shard_map/ppermute | solution.py:688
  124.2 21.8 %collective-permute-done.48 = bf16[256,1024]{1,0:T(8,128)(2,1)S(1)} collective-permute-done((bf16[256,1024]{1,0:T(8,128)(2,1)}, bf16[256,1024]{1,0:T(8,128)(2,1)S(1)}, u32[]{:S(2)}, u32[]{:S(2)}) %collective-permute-start.48) | collective-permute-done | bytes 524320 | tf_op jit(solution)/shard_map/ppermute | solution.py:688
  153.2 14.7 %shard_map.229 = (bf16[256,1024]{1,0:T(8,128)(2,1)}, bf16[2048,512]{1,0:T(8,128)(2,1)}, bf16[2048,512]{1,0:T(8,128)(2,1)}) custom-call(s32[4]{0:T(128)} %pad_add_fusion.ids, bf16[8,256,1024]{2,1,0:T(8,128)(2,1)} %copy-done.66, f32[1,1024]{1,0:T(1,128)} %bitcast.328, f32[2048,128]{1,0:T(8,128)} %get-tuple-element.186.cos_ref, ...), custom_call_target="tpu_custom_call" | custom-call | flops 4294967296 | bytes 15732736 | tf_op jit(solution)/shard_map/pallas_call | solution.py:41
  172.1 16.6 %shard_map.230 = (f32[256,1024]{1,0:T(8,128)}, bf16[256,1024]{1,0:T(8,128)(2,1)}, f32[4,256,128]{2,1,0:T(8,128)}) custom-call(s32[4]{0:T(128)} %pad_add_fusion.ids, bf16[256,1024]{1,0:T(8,128)(2,1)} %get-tuple-element.58.q_ref, bf16[2048,512]{1,0:T(8,128)(2,1)} %get-tuple-element.59.k_ref, bf16[2048,512]{1,0:T(8,128)(2,1)} %get-tuple-element.60.v_ref, ...), custom_call_target="tpu_custom_call" | custom-call | flops 6442450944 | bytes 7405568 | tf_op jit(solution)/shard_map/pallas_call | solution.py:41
  196.9 8.6 %collective-permute-done.49 = bf16[256,1024]{1,0:T(8,128)(2,1)S(1)} collective-permute-done((bf16[256,1024]{1,0:T(8,128)(2,1)S(1)}, bf16[256,1024]{1,0:T(8,128)(2,1)S(1)}, u32[]{:S(2)}, u32[]{:S(2)}) %collective-permute-start.49) | collective-permute-done | bytes 524320 | tf_op jit(solution)/shard_map/ppermute | solution.py:688
  251.7 36.2 %collective-permute-done.55.rest_2_ = bf16[2,3,256,512]{3,2,1,0:T(8,128)(2,1)} collective-permute-done((bf16[2,3,256,512]{3,2,1,0:T(8,128)(2,1)S(1)}, bf16[2,3,256,512]{3,2,1,0:T(8,128)(2,1)}, u32[]{:S(2)}, u32[]{:S(2)}) %collective-permute-start.55) | collective-permute-done | bytes 1572896 | tf_op jit(solution)/shard_map/ppermute | solution.py:688
  291.5 15.4 %shard_map.233 = (bf16[2,16,80,1024]{3,2,1,0:T(8,128)(2,1)}, f32[2,16,80,128]{3,2,1,0:T(8,128)}) custom-call(s32[4]{0:T(128)} %pad_add_fusion.ids, f32[16,2,256]{2,1,0:T(2,128)} %copy_select_fusion.slot_ref, f32[16,2,256]{2,1,0:T(2,128)} %get-tuple-element.115.rest_0_, bf16[4,256,1024]{2,1,0:T(8,128)(2,1)} %copy-done.1, bf16[4,256,1024]{2,1,0:T(8,128)(2,1)} %copy-done.18, ...), custom_call_target="tpu_custom_call" | custom-call | flops 1342177280 | bytes 15007744 | tf_op jit(solution)/shard_map/pallas_call | solution.py:41
  307.0 14.1 %shard_map.232 = bf16[2,16,80,1024]{3,2,1,0:T(8,128)(2,1)} custom-call(s32[4]{0:T(128)} %pad_add_fusion.ids, f32[16,2,256]{2,1,0:T(2,128)} %copy_select_fusion.slot_ref, bf16[4,256,1024]{2,1,0:T(8,128)(2,1)} %copy-done.2, bf16[4,256,1024]{2,1,0:T(8,128)(2,1)} %collective-permute-done.38.rest_1_, bf16[4,256,1024]{2,1,0:T(8,128)(2,1)} %pad_maximum_fusion.3.rest_2_, ...), custom_call_target="tpu_custom_call" | custom-call | flops 1342177280 | bytes 13664256 | tf_op jit(solution)/shard_map/pallas_call | solution.py:41
  321.5 33.7 %collective-permute-done.56.rest_3_ = bf16[2,3,256,512]{3,2,1,0:T(8,128)(2,1)} collective-permute-done((bf16[2,3,256,512]{3,2,1,0:T(8,128)(2,1)}, bf16[2,3,256,512]{3,2,1,0:T(8,128)(2,1)}, u32[]{:S(2)}, u32[]{:S(2)}) %collective-permute-start.56) | collective-permute-done | bytes 1572896 | tf_op jit(solution)/shard_map/ppermute | solution.py:688
  355.2 38.7 %shard_map.234 = (bf16[2,1280,1024]{2,1,0:T(8,128)(2,1)}, bf16[2,1280,1024]{2,1,0:T(8,128)(2,1)}, f32[2,1280,128]{2,1,0:T(8,128)}, bf16[2,3,256,512]{3,2,1,0:T(8...) custom-call(s32[4]{0:T(128)} %pad_add_fusion.ids, ...), custom_call_target="tpu_custom_call" | custom-call | flops 24159191040 | bytes 36175872 | tf_op jit(solution)/shard_map/pallas_call | solution.py:41
  394.0 15.2 %shard_map.236 = (bf16[4,256,1024]{2,1,0:T(8,128)(2,1)}, bf16[4,256,1024]{2,1,0:T(8,128)(2,1)}, bf16[4,256,1024]{2,1,0:T(8,128)(2,1)}, bf16[4,256,1024]{2,1,0:T(8,128)(2,1)}) custom-call(s32[4]{0:T(128)} %pad_add_fusion.ids, f32[16,2,256]{2,1,0:T(2,128)} %copy_select_fusion.slot_ref, bf16[2,16,80,1024]{3,2,1,0:T(8,128)(2,1)} %bitcast.267), custom_call_target="tpu_custom_call" | custom-call | flops 1342177280 | bytes 13664256 | tf_op jit(solution)/shard_map/pallas_call | solution.py:41
  411.5 15.5 %shard_map.235 = (bf16[4,272,1024]{2,1,0:T(8,128)(2,1)}, bf16[4,272,1024]{2,1,0:T(8,128)(2,1)}, bf16[4,272,1024]{2,1,0:T(8,128)(2,1)}, bf16[4,272,1024]{2,1,0:T(8,128)(2,1)}) custom-call(s32[4]{0:T(128)} %pad_add_fusion.ids, f32[16,2,256]{2,1,0:T(2,128)} %copy_select_fusion.slot_ref, bf16[2,16,80,1024]{3,2,1,0:T(8,128)(2,1)} %bitcast.268, ...), custom_call_target="tpu_custom_call" | custom-call | flops 1342177280 | bytes 15499264 | tf_op jit(solution)/shard_map/pallas_call | solution.py:41
  434.0 30.4 %collective-permute-done.101 = bf16[2,3,256,512]{3,2,1,0:T(8,128)(2,1)} collective-permute-done((bf16[2,3,256,512]{3,2,1,0:T(8,128)(2,1)}, bf16[2,3,256,512]{3,2,1,0:T(8,128)(2,1)}, u32[]{:S(2)}, u32[]{:S(2)}) %collective-permute-start.101) | collective-permute-done | bytes 1572896 | tf_op jit(solution)/shard_map/ppermute | solution.py:688
  485.8 10.2 %collective-permute-done.73 = bf16[256,1024]{1,0:T(8,128)(2,1)S(1)} collective-permute-done((bf16[256,1024]{1,0:T(8,128)(2,1)S(1)}, bf16[256,1024]{1,0:T(8,128)(2,1)S(1)}, u32[]{:S(2)}, u32[]{:S(2)}) %collective-permute-start.73) | collective-permute-done | bytes 524320 | tf_op jit(solution)/shard_map/ppermute | solution.py:688
  509.1 10.9 %collective-permute-done.64 = bf16[272,1024]{1,0:T(8,128)(2,1)S(1)} collective-permute-done((bf16[272,1024]{1,0:T(8,128)(2,1)S(1)}, bf16[272,1024]{1,0:T(8,128)(2,1)S(1)}, u32[]{:S(2)}, u32[]{:S(2)}) %collective-permute-start.64) | collective-permute-done | bytes 557088 | tf_op jit(solution)/shard_map/ppermute | solution.py:688
  527.4 18.5 %collective-permute-done.103 = bf16[2,3,256,512]{3,2,1,0:T(8,128)(2,1)S(1)} collective-permute-done((bf16[2,3,256,512]{3,2,1,0:T(8,128)(2,1)S(1)}, bf16[2,3,256,512]{3,2,1,0:T(8,128)(2,1)S(1)}, u32[]{:S(2)}, u32[]{:S(2)}) %collective-permute-start.103) | collective-permute-done | bytes 1572896 | tf_op jit(solution)/shard_map/ppermute | solution.py:688
  552.0 17.0 %collective-permute-done.74 = bf16[256,1024]{1,0:T(8,128)(2,1)S(1)} collective-permute-done((bf16[256,1024]{1,0:T(8,128)(2,1)S(1)}, bf16[256,1024]{1,0:T(8,128)(2,1)S(1)}, u32[]{:S(2)}, u32[]{:S(2)}) %collective-permute-start.74) | collective-permute-done | bytes 524320 | tf_op jit(solution)/shard_map/ppermute | solution.py:688
  578.0 44.7 %shard_map.238 = (bf16[256,1024]{1,0:T(8,128)(2,1)}, bf16[2048,512]{1,0:T(8,128)(2,1)}, bf16[2048,512]{1,0:T(8,128)(2,1)}) custom-call(s32[4]{0:T(128)} %pad_add_fusion.ids, bf16[256,1024]{1,0:T(8,128)(2,1)} %get-tuple-element.58.q_ref, bf16[256,1024]{1,0:T(8,128)(2,1)} %get-tuple-element.77.do_ref, f32[256,1024]{1,0:T(8,128)} %get-tuple-element.78.o_ref, ...), custom_call_target="tpu_custom_call" | custom-call | flops 15032385536 | bytes 14221312 | tf_op jit(solution)/shard_map/pallas_call | solution.py:41
  626.9 13.7 %shard_map.240 = (bf16[256,1024]{1,0:T(8,128)(2,1)}, bf16[256,1024]{1,0:T(8,128)(2,1)}, bf16[256,1024]{1,0:T(8,128)(2,1)}, bf16[256,1024]{1,0:T(8,128)(2,1)}, bf...) custom-call(s32[4]{0:T(128)} %pad_add_fusion.ids, ...), custom_call_target="tpu_custom_call" | custom-call | flops 4294967296 | bytes 13111296 | tf_op jit(solution)/shard_map/pallas_call | solution.py:41
  707.9 10.7 %collective-permute-done.77 = bf16[256,1024]{1,0:T(8,128)(2,1)S(1)} collective-permute-done((bf16[256,1024]{1,0:T(8,128)(2,1)S(1)}, bf16[256,1024]{1,0:T(8,128)(2,1)S(1)}, u32[]{:S(2)}, u32[]{:S(2)}) %collective-permute-start.77) | collective-permute-done | bytes 524320 | tf_op jit(solution)/shard_map/ppermute | solution.py:688
  723.0 14.6 %collective-permute-done.76 = bf16[256,1024]{1,0:T(8,128)(2,1)S(1)} collective-permute-done((bf16[256,1024]{1,0:T(8,128)(2,1)S(1)}, bf16[256,1024]{1,0:T(8,128)(2,1)S(1)}, u32[]{:S(2)}, u32[]{:S(2)}) %collective-permute-start.76) | collective-permute-done | bytes 524320 | tf_op jit(solution)/shard_map/ppermute | solution.py:688
  (498 shorter events, 301.8 us)
Async XLA Ops:
  1.5 53.4 %collective-permute-start.30 = (f32[32,256]{1,0:T(8,128)S(1)}, f32[32,256]{1,0:T(8,128)S(1)}, u32[]{:S(2)}, u32[]{:S(2)}) collective-permute-start(f32[32,256]{1,0:T(8,128)S(1)} %select_reduce_fusion.1), channel_id=1, source_target_pairs={{0,4},{1,5},{2,6},{3,7},{4,0},{5,1},{6,2},{7,3},{8,12},{9,13},{10,... | collective-permute-start | bytes 98312 | tf_op jit(solution)/shard_map/ppermute | solution.py:688
  15.3 48.3 %collective-permute-start.1 = (bf16[256,1024]{1,0:T(8,128)(2,1)}, bf16[256,1024]{1,0:T(8,128)(2,1)}, u32[]{:S(2)}, u32[]{:S(2)}) collective-permute-start(bf16[256,1024]{1,0:T(8,128)(2,1)} %multiply_convert_fusion), channel_id=1, source_target_pairs={{0,4},{1,5},{2,6},{3,7},{4,0},{5,1},{6,2},{7,3},{8,12},{9,13},{10,... | collective-permute-start | bytes 1572872 | tf_op jit(solution)/shard_map/ppermute | solution.py:688
  87.0 61.8 %collective-permute-start.3 = (bf16[4,256,1024]{2,1,0:T(8,128)(2,1)S(1)}, bf16[4,256,1024]{2,1,0:T(8,128)(2,1)S(1)}, u32[]{:S(2)}, u32[]{:S(2)}) collective-permute-start(bf16[4,256,1024]{2,1,0:T(8,128)(2,1)S(1)} %pad_maximum_fusion.1), channel_id=1, source_target_pairs={{0,1},{1,0},{2,3},{3,2},{4,5},{5,4},{6,7},{7,6},{8,9},{9,8},{10,11... | collective-permute-start | bytes 6291464 | tf_op jit(solution)/shard_map/ppermute | solution.py:688
  147.8 59.8 %collective-permute-start.53 = (bf16[4,3,128,512]{3,2,1,0:T(8,128)(2,1)S(1)}, bf16[4,3,128,512]{3,2,1,0:T(8,128)(2,1)S(1)}, u32[]{:S(2)}, u32[]{:S(2)}) collective-permute-start(bf16[4,3,128,512]{3,2,1,0:T(8,128)(2,1)S(1)} %copy-done.22), channel_id=1, source_target_pairs={{0,1},{1,0},{2,3},{3,2},{4,5},{5,4},{6,7},{7,6},{8,9},{9,8},{10,11... | collective-permute-start | bytes 4718600 | tf_op jit(solution)/shard_map/ppermute | solution.py:688
  207.5 44.0 %collective-permute-start.47 = (bf16[4,256,1024]{2,1,0:T(8,128)(2,1)S(1)}, bf16[4,256,1024]{2,1,0:T(8,128)(2,1)S(1)}, u32[]{:S(2)}, u32[]{:S(2)}) collective-permute-start(bf16[4,256,1024]{2,1,0:T(8,128)(2,1)S(1)} %pad_maximum_fusion.4.rest_1_), channel_id=1, source_target_pairs={{0,1},{1,0},{2,3},{3,2},{4,5},{5,4},{6,7},{7,6},{8,9},{9,8},{10,11... | collective-permute-start | bytes 6291464 | tf_op jit(solution)/shard_map/ppermute | solution.py:688
  217.6 70.3 %collective-permute-start.55 = (bf16[2,3,256,512]{3,2,1,0:T(8,128)(2,1)S(1)}, bf16[2,3,256,512]{3,2,1,0:T(8,128)(2,1)}, u32[]{:S(2)}, u32[]{:S(2)}) collective-permute-start(bf16[2,3,256,512]{3,2,1,0:T(8,128)(2,1)S(1)} %get-tuple-element.137), channel_id=1, source_target_pairs={{0,4},{1,5},{2,6},{3,7},{4,0},{5,1},{6,2},{7,3},{8,12},{9,13},{10,... | collective-permute-start | bytes 4718600 | tf_op jit(solution)/shard_map/ppermute | solution.py:688
  250.9 56.0 %collective-permute-start.38 = (bf16[4,256,1024]{2,1,0:T(8,128)(2,1)S(1)}, bf16[4,256,1024]{2,1,0:T(8,128)(2,1)}, u32[]{:S(2)}, u32[]{:S(2)}) collective-permute-start(bf16[4,256,1024]{2,1,0:T(8,128)(2,1)S(1)} %pad_maximum_fusion.2.rest_0_), channel_id=1, source_target_pairs={{0,1},{1,0},{2,3},{3,2},{4,5},{5,4},{6,7},{7,6},{8,9},{9,8},{10,11... | collective-permute-start | bytes 6291464 | tf_op jit(solution)/shard_map/ppermute | solution.py:688
  251.4 55.5 %collective-permute-start.43 = (bf16[4,256,1024]{2,1,0:T(8,128)(2,1)}, bf16[4,256,1024]{2,1,0:T(8,128)(2,1)}, u32[]{:S(2)}, u32[]{:S(2)}) collective-permute-start(bf16[4,256,1024]{2,1,0:T(8,128)(2,1)} %pad_maximum_fusion.3.rest_2_), channel_id=1, source_target_pairs={{0,1},{1,0},{2,3},{3,2},{4,5},{5,4},{6,7},{7,6},{8,9},{9,8},{10,11... | collective-permute-start | bytes 6291464 | tf_op jit(solution)/shard_map/ppermute | solution.py:688
  251.6 69.9 %collective-permute-start.54 = (bf16[2,3,256,512]{3,2,1,0:T(8,128)(2,1)S(1)}, bf16[2,3,256,512]{3,2,1,0:T(8,128)(2,1)}, u32[]{:S(2)}, u32[]{:S(2)}) collective-permute-start(bf16[2,3,256,512]{3,2,1,0:T(8,128)(2,1)S(1)} %get-tuple-element.138.rest_0_), channel_id=1, source_target_pairs={{0,2},{1,3},{2,0},{3,1},{4,6},{5,7},{6,4},{7,5},{8,10},{9,11},{10,... | collective-permute-start | bytes 4718600 | tf_op jit(solution)/shard_map/ppermute | solution.py:688
  287.9 67.3 %collective-permute-start.56 = (bf16[2,3,256,512]{3,2,1,0:T(8,128)(2,1)}, bf16[2,3,256,512]{3,2,1,0:T(8,128)(2,1)}, u32[]{:S(2)}, u32[]{:S(2)}) collective-permute-start(bf16[2,3,256,512]{3,2,1,0:T(8,128)(2,1)} %collective-permute-done.55.rest_2_), channel_id=1, source_target_pairs={{0,2},{1,3},{2,0},{3,1},{4,6},{5,7},{6,4},{7,5},{8,10},{9,11},{10,... | collective-permute-start | bytes 4718600 | tf_op jit(solution)/shard_map/ppermute | solution.py:688
  409.2 58.1 %collective-permute-start.70 = (bf16[4,256,1024]{2,1,0:T(8,128)(2,1)}, bf16[4,256,1024]{2,1,0:T(8,128)(2,1)}, u32[]{:S(2)}, u32[]{:S(2)}) collective-permute-start(bf16[4,256,1024]{2,1,0:T(8,128)(2,1)} %get-tuple-element.76), channel_id=1, source_target_pairs={{0,1},{1,0},{2,3},{3,2},{4,5},{5,4},{6,7},{7,6},{8,9},{9,8},{10,11... | collective-permute-start | bytes 6291464 | tf_op jit(solution)/shard_map/ppermute | solution.py:688
  409.3 55.1 %collective-permute-start.101 = (bf16[2,3,256,512]{3,2,1,0:T(8,128)(2,1)}, bf16[2,3,256,512]{3,2,1,0:T(8,128)(2,1)}, u32[]{:S(2)}, u32[]{:S(2)}) collective-permute-start(bf16[2,3,256,512]{3,2,1,0:T(8,128)(2,1)} %get-tuple-element.101), channel_id=1, source_target_pairs={{0,2},{1,3},{2,0},{3,1},{4,6},{5,7},{6,4},{7,5},{8,10},{9,11},{10,... | collective-permute-start | bytes 4718600 | tf_op jit(solution)/shard_map/ppermute | solution.py:688
  411.3 59.2 %collective-permute-start.66 = (bf16[4,256,1024]{2,1,0:T(8,128)(2,1)}, bf16[4,256,1024]{2,1,0:T(8,128)(2,1)}, u32[]{:S(2)}, u32[]{:S(2)}) collective-permute-start(bf16[4,256,1024]{2,1,0:T(8,128)(2,1)} %get-tuple-element.74), channel_id=1, source_target_pairs={{0,1},{1,0},{2,3},{3,2},{4,5},{5,4},{6,7},{7,6},{8,9},{9,8},{10,11... | collective-permute-start | bytes 6291464 | tf_op jit(solution)/shard_map/ppermute | solution.py:688
  427.0 47.1 %collective-permute-start.61 = (bf16[4,272,1024]{2,1,0:T(8,128)(2,1)}, bf16[4,272,1024]{2,1,0:T(8,128)(2,1)}, u32[]{:S(2)}, u32[]{:S(2)}) collective-permute-start(bf16[4,272,1024]{2,1,0:T(8,128)(2,1)} %get-tuple-element.71), channel_id=1, source_target_pairs={{0,1},{1,0},{2,3},{3,2},{4,5},{5,4},{6,7},{7,6},{8,9},{9,8},{10,11... | collective-permute-start | bytes 6684680 | tf_op jit(solution)/shard_map/ppermute | solution.py:688
  431.6 46.1 %collective-permute-start.57 = (bf16[4,272,1024]{2,1,0:T(8,128)(2,1)}, bf16[4,272,1024]{2,1,0:T(8,128)(2,1)S(1)}, u32[]{:S(2)}, u32[]{:S(2)}) collective-permute-start(bf16[4,272,1024]{2,1,0:T(8,128)(2,1)} %get-tuple-element.69), channel_id=1, source_target_pairs={{0,1},{1,0},{2,3},{3,2},{4,5},{5,4},{6,7},{7,6},{8,9},{9,8},{10,11... | collective-permute-start | bytes 6684680 | tf_op jit(solution)/shard_map/ppermute | solution.py:688
  464.4 81.5 %collective-permute-start.103 = (bf16[2,3,256,512]{3,2,1,0:T(8,128)(2,1)S(1)}, bf16[2,3,256,512]{3,2,1,0:T(8,128)(2,1)S(1)}, u32[]{:S(2)}, u32[]{:S(2)}) collective-permute-start(bf16[2,3,256,512]{3,2,1,0:T(8,128)(2,1)S(1)} %add_convert_fusion), channel_id=1, source_target_pairs={{0,4},{1,5},{2,6},{3,7},{4,0},{5,1},{6,2},{7,3},{8,12},{9,13},{10,... | collective-permute-start | bytes 4718600 | tf_op jit(solution)/shard_map/ppermute | solution.py:688
  500.3 48.8 %collective-permute-start.67 = (bf16[256,1024]{1,0:T(8,128)(2,1)S(1)}, bf16[256,1024]{1,0:T(8,128)(2,1)S(1)}, u32[]{:S(2)}, u32[]{:S(2)}) collective-permute-start(bf16[256,1024]{1,0:T(8,128)(2,1)S(1)} %get-tuple-element.129), channel_id=1, source_target_pairs={{0,8},{8,0},{16,24},{24,16},{1,9},{9,1},{17,25},{25,17},{2,10},{10... | collective-permute-start | bytes 1572872 | tf_op jit(solution)/shard_map/ppermute | solution.py:688
  507.7 43.1 %collective-permute-start.69 = (bf16[256,1024]{1,0:T(8,128)(2,1)S(1)}, bf16[256,1024]{1,0:T(8,128)(2,1)S(1)}, u32[]{:S(2)}, u32[]{:S(2)}) collective-permute-start(bf16[256,1024]{1,0:T(8,128)(2,1)S(1)} %get-tuple-element.130), channel_id=1, source_target_pairs={{0,24},{8,16},{16,8},{24,0},{1,25},{9,17},{17,9},{25,1},{2,26},{10... | collective-permute-start | bytes 1572872 | tf_op jit(solution)/shard_map/ppermute | solution.py:688
  524.0 45.0 %collective-permute-start.74 = (bf16[256,1024]{1,0:T(8,128)(2,1)S(1)}, bf16[256,1024]{1,0:T(8,128)(2,1)S(1)}, u32[]{:S(2)}, u32[]{:S(2)}) collective-permute-start(bf16[256,1024]{1,0:T(8,128)(2,1)S(1)} %fusion.14), channel_id=1, source_target_pairs={{0,4},{1,5},{2,6},{3,7},{4,0},{5,1},{6,2},{7,3},{8,12},{9,13},{10,... | collective-permute-start | bytes 1572872 | tf_op jit(solution)/shard_map/ppermute | solution.py:688
  545.9 94.7 %collective-permute-start.58 = (bf16[272,1024]{1,0:T(8,128)(2,1)}, bf16[272,1024]{1,0:T(8,128)(2,1)S(1)}, u32[]{:S(2)}, u32[]{:S(2)}) collective-permute-start(bf16[272,1024]{1,0:T(8,128)(2,1)} %get-tuple-element.121), channel_id=1, source_target_pairs={{0,8},{8,0},{16,24},{24,16},{1,9},{9,1},{17,25},{25,17},{2,10},{10... | collective-permute-start | bytes 1671176 | tf_op jit(solution)/shard_map/ppermute | solution.py:688
  549.1 92.1 %collective-permute-start.60 = (bf16[272,1024]{1,0:T(8,128)(2,1)S(1)}, bf16[272,1024]{1,0:T(8,128)(2,1)S(1)}, u32[]{:S(2)}, u32[]{:S(2)}) collective-permute-start(bf16[272,1024]{1,0:T(8,128)(2,1)S(1)} %get-tuple-element.122), channel_id=1, source_target_pairs={{0,24},{8,16},{16,8},{24,0},{1,25},{9,17},{17,9},{25,1},{2,26},{10... | collective-permute-start | bytes 1671176 | tf_op jit(solution)/shard_map/ppermute | solution.py:688
  550.8 90.5 %collective-permute-start.59 = (bf16[272,1024]{1,0:T(8,128)(2,1)S(1)}, bf16[272,1024]{1,0:T(8,128)(2,1)S(1)}, u32[]{:S(2)}, u32[]{:S(2)}) collective-permute-start(bf16[272,1024]{1,0:T(8,128)(2,1)S(1)} %get-tuple-element.123), channel_id=1, source_target_pairs={{0,16},{8,24},{16,0},{24,8},{1,17},{9,25},{17,1},{25,9},{2,18},{10... | collective-permute-start | bytes 1671176 | tf_op jit(solution)/shard_map/ppermute | solution.py:688
  552.0 89.7 %collective-permute-start.65 = (bf16[272,1024]{1,0:T(8,128)(2,1)S(1)}, bf16[272,1024]{1,0:T(8,128)(2,1)}, u32[]{:S(2)}, u32[]{:S(2)}) collective-permute-start(bf16[272,1024]{1,0:T(8,128)(2,1)S(1)} %fusion.5), channel_id=1, source_target_pairs={{0,4},{1,5},{2,6},{3,7},{4,0},{5,1},{6,2},{7,3},{8,12},{9,13},{10,... | collective-permute-start | bytes 1671176 | tf_op jit(solution)/shard_map/ppermute | solution.py:688
  578.0 71.4 %collective-permute-start.90 = (bf16[256,640]{1,0:T(8,128)(2,1)}, bf16[256,640]{1,0:T(8,128)(2,1)}, u32[]{:S(2)}, u32[]{:S(2)}) collective-permute-start(bf16[256,640]{1,0:T(8,128)(2,1)} %get-tuple-element.93), channel_id=1, source_target_pairs={{0,1},{1,0},{2,3},{3,2},{4,5},{5,4},{6,7},{7,6},{8,9},{9,8},{10,11... | collective-permute-start | bytes 983048 | tf_op jit(solution)/shard_map/ppermute | solution.py:688
  (155 other events, 2652.1 us)

commit v2 on v1

v2 whole, which is shorter than its diff:
```python
import functools

import jax
import jax.numpy as jnp
from jax import lax
from jax.experimental import pallas as pl
from jax.experimental.pallas import tpu as pltpu
from jax.sharding import PartitionSpec as P

H = 16
KVH = 8
HD = 64
EXPERTS = 32
TOP = 8
CAP = 80
EPSILON = 1e-06
LANES = 128
PAIRS = KVH // 2
GATE_ROWS = 16

BF = jnp.bfloat16
F32 = jnp.float32
VMEM_BYTES = 56 * 1024 * 1024


def dot(left, right):
    return lax.dot_general(left, right, (((1,), (0,)), ((), ())), preferred_element_type=F32)


def dot_nt(left, right):
    return lax.dot_general(left, right, (((1,), (1,)), ((), ())), preferred_element_type=F32)


def dot_tn(left, right):
    return lax.dot_general(left, right, (((0,), (0,)), ((), ())), preferred_element_type=F32)


def call(kernel, grid, scalars, inputs, in_specs, out_shapes, out_specs, scratch=(), aliases=None):
    return pl.pallas_call(
        kernel,
        grid_spec=pltpu.PrefetchScalarGridSpec(
            num_scalar_prefetch=1,
            grid=grid,
            in_specs=in_specs,
            out_specs=out_specs,
            scratch_shapes=list(scratch),
        ),
        out_shape=out_shapes,
        input_output_aliases=aliases or {},
        compiler_params=pltpu.CompilerParams(vmem_limit_bytes=VMEM_BYTES),
        cost_estimate=pl.CostEstimate(flops=0, bytes_accessed=0, transcendentals=0),
    )(scalars, *inputs)


def whole_spec(shape):
    return pl.BlockSpec(tuple(shape), lambda *_: (0,) * len(shape))


def lane_ids(rows):
    return lax.broadcasted_iota(jnp.int32, (rows, LANES), 1)


def swap_halves(tile):
    first = lane_ids(tile.shape[0]) % HD < HD // 2
    return jnp.where(first, pltpu.roll(tile, LANES - HD // 2, 1), pltpu.roll(tile, HD // 2, 1))


def turn(value, cosine, signed_sine, direction):
    tiles = []
    for i in range(value.shape[1] // LANES):
        tile = value[:, i * LANES : (i + 1) * LANES]
        tiles.append(tile * cosine + direction * (swap_halves(tile) * signed_sine))
    return tiles[0] if len(tiles) == 1 else jnp.concatenate(tiles, axis=1)


def row_chunk(ids, r, count):
    return ids[0] ^ r if count > 1 else 0


def z_chunk(ids, r, count):
    return ids[1] ^ r if count > 1 else 0


def half_chunk(ids, h, count):
    return ids[2] ^ h if count > 1 else 0


def span(index, size):
    return pl.ds(pl.multiple_of(index * size, size), size)


def columns(nh, width):
    on, qn, kn = width // nh, H * HD // nh, KVH * HD // nh
    return on, on + qn, on + qn + kn, on + qn + 2 * kn


def qkv_kernel(nr, nh, ids, rows_ref, gain_ref, cos_ref, sin_ref, *rest):
    weights = rest[:nh]
    q_ref, k_ref, v_ref, normed_ref = rest[nh:]
    width = rows_ref.shape[-1]
    chunk = width // nr
    qn, kn = H * HD // nh, KVH * HD // nh
    at_q, at_k, _, at_end = columns(nh, width)
    normed_ref[...] = (rows_ref[0].astype(F32) * gain_ref[...]).astype(BF)
    cosine, sine = cos_ref[...], sin_ref[...]
    for h in range(nh):
        total = None
        for r in range(nr):
            part = dot(
                normed_ref[:, span(row_chunk(ids, r, nr), chunk)],
                weights[h][r, :, at_k:at_end],
            )
            total = part if total is None else total + part
        here = span(half_chunk(ids, h, nh), kn)
        k_ref[:, here] = turn(total[:, :kn], cosine, sine, 1.0).astype(BF)
        v_ref[:, here] = total[:, kn:].astype(BF)

    @pl.when(pl.program_id(0) == 0)
    def _():
        for h in range(nh):
            total = None
            for r in range(nr):
                part = dot(
                    normed_ref[:, span(row_chunk(ids, r, nr), chunk)], weights[h][r, :, at_q:at_k]
                )
                total = part if total is None else total + part
            turned = turn(total, cosine, sine, 1.0).astype(BF).astype(F32) * HD**-0.5
            q_ref[:, span(half_chunk(ids, h, nh), qn)] = turned.astype(BF)


def project(ids, rows, gain, cosine, sine, weights):
    slots, length, width = rows.shape
    nr, nh = weights[0].shape[0], len(weights)
    flat = weights
    return call(
        functools.partial(qkv_kernel, nr, nh),
        (slots,),
        ids,
        [rows, gain, cosine, sine, *flat],
        [
            pl.BlockSpec((1, length, width), lambda i, _: (i, 0, 0)),
            whole_spec(gain.shape),
            pl.BlockSpec((length, LANES), lambda i, _: (i, 0)),
            pl.BlockSpec((length, LANES), lambda i, _: (i, 0)),
            *[whole_spec(w.shape) for w in flat],
        ],
        [
            jax.ShapeDtypeStruct((length, H * HD), BF),
            jax.ShapeDtypeStruct((slots * length, KVH * HD), BF),
            jax.ShapeDtypeStruct((slots * length, KVH * HD), BF),
        ],
        [
            whole_spec((length, H * HD)),
            pl.BlockSpec((length, KVH * HD), lambda i, _: (i, 0)),
            pl.BlockSpec((length, KVH * HD), lambda i, _: (i, 0)),
        ],
        [pltpu.VMEM((length, width), BF)],
    )


def to_half(tile, which, wanted):
    if which != wanted:
        tile = pltpu.roll(tile, HD, 1)
    return jnp.where(lane_ids(tile.shape[0]) // HD == wanted, tile, 0.0)


def attend_kernel(ids, q_ref, k_ref, v_ref, kx_ref, qx_ref, o_ref, low_ref, lse_ref):
    keys = jnp.concatenate([k_ref[...], kx_ref[...]], axis=1)
    values = v_ref[...]
    extra = qx_ref[...]
    rows = q_ref.shape[0]
    lanes = lane_ids(rows)
    sums = jnp.zeros((rows, LANES), F32)
    for t in range(2):
        tile = q_ref[:, t * LANES : (t + 1) * LANES].astype(F32)
        mixed = jnp.zeros((rows, LANES), F32)
        for w in range(2):
            query = jnp.concatenate([to_half(tile, w, t).astype(BF), extra], axis=1)
            scores = dot_nt(query, keys)
            highest = jnp.max(scores, axis=1, keepdims=True)
            weights = jnp.exp(scores - highest)
            total = jnp.sum(weights, axis=1, keepdims=True)
            out = dot(weights.astype(BF), values) / total
            mixed = mixed + to_half(out, t, w)
            sums = jnp.where(lanes == 2 * t + w, highest + jnp.log(total), sums)
        o_ref[:, t * LANES : (t + 1) * LANES] = mixed
        low_ref[:, t * LANES : (t + 1) * LANES] = mixed.astype(BF)
    lse_ref[0] = sums


def attend(ids, q, k, v, key_extra, query_extra):
    length, keys = q.shape[0], k.shape[0]
    quad = pl.BlockSpec((length, 2 * LANES), lambda p, _: (0, p))
    pair = pl.BlockSpec((keys, LANES), lambda p, _: (0, p))
    return call(
        attend_kernel,
        (PAIRS,),
        ids,
        [q, k, v, key_extra, query_extra],
        [quad, pair, pair, whole_spec(key_extra.shape), whole_spec(query_extra.shape)],
        [
            jax.ShapeDtypeStruct((length, H * HD), F32),
            jax.ShapeDtypeStruct((length, H * HD), BF),
            jax.ShapeDtypeStruct((PAIRS, length, LANES), F32),
        ],
        [quad, quad, pl.BlockSpec((1, length, LANES), lambda p, _: (p, 0, 0))],
    )


def three_parts(value):
    high = value.astype(BF)
    rest = value - high.astype(F32)
    middle = rest.astype(BF)
    return high.astype(F32), middle.astype(F32), (rest - middle.astype(F32))


def with_parts(base, value, lanes):
    high, middle, low = three_parts(value)
    base = jnp.where(lanes == 16, high, base)
    base = jnp.where(lanes == 17, middle, base)
    return jnp.where(lanes == 18, low, base).astype(BF)


def attend_back_kernel(
    span_rows, ids, q_ref, do_ref, o_ref, lse_ref, k_ref, v_ref, kx_ref, qx_ref, cos_ref, sin_ref,
    dq_ref, own_ref, other_ref, sum_ref,
):
    rows = q_ref.shape[0]
    lanes = lane_ids(rows)
    extra = qx_ref[...].astype(F32)
    nothing = jnp.zeros((rows, LANES), F32)
    sums = lse_ref[0]
    queries, outs, pads_q, pads_o = [], [], [], []
    for t in range(2):
        at = slice(t * LANES, (t + 1) * LANES)
        tile, grad = q_ref[:, at].astype(F32), do_ref[:, at].astype(F32)
        product = grad * o_ref[:, at]
        for w in range(2):
            here = lanes // HD == w
            delta = jnp.sum(jnp.where(here, product, 0.0), axis=1, keepdims=True)
            log_sum = jnp.sum(jnp.where(lanes == 2 * t + w, sums, 0.0), axis=1, keepdims=True)
            q_pad = to_half(tile, w, t).astype(BF)
            o_pad = to_half(grad, w, t).astype(BF)
            queries.append(jnp.concatenate([q_pad, with_parts(extra, -log_sum, lanes)], axis=1))
            outs.append(jnp.concatenate([o_pad, with_parts(nothing, -delta, lanes)], axis=1))
            pads_q.append(q_pad)
            pads_o.append(o_pad)
    all_q = jnp.concatenate(pads_q, axis=0)
    all_o = jnp.concatenate(pads_o, axis=0)
    sum_ref[...] = jnp.zeros_like(sum_ref)

    spans = k_ref.shape[0] // 2 // span_rows

    def one_span(i, _, part, out_ref):
        put = pl.ds(pl.multiple_of(i * span_rows, span_rows), span_rows)
        first = part * spans * span_rows
        at = pl.ds(pl.multiple_of(first + i * span_rows, span_rows), span_rows)
        k_here, x_here = k_ref[at, :], kx_ref[at, :]
        keys = jnp.concatenate([k_here, x_here], axis=1)
        values = jnp.concatenate([v_ref[at, :], x_here], axis=1)
        probs, d_scores = [], []
        for n in range(4):
            prob = jnp.exp(dot_nt(keys, queries[n]))
            d_score = (prob * dot_nt(values, outs[n])).astype(BF)
            probs.append(prob.astype(BF))
            d_scores.append(d_score)
            sum_ref[n] += dot_tn(d_score, k_here)
        out_ref[1, put, :] = dot(jnp.concatenate(probs, axis=1), all_o).astype(BF)
        d_key = dot(jnp.concatenate(d_scores, axis=1), all_q)
        d_key = turn(d_key, cos_ref[at, :], sin_ref[at, :], -1.0)
        out_ref[0, put, :] = d_key.astype(BF)
        return 0

    for part, out_ref in enumerate((own_ref, other_ref)):
        lax.fori_loop(0, spans, functools.partial(one_span, part=part, out_ref=out_ref), 0)
    cosine, sine = cos_ref[:rows, :], sin_ref[:rows, :]
    for t in range(2):
        tile = to_half(sum_ref[2 * t], t, 0) + to_half(sum_ref[2 * t + 1], t, 1)
        turned = turn(tile * HD**-0.5, cosine, sine, -1.0)
        dq_ref[:, t * LANES : (t + 1) * LANES] = turned.astype(BF)


def attend_back_part(*refs):
    attend_back_kernel(512, *refs[:11], *refs[14:])


def attend_back(ids, q, d_out, out, lse, k, v, key_extra, query_extra, cosine, sine, first, count, done):
    length, keys = q.shape[0], k.shape[0]
    quad = pl.BlockSpec((length, 2 * LANES), lambda p, _: (0, first + p))
    pair = pl.BlockSpec((keys, LANES), lambda p, _: (0, first + p))
    ins = [q, d_out, out, lse, k, v, key_extra, query_extra, cosine, sine]
    specs = [
        quad,
        quad,
        quad,
        pl.BlockSpec((1, length, LANES), lambda p, _: (first + p, 0, 0)),
        pair,
        pair,
        whole_spec(key_extra.shape),
        whole_spec(query_extra.shape),
        whole_spec(cosine.shape),
        whole_spec(sine.shape),
    ]
    if done is not None:
        ins += done
        specs += [pl.BlockSpec(memory_space=pl.ANY)] * 3
    return call(
        attend_back_part if done is not None else functools.partial(attend_back_kernel, 512),
        (count,),
        ids,
        ins,
        specs,
        [
            jax.ShapeDtypeStruct((length, H * HD), BF),
            jax.ShapeDtypeStruct((2, keys // 2, KVH * HD), BF),
            jax.ShapeDtypeStruct((2, keys // 2, KVH * HD), BF),
        ],
        [quad] + [pl.BlockSpec((2, keys // 2, LANES), lambda p, _: (0, 0, first + p))] * 2,
        [pltpu.VMEM((4, length, LANES), F32)],
        aliases={11: 0, 12: 1, 13: 2} if done is not None else None,
    )


def out_kernel(nr, nh, ids, x_ref, o_ref, gain_ref, *rest):
    weights = rest[:nh]
    x2_ref, n2_ref = rest[nh:]
    width = x_ref.shape[1]
    chunk, cols = H * HD // nr, width // nh
    for h in range(nh):
        at = span(half_chunk(ids, h, nh), cols)
        total = x_ref[:, at]
        for r in range(nr):
            total = total + dot(
                o_ref[:, span(row_chunk(ids, r, nr), chunk)], weights[h][r]
            )
        x2_ref[:, at] = total
    middle = x2_ref[...]
    inverse = lax.rsqrt(jnp.mean(middle * middle, axis=1, keepdims=True) + EPSILON)
    n2_ref[...] = (middle * inverse * gain_ref[...]).astype(BF)


def out_spec(weight, cols):
    return pl.BlockSpec(weight.shape[:2] + (cols,), lambda *_: (0, 0, 0))


def project_out(ids, x, low, gain, weights):
    nr, nh = weights[0].shape[0], len(weights)
    ins = [x, low, gain, *weights]
    outs = [jax.ShapeDtypeStruct(x.shape, F32), jax.ShapeDtypeStruct(x.shape, BF)]
    return call(
        functools.partial(out_kernel, nr, nh),
        (1,),
        ids,
        ins,
        [whole_spec(i.shape) for i in ins[:3]] + [out_spec(w, x.shape[1] // nh) for w in weights],
        outs,
        [whole_spec(o.shape) for o in outs],
    )


def out_back_kernel(nr, nh, ids, c_ref, x2_ref, gain_ref, dn2_ref, low_ref, *rest):
    weights = rest[:nh]
    dx2_ref, do_ref = rest[nh : nh + 2]
    grads = rest[nh + 2 : 2 * nh + 2]
    dr_ref, term_ref = rest[2 * nh + 2 :]
    width = c_ref.shape[1]
    chunk, cols = H * HD // nr, width // nh
    middle, d_normed = x2_ref[...], dn2_ref[...]
    inverse = lax.rsqrt(jnp.mean(middle * middle, axis=1, keepdims=True) + EPSILON)
    scaled = d_normed * gain_ref[...]
    inner = jnp.mean(scaled * middle, axis=1, keepdims=True)
    d_middle = c_ref[...] + inverse * scaled - middle * (inverse * inverse * inverse * inner)
    dx2_ref[...] = d_middle
    dr_ref[...] = d_middle.astype(BF)
    term_ref[...] = (d_normed * middle * inverse).astype(BF)
    ones = jnp.ones((middle.shape[0], LANES), BF)
    for r in range(nr):
        at = span(row_chunk(ids, r, nr), chunk)
        low = low_ref[:, at]
        gain_grad = dot_tn(term_ref[:, at], ones).astype(BF)
        total = None
        for h in range(nh):
            branch = dr_ref[:, span(half_chunk(ids, h, nh), cols)]
            part = dot_nt(branch, weights[h][r])
            total = part if total is None else total + part
            grads[h][r, :, :cols] = dot_tn(low, branch).astype(BF)
            grads[h][r, :, cols:] = gain_grad
        do_ref[:, at] = total.astype(BF)


def project_out_back(ids, c, x2, gain, dn2, low, weights):
    nr, nh = weights[0].shape[0], len(weights)
    ins = [c, x2, gain, dn2, low, *weights]
    rows, cols = H * HD // nr, c.shape[1] // nh
    outs = [jax.ShapeDtypeStruct(c.shape, F32), jax.ShapeDtypeStruct((c.shape[0], H * HD), BF)]
    outs += [jax.ShapeDtypeStruct((nr, rows, cols + LANES), BF)] * nh
    got = call(
        functools.partial(out_back_kernel, nr, nh),
        (1,),
        ids,
        ins,
        [whole_spec(i.shape) for i in ins[:5]] + [out_spec(w, cols) for w in weights],
        outs,
        [whole_spec(o.shape) for o in outs],
        [pltpu.VMEM(c.shape, BF), pltpu.VMEM(c.shape, BF)],
    )
    return got[0], got[1], got[2:]


def picks(slot_ref, experts):
    tokens = slot_ref.shape[-1]
    places = lax.broadcasted_iota(jnp.int32, (CAP, tokens), 0).astype(F32)
    rows = [places == slot_ref[0, j : j + 1, :] for j in range(experts)]
    return rows[0] if experts == 1 else jnp.concatenate(rows, axis=0)


def gather_kernel(groups, per, experts, with_gates, ids, slot_ref, *rest):
    if with_gates:
        gate_ref, rest = rest[0], rest[1:]
    tokens, out_ref = rest[:groups], rest[groups]
    chosen = picks(slot_ref, experts)
    low = chosen.astype(F32).astype(BF)
    for g in range(groups):

        @pl.when(pl.program_id(0) // per == g)
        def _(g=g):
            rows = dot(low, tokens[g][0, : slot_ref.shape[-1]]).astype(BF)
            for j in range(experts):
                out_ref[j, 0] = rows[j * CAP : (j + 1) * CAP]

    if with_gates:
        for j in range(experts):
            mine = chosen[j * CAP : (j + 1) * CAP]
            gates = jnp.sum(jnp.where(mine, gate_ref[0, j : j + 1, :], 0.0), axis=1, keepdims=True)
            rest[groups + 1][j, 0] = jnp.broadcast_to(gates, (CAP, LANES))


def gather_rows(ids, slots, groups, gates=None):
    blocks, experts, length = slots.shape
    per, width = groups[0].shape[0], groups[0].shape[-1]
    ins, specs = [slots], [pl.BlockSpec((1, experts, length), lambda i, _: (i, 0, 0))]
    if gates is not None:
        ins.append(gates)
        specs.append(specs[0])
    for g, tokens in enumerate(groups):
        ins.append(tokens)
        specs.append(
            pl.BlockSpec(
                (1,) + tokens.shape[1:], lambda i, _, g=g: (jnp.clip(i - g * per, 0, per - 1), 0, 0)
            )
        )
    outs = [jax.ShapeDtypeStruct((experts, blocks, CAP, width), BF)]
    out_specs = [pl.BlockSpec((experts, 1, CAP, width), lambda i, _: (0, i, 0, 0))]
    if gates is not None:
        outs.append(jax.ShapeDtypeStruct((experts, blocks, CAP, LANES), F32))
        out_specs.append(pl.BlockSpec((experts, 1, CAP, LANES), lambda i, _: (0, i, 0, 0)))
    return call(
        functools.partial(gather_kernel, len(groups), per, experts, gates is not None),
        (blocks,),
        ids,
        ins,
        specs,
        outs,
        out_specs,
    )


def expert_kernel(nz, ids, x_ref, c_ref, gate_ref, *rest):
    weights, rest = rest[:nz], rest[nz:]
    y_ref, dx_ref, gg_ref = rest[:3]
    grads, acc_ref = rest[3 : 3 + nz], rest[3 + nz]
    chunk = x_ref.shape[-1] // nz
    step, last = pl.program_id(1), pl.num_programs(1) - 1
    a = b = ch = None
    for r in range(nz):
        at = span(z_chunk(ids, r, nz), chunk)
        x, c = x_ref[0, :, at], c_ref[0, :, at]
        parts = (
            dot(x, weights[r][0, 0]),
            dot(x, weights[r][0, 1]),
            dot(c, weights[r][0, 2]),
        )
        a, b, ch = parts if a is None else (a + parts[0], b + parts[1], ch + parts[2])
    gate = gate_ref[0][:, :1]
    sig = 1.0 / (1.0 + jnp.exp(-a))
    act = a * sig
    hidden = (act * b).astype(BF).astype(F32)
    gg_ref[0] = jnp.broadcast_to(jnp.sum(hidden * ch, axis=1, keepdims=True), gg_ref.shape[1:])
    hg = (hidden * gate).astype(BF)
    dh = ch * gate
    da = (dh * b * sig * (1.0 + a * (1.0 - sig))).astype(BF)
    db = (dh * act).astype(BF)

    @pl.when(step == 0)
    def _():
        acc_ref[...] = jnp.zeros_like(acc_ref)

    for r in range(nz):
        at = span(z_chunk(ids, r, nz), chunk)
        x, c = x_ref[0, :, at], c_ref[0, :, at]
        y_ref[0, :, at] = dot_nt(hg, weights[r][0, 2]).astype(BF)
        dx_ref[0, :, at] = (dot_nt(da, weights[r][0, 0]) + dot_nt(db, weights[r][0, 1])).astype(BF)
        acc_ref[r, 0] += dot_tn(x, da)
        acc_ref[r, 1] += dot_tn(x, db)
        acc_ref[r, 2] += dot_tn(c, hg)

    @pl.when(step == last)
    def _():
        for r in range(nz):
            grads[r][0] = acc_ref[r].astype(BF)


def run_experts(ids, x_rows, c_rows, gate_rows, weights):
    experts, rows, width = x_rows.shape
    nz = len(weights)
    hidden = weights[0].shape[-1]
    tile = 256
    block = pl.BlockSpec((1, tile, width), lambda j, i, _: (j, i, 0))
    narrow = pl.BlockSpec((1, tile, LANES), lambda j, i, _: (j, i, 0))
    matrix = pl.BlockSpec((1,) + weights[0].shape[1:], lambda j, i, _: (j, 0, 0, 0))
    got = call(
        functools.partial(expert_kernel, nz),
        (experts, rows // tile),
        ids,
        [x_rows, c_rows, gate_rows, *weights],
        [block, block, narrow] + [matrix] * nz,
        [
            jax.ShapeDtypeStruct(x_rows.shape, BF),
            jax.ShapeDtypeStruct(x_rows.shape, BF),
            jax.ShapeDtypeStruct((experts, rows, LANES), F32),
        ]
        + [jax.ShapeDtypeStruct(w.shape, BF) for w in weights],
        [block, block, narrow] + [matrix] * nz,
        [pltpu.VMEM((nz,) + weights[0].shape[1:], F32)],
    )
    return got[0], got[1], got[2], got[3:]


def spread_kernel(groups, per, experts, with_grads, ids, slot_ref, rows_ref, *rest):
    if with_grads:
        grad_ref, rest = rest[0], rest[1:]
    chosen = picks(slot_ref, experts)
    low = chosen.astype(F32).astype(BF)
    rows = [rows_ref[j, 0] for j in range(experts)]
    rows = rows[0] if experts == 1 else jnp.concatenate(rows, axis=0)
    total = dot_tn(low, rows).astype(BF)
    length, width = total.shape
    tail = None
    if with_grads:
        fit = width // length
        line = lax.broadcasted_iota(jnp.int32, (GATE_ROWS, width), 0)
        place = lax.broadcasted_iota(jnp.int32, (GATE_ROWS, width), 1) // length
        tail = jnp.zeros((GATE_ROWS, width), F32)
        for j in range(experts):
            mine = chosen[j * CAP : (j + 1) * CAP]
            sums = jnp.sum(jnp.where(mine, grad_ref[j, 0][:, :1], 0.0), axis=0, keepdims=True)
            wide = jnp.concatenate([sums] * fit, axis=1)
            number = ids[3] + j
            tail = tail + jnp.where((line == number // fit) & (place == number % fit), wide, 0.0)
    for g in range(groups):

        @pl.when(pl.program_id(0) // per == g)
        def _(g=g):
            rest[g][0, :length] = total
            if with_grads:
                rest[g][0, length:] = tail.astype(BF)


def spread_rows(ids, slots, rows, groups, grads=None):
    blocks, experts, length = slots.shape
    per, width = blocks // groups, rows.shape[-1]
    high = length + (GATE_ROWS if grads is not None else 0)
    ins = [slots, rows]
    specs = [
        pl.BlockSpec((1, experts, length), lambda i, _: (i, 0, 0)),
        pl.BlockSpec((experts, 1, CAP, width), lambda i, _: (0, i, 0, 0)),
    ]
    if grads is not None:
        ins.append(grads)
        specs.append(pl.BlockSpec((experts, 1, CAP, LANES), lambda i, _: (0, i, 0, 0)))
    return call(
        functools.partial(spread_kernel, groups, per, experts, grads is not None),
        (blocks,),
        ids,
        ins,
        specs,
        [jax.ShapeDtypeStruct((per, high, width), BF)] * groups,
        [
            pl.BlockSpec(
                (1, high, width), lambda i, _, g=g: (jnp.clip(i - g * per, 0, per - 1), 0, 0)
            )
            for g in range(groups)
        ],
    )


def mixture_kernel(nz, groups, per, experts, tile, ids, slot_ref, gate_ref, *rest):
    n2_in, rest = rest[:groups], rest[groups:]
    c_in, rest = rest[:groups], rest[groups:]
    w_in, rest = rest[: 3 * nz], rest[3 * nz :]
    dn2_out, rest = rest[:groups], rest[groups:]
    y_out, rest = rest[: groups // 2], rest[groups // 2 :]
    dw_out, rest = rest[:nz], rest[nz:]
    n2_ref, c_ref, w_ref, x_rows, c_rows, gate_rows, grad_rows, inner_ref, dw_ref = rest[:9]
    n2_sem, c_sem, w_sem, dn2_sem, y_sem, dw_sem = rest[9:]
    length = slot_ref.shape[-1]
    width = n2_ref.shape[-1]
    chunk = width // nz
    blocks = groups * per

    def n2_copy(g):
        return pltpu.make_async_copy(n2_in[g], n2_ref.at[pl.ds(g * per, per)], n2_sem.at[g])

    def c_copy(g):
        return pltpu.make_async_copy(c_in[g], c_ref.at[pl.ds(g * per, per)], c_sem.at[g])

    def w_copy(r, k):
        return pltpu.make_async_copy(w_in[3 * r + k], w_ref.at[r, :, k], w_sem.at[r, k])

    for g in range(groups):
        c_copy(g).start()
        n2_copy(g).start()
    for r in range(nz):
        for k in range(3):
            w_copy(r, k).start()

    def chosen_rows(i):
        places = lax.broadcasted_iota(jnp.int32, (CAP, length), 0).astype(F32)
        return [places == slot_ref[i, j : j + 1, :] for j in range(experts)]

    def one_hot(chosen):
        chosen = [jnp.where(c, 1.0, 0.0).astype(BF) for c in chosen]
        return chosen[0] if experts == 1 else jnp.concatenate(chosen, axis=0)

    def gather(i, _):
        chosen = chosen_rows(i)
        low = one_hot(chosen)
        at = pl.ds(pl.multiple_of(i * CAP, CAP), CAP)
        got_x = dot(low, n2_ref[i]).astype(BF)
        got_c = dot(low, c_ref[i, :length]).astype(BF)
        for j in range(experts):
            x_rows[j, at] = got_x[j * CAP : (j + 1) * CAP]
            c_rows[j, at] = got_c[j * CAP : (j + 1) * CAP]
            gates = jnp.where(chosen[j], gate_ref[i, j : j + 1, :], 0.0)
            gate_rows[j, at] = jnp.broadcast_to(jnp.sum(gates, axis=1, keepdims=True), (CAP, LANES))
        return 0

    for g in range(groups):
        c_copy(g).wait()
        n2_copy(g).wait()
        lax.fori_loop(g * per, (g + 1) * per, gather, 0)
    for r in range(nz):
        for k in range(3):
            w_copy(r, k).wait()

    def dw_copy(j, r):
        return pltpu.make_async_copy(dw_ref.at[j, r], dw_out[r].at[j], dw_sem.at[j, r])

    for j in range(experts):

        def one_tile(i, _, j=j):
            at = pl.ds(pl.multiple_of(i * tile, tile), tile)
            a = b = ch = None
            for r in range(nz):
                cols = span(z_chunk(ids, r, nz), chunk)
                x, c = x_rows[j, at, cols], c_rows[j, at, cols]
                parts = (dot(x, w_ref[r, j, 0]), dot(x, w_ref[r, j, 1]), dot(c, w_ref[r, j, 2]))
                a, b, ch = parts if a is None else (a + parts[0], b + parts[1], ch + parts[2])
            gate = gate_rows[j, at][:, :1]
            sig = 1.0 / (1.0 + jnp.exp(-a))
            act = a * sig
            hidden = (act * b).astype(BF).astype(F32)
            grad = jnp.sum(hidden * ch, axis=1, keepdims=True)
            grad_rows[j, at] = jnp.broadcast_to(grad, (tile, LANES))
            hg = (hidden * gate).astype(BF)
            dh = ch * gate
            da = (dh * b * sig * (1.0 + a * (1.0 - sig))).astype(BF)
            db = (dh * act).astype(BF)
            inner_ref[0, at], inner_ref[1, at], inner_ref[2, at] = da, db, hg
            return 0

        lax.fori_loop(0, blocks * CAP // tile, one_tile, 0)
        for r in range(nz):
            cols = span(z_chunk(ids, r, nz), chunk)
            x, c = x_rows[j, :, cols], c_rows[j, :, cols]
            for k in range(3):
                dw_ref[j, r, k] = dot_tn(c if k == 2 else x, inner_ref[k]).astype(BF)
            dw_copy(j, r).start()

        def back_tile(i, _, j=j):
            at = pl.ds(pl.multiple_of(i * tile, tile), tile)
            da, db, hg = inner_ref[0, at], inner_ref[1, at], inner_ref[2, at]
            for r in range(nz):
                cols = span(z_chunk(ids, r, nz), chunk)
                c_rows[j, at, cols] = dot_nt(hg, w_ref[r, j, 2]).astype(BF)
                x_rows[j, at, cols] = (dot_nt(da, w_ref[r, j, 0]) + dot_nt(db, w_ref[r, j, 1])).astype(BF)
            return 0

        lax.fori_loop(0, blocks * CAP // tile, back_tile, 0)

    fit = width // length
    line = lax.broadcasted_iota(jnp.int32, (GATE_ROWS, width), 0)
    place = lax.broadcasted_iota(jnp.int32, (GATE_ROWS, width), 1) // length

    def spread(i, _):
        chosen = chosen_rows(i)
        low = one_hot(chosen)
        at = pl.ds(pl.multiple_of(i * CAP, CAP), CAP)
        both = []
        for rows_ref in (x_rows, c_rows):
            rows = [rows_ref[j, at] for j in range(experts)]
            both.append(rows[0] if experts == 1 else jnp.concatenate(rows, axis=0))
        n2_ref[i] = dot_tn(low, both[0]).astype(BF)
        c_ref[i, :length] = dot_tn(low, both[1]).astype(BF)
        tail = jnp.zeros((GATE_ROWS, width), F32)
        for j in range(experts):
            sums = jnp.where(chosen[j], grad_rows[j, at][:, :1], 0.0)
            wide = jnp.concatenate([jnp.sum(sums, axis=0, keepdims=True)] * fit, axis=1)
            number = ids[3] + j
            tail = tail + jnp.where((line == number // fit) & (place == number % fit), wide, 0.0)
        c_ref[i, length:] = tail.astype(BF)
        return 0

    def dn2_copy(g):
        return pltpu.make_async_copy(n2_ref.at[pl.ds(g * per, per)], dn2_out[g], dn2_sem.at[g])

    def y_copy(g):
        here = pl.ds((g % (groups // 2)) * per, per)
        return pltpu.make_async_copy(
            c_ref.at[pl.ds(g * per, per)], y_out[g // (groups // 2)].at[here], y_sem.at[g]
        )

    for g in range(groups):
        lax.fori_loop(g * per, (g + 1) * per, spread, 0)
        dn2_copy(g).start()
        y_copy(g).start()
    for g in range(groups):
        dn2_copy(g).wait()
        y_copy(g).wait()
    for j in range(experts):
        for r in range(nz):
            dw_copy(j, r).wait()


def mixture(ids, slots, gates, n2_groups, c_groups, weights):
    groups, nz = len(n2_groups), len(weights)
    per, length, width = n2_groups[0].shape
    blocks, experts, _ = slots.shape
    high, rows = c_groups[0].shape[1], blocks * CAP
    part = weights[0][0].shape
    matrices = (part[0], 3) + part[1:]
    anywhere = pl.BlockSpec(memory_space=pl.ANY)
    outs = [jax.ShapeDtypeStruct((per, length, width), BF)] * groups
    outs += [jax.ShapeDtypeStruct((groups // 2 * per, high, width), BF)] * 2
    outs += [jax.ShapeDtypeStruct(matrices, BF)] * nz
    got = call(
        functools.partial(mixture_kernel, nz, groups, per, experts, 256),
        (1,),
        ids,
        [slots, gates, *n2_groups, *c_groups, *[w for row in weights for w in row]],
        [whole_spec(slots.shape), whole_spec(gates.shape)] + [anywhere] * (2 * groups + 3 * nz),
        outs,
        [anywhere] * len(outs),
        [
            pltpu.VMEM((blocks, length, width), BF),
            pltpu.VMEM((blocks, high, width), BF),
            pltpu.VMEM((nz,) + matrices, BF),
            pltpu.VMEM((experts, rows, width), BF),
            pltpu.VMEM((experts, rows, width), BF),
            pltpu.VMEM((experts, rows, LANES), F32),
            pltpu.VMEM((experts, rows, LANES), F32),
            pltpu.VMEM((3, rows, part[-1]), BF),
            pltpu.VMEM((experts, nz) + matrices[1:], BF),
            pltpu.SemaphoreType.DMA((groups,)),
            pltpu.SemaphoreType.DMA((groups,)),
            pltpu.SemaphoreType.DMA((nz, 3)),
            pltpu.SemaphoreType.DMA((groups,)),
            pltpu.SemaphoreType.DMA((groups,)),
            pltpu.SemaphoreType.DMA((experts, nz)),
        ],
    )
    return got[:groups], got[groups : groups + 2], got[groups + 2 :]


def keys_grad_kernel(nr, nh, ids, rows_ref, gain_ref, own_ref, other_ref, *rest):
    grads, (normed_ref, acc_ref) = rest[:nh], rest[nh:]
    chunk, kn = rows_ref.shape[-1] // nr, KVH * HD // nh
    step, last = pl.program_id(0), pl.num_programs(0) - 1
    normed_ref[...] = (rows_ref[0].astype(F32) * gain_ref[...]).astype(BF)

    @pl.when(step == 0)
    def _():
        acc_ref[...] = jnp.zeros_like(acc_ref)

    def add(dkv_ref):
        for r in range(nr):
            x = normed_ref[:, span(row_chunk(ids, r, nr), chunk)]
            for h in range(nh):
                here = span(half_chunk(ids, h, nh), kn)
                acc_ref[r * nh + h, :, :kn] += dot_tn(x, dkv_ref[0, :, here])
                acc_ref[r * nh + h, :, kn:] += dot_tn(x, dkv_ref[1, :, here])

    half = pl.num_programs(0) // 2
    pl.when(step < half)(lambda: add(own_ref))
    pl.when(step >= half)(lambda: add(other_ref))

    @pl.when(step == last)
    def _():
        for n in range(nr * nh):
            grads[n % nh][n // nh] = acc_ref[n].astype(BF)


def keys_grads(ids, rows, gain, dkv, nr, nh):
    slots, length, width = rows.shape
    cols, half = 2 * KVH * HD // nh, slots // 2
    outs = [jax.ShapeDtypeStruct((nr, width // nr, cols), BF)] * nh
    return call(
        functools.partial(keys_grad_kernel, nr, nh),
        (slots,),
        ids,
        [rows, gain, *dkv],
        [
            pl.BlockSpec((1, length, width), lambda i, _: (i, 0, 0)),
            whole_spec(gain.shape),
            pl.BlockSpec((2, length, KVH * HD), lambda i, _: (0, jnp.minimum(i, half - 1), 0)),
            pl.BlockSpec((2, length, KVH * HD), lambda i, _: (0, jnp.maximum(i - half, 0), 0)),
        ],
        outs,
        [whole_spec(o.shape) for o in outs],
        [pltpu.VMEM((length, width), BF), pltpu.VMEM((nr * nh, width // nr, cols), F32)],
    )


def queries_grad_kernel(nr, nh, ids, rows_ref, gain_ref, dq_ref, *rest):
    grads, normed_ref = rest[:nh], rest[nh]
    chunk, qn = rows_ref.shape[-1] // nr, H * HD // nh
    normed_ref[...] = (rows_ref[...].astype(F32) * gain_ref[...]).astype(BF)
    for r in range(nr):
        x = normed_ref[:, span(row_chunk(ids, r, nr), chunk)]
        for h in range(nh):
            grads[h][r] = dot_tn(x, dq_ref[:, span(half_chunk(ids, h, nh), qn)]).astype(BF)


def queries_grads(ids, rows, gain, dq, nr, nh):
    ins = [rows, gain, dq]
    outs = [jax.ShapeDtypeStruct((nr, rows.shape[1] // nr, H * HD // nh), BF)] * nh
    return call(
        functools.partial(queries_grad_kernel, nr, nh),
        (1,),
        ids,
        ins,
        [whole_spec(i.shape) for i in ins],
        outs,
        [whole_spec(o.shape) for o in outs],
        [pltpu.VMEM(rows.shape, BF)],
    )


def rows_back_kernel(nr, nh, ids, dq_ref, dkv_ref, x_ref, dx2_ref, gain_ref, *rest):
    weights = rest[:nh]
    out_ref, grad_ref, low_ref = rest[nh:]
    width = x_ref.shape[1]
    chunk = width // nr
    qn, kn = H * HD // nh, KVH * HD // nh
    at_q, at_k, at_v, at_end = columns(nh, width)
    low_ref[...] = dkv_ref[...].astype(BF)
    for r in range(nr):
        total = None
        for h in range(nh):
            at = half_chunk(ids, h, nh)
            weight = weights[h]
            part = dot_nt(dq_ref[:, span(at, qn)], weight[r, :, at_q:at_k])
            part = part + dot_nt(low_ref[0, :, span(at, kn)], weight[r, :, at_k:at_v])
            part = part + dot_nt(low_ref[1, :, span(at, kn)], weight[r, :, at_v:at_end])
            total = part if total is None else total + part
        grad_ref[:, span(row_chunk(ids, r, nr), chunk)] = total
    x = x_ref[...]
    scaled = grad_ref[...] * gain_ref[...]
    inverse = lax.rsqrt(jnp.mean(x * x, axis=1, keepdims=True) + EPSILON)
    inner = jnp.mean(scaled * x, axis=1, keepdims=True)
    out_ref[...] = dx2_ref[...] + inverse * scaled - x * (inverse * inverse * inverse * inner)


def rows_back(ids, dq, dkv, x, dx2, gain, weights):
    nr, nh = weights[0].shape[0], len(weights)
    ins = [dq, dkv, x, dx2, gain, *weights]
    return call(
        functools.partial(rows_back_kernel, nr, nh),
        (1,),
        ids,
        ins,
        [whole_spec(i.shape) for i in ins],
        jax.ShapeDtypeStruct(x.shape, F32),
        whole_spec(x.shape),
        [pltpu.VMEM(x.shape, F32), pltpu.VMEM(dkv.shape, BF)],
    )


def swap(value, axis, distance):
    count = lax.axis_size(axis)
    return lax.ppermute(value, axis, [(i, i ^ distance) for i in range(count)])


def after(value, *done):
    return lax.optimization_barrier((value,) + done)[0]


def pick(array, index):
    return lax.dynamic_index_in_dim(array, index, 0, keepdims=False)


def gather_z(value):
    chips = lax.axis_size("shard") // 2
    if chips != 4:
        return [value] + [swap(value, "shard", 2 * r) for r in range(1, chips)]
    near, far = swap(value, "shard", 2), swap(value, "shard", 4)
    return [value, near, far, swap(far, "shard", 2)]


def scatter_z(parts):
    total = parts[0].astype(F32)
    for r in range(1, len(parts)):
        total = total + swap(parts[r], "shard", 2 * r).astype(F32)
    return total


def in_order(mine, other, core, axis):
    return jnp.where(
        core == 0,
        jnp.concatenate([mine, other], axis=axis),
        jnp.concatenate([other, mine], axis=axis),
    )


def add_low(*values):
    total = values[0].astype(F32)
    for value in values[1:]:
        total = total + value.astype(F32)
    return total.astype(BF)


def scatter_rows(total, z, core):
    chips = lax.axis_size("shard") // 2
    parts = total.reshape(chips, total.shape[0] // chips, total.shape[1])
    parts = [pick(parts, z ^ r) for r in range(chips)]
    step, near = swap(parts[3], "shard", 2), swap(parts[1], "shard", 2)
    far = add_low(parts[2], step)
    rows = parts[0].astype(F32) + near.astype(F32) + swap(far, "shard", 4).astype(F32)
    rows = rows.reshape(2, rows.shape[0] // 2, rows.shape[1])
    mine = pick(rows, core)
    other = swap(pick(rows, 1 - core).astype(BF), "shard", 1).astype(F32)
    return (jnp.where(core == 0, mine, other), jnp.where(core == 0, other, mine)), far


def body(
    tokens,
    block_ids,
    routes,
    gates,
    attn_gain,
    w_query,
    w_key,
    w_value,
    w_out,
    moe_gain,
    w_gate,
    w_up,
    w_down,
    cotangent,
):
    length, width = tokens.shape[1], tokens.shape[2]
    n_expert, n_shard = lax.axis_size("expert"), lax.axis_size("shard")
    chips = n_shard // 2
    local = w_gate.shape[0]
    fast = n_expert == 4 and n_shard == 8 and local % 4 == 0
    sides = 2 if fast else 1
    experts = local // (2 * sides)
    e, s = lax.axis_index("expert"), lax.axis_index("shard")
    z, core = s // 2, s % 2
    side = z // 2 if fast else 0
    first_expert = e * local + core * (local // 2) + side * experts
    ids = jnp.stack([e, z, core, first_expert]).astype(jnp.int32)
    nh = 2 if fast else 1

    x = tokens[0]
    c = cotangent[0]

    inverse_one = lax.rsqrt(jnp.mean(x * x, axis=-1, keepdims=True) + EPSILON)
    scaled_rows = (x * inverse_one).astype(BF)

    def halves(matrix):
        low = matrix.astype(BF)
        return low.reshape(low.shape[0], nh, low.shape[1] // nh).transpose(1, 0, 2)

    def column(gain):
        return jnp.broadcast_to(gain.astype(BF)[None, :, None], (nh, gain.shape[0], LANES // 2))

    packed = jnp.concatenate(
        [halves(w_out), halves(w_query), halves(w_key), halves(w_value), column(attn_gain), column(moe_gain)],
        axis=2,
    )
    at_q, at_k, at_v, at_end = columns(nh, width)

    numbers = jnp.arange(EXPERTS, dtype=jnp.int32)
    lines = EXPERTS * length // width

    def named_experts(routed):
        return routed[0][None, :, :] == numbers[:, None, None]

    def cotangent_rows(start):
        value, routed, gated = after((c, routes, gates), start)
        dense = jnp.sum(jnp.where(named_experts(routed), gated[0][None, :, :], 0.0), axis=-1)
        dense = dense.reshape(lines, width)
        high = dense.astype(BF)
        low = (dense - high.astype(F32)).astype(BF)
        return jnp.concatenate([value.astype(BF), high, low], axis=0)

    def own_experts(start):
        low = jnp.stack([m.astype(BF) for m in after((w_gate, w_up, w_down), start)], axis=1)
        low = low.reshape((2, local // 2) + low.shape[1:])
        return in_order(pick(low, core), swap(pick(low, 1 - core), "shard", 1), core, 2)

    def over_columns(value):
        return [swap(value, "expert", r) for r in range(1, n_expert)]

    if fast:
        mine, other = pick(packed, core), pick(packed, 1 - core)
        chip = in_order(mine, swap(other, "shard", 1), core, 0)

    s_late = after(s, chip) if fast else s
    owners = jnp.stack([s_late ^ (2 * r + k) for k in range(2) for r in range(chips)])
    places = (owners[:, None] * length + jnp.arange(length)[None, :]).reshape(n_shard * length)
    freqs = 10000.0 ** (-(jnp.arange(HD // 2, dtype=F32) * 2.0 / HD))
    angles = places.astype(F32)[:, None] * freqs[None, :]
    cosine, sine = jnp.cos(angles), jnp.sin(angles)
    cosine = jnp.concatenate([cosine] * 4, axis=1)
    sine = jnp.concatenate([-sine, sine] * 2, axis=1)
    every = block_ids[0].reshape(n_shard, length)
    key_blocks = jnp.concatenate(
        [pick(every, s_late ^ (2 * r + k)) for k in range(2) for r in range(chips)]
    )
    own_blocks = pick(every, s_late)
    lanes = jnp.arange(LANES, dtype=jnp.int32)[None, :]
    key_extra = ((lanes == key_blocks[:, None]) | ((lanes >= 16) & (lanes < 19))).astype(BF)
    query_extra = jnp.where((lanes < 16) & (lanes > own_blocks[:, None]), -1e30, 0.0).astype(BF)

    if fast:
        w_near, w_far = swap(chip, "shard", 2), swap(chip, "shard", 4)
        x_near = swap(scaled_rows, "shard", 2)
        x_far = swap(after(scaled_rows, w_far), "shard", 4)
        stacked = jnp.stack([chip, w_near, w_far, swap(w_far, "shard", 2)])
        block = jnp.concatenate([pick(stacked, z ^ i) for i in range(chips)], axis=0)
        c_pack = cotangent_rows(chip)
        chip_w = own_experts(chip).reshape((2, experts, 3, 2 * w_gate.shape[1], w_gate.shape[2]))
        here = [pick(chip_w, side)[:, k] for k in range(3)]
        there = [pick(chip_w, 1 - side)[:, k] for k in range(3)]
        w_got = over_columns(after(block, x_near, *here, *there))
        x_cross = swap(x_far, "shard", 2)
        c_far = swap(after(c_pack, x_far), "shard", 4)
        own_core = jnp.stack([scaled_rows, x_near, x_far, x_cross])
        x_other = swap(own_core, "shard", 1)
        rows = jnp.concatenate([own_core, x_other], axis=0)
        w_got = [after(got, own_core, c_far, cosine, sine, key_extra, query_extra) for got in w_got]
        blocks = jnp.stack([block] + w_got)
        attn_w = [blocks, swap(blocks, "shard", 1)]
        gain_cols = blocks[:, :, at_end:]
        gain_cols = jnp.concatenate([pick(gain_cols, e ^ i) for i in range(n_expert)], axis=0)
        near_a = swap(after(here[0], blocks), "shard", 2)
        far_a = swap(after(there[0], blocks), "shard", 4)
        c_own_got = over_columns(after(c_pack, attn_w[1]))
    else:
        c_pack = cotangent_rows(packed)
        own_core = jnp.stack(gather_z(scaled_rows))
        rows = jnp.concatenate([own_core, swap(own_core, "shard", 1)], axis=0)
        blocks = lax.all_gather(packed[0], ("expert", "shard"), axis=0, tiled=True)
        attn_w = [blocks[None]]
        gain_cols = blocks[:, at_end:]
        expert_w = gather_z(own_experts(packed))
    gain_one = gain_cols[:, 0].astype(F32)[None]
    gain_two = gain_cols[:, LANES // 2].astype(F32)[None]
    nr = attn_w[0].shape[0]

    q, k, v = project(ids, rows, gain_one, cosine, sine, attn_w)
    if fast:
        c_far_got = over_columns(after(c_far, q))
        near_b = swap(after(jnp.stack(here[1:], axis=1), near_a, q), "shard", 2)
        far_b = swap(after(there[1], far_a, q), "shard", 4)
        c_own = jnp.stack([c_pack] + c_own_got)
        q = after(q, near_a, far_a, c_own)
    mixed, mixed_low, lse = attend(ids, q, k, v, key_extra, query_extra)
    x2, n2 = project_out(ids, x, mixed_low, gain_two, attn_w)

    def places_of(groups):
        tails = jnp.concatenate([group[:, length:] for group in groups], axis=0).astype(F32)
        dense = (tails[:, :lines] + tails[:, lines:]).reshape(-1, EXPERTS, length)
        gate_here = lax.dynamic_slice_in_dim(dense, first_expert, experts, 1)
        chosen = gate_here > 0.0
        before = jnp.triu(jnp.ones((length, length), BF), 1)
        ranks = jnp.einsum("net,tu->neu", chosen.astype(BF), before, preferred_element_type=F32)
        return gate_here, jnp.where(chosen, ranks, -1.0)

    if fast:
        n2 = after(n2, near_b, far_b, *c_far_got)
        n2_far = swap(n2, "shard", 4)
        n2_own_got = over_columns(n2)
        cross_b = swap(after(jnp.stack([far_a, far_b], axis=1), n2), "shard", 2)
        n2_far_got = over_columns(after(n2_far, *n2_own_got))
        c_across = jnp.stack([after(piece, *n2_own_got) for piece in [c_far, *c_far_got]])
        c_own_other = swap(after(c_own, n2_far), "shard", 1)
        far_c = swap(after(there[2], n2_far), "shard", 4)
        cross_c = swap(far_c, "shard", 2)
        n2_own = jnp.stack([n2] + n2_own_got)
        n2_own_other = swap(n2_own, "shard", 1)
        n2_far_got = [after(got, far_c, cross_b, n2_own, c_own_other, c_across) for got in n2_far_got]
        n2_across = jnp.stack([n2_far] + n2_far_got)
        c_groups = [c_own, c_across, c_own_other, swap(after(c_across, n2_across), "shard", 1)]
        gate_here, slots = places_of(c_groups)
        n2_groups = [n2_own, n2_across, n2_own_other, swap(n2_across, "shard", 1)]
        expert_w = [here, [near_a, near_b[:, 0], near_b[:, 1]], [far_a, far_b, far_c], [cross_b[:, 0], cross_b[:, 1], cross_c]]
        dn2_parts, y_parts, d_experts = mixture(
            ids, slots, gate_here, n2_groups, c_groups, expert_w
        )
        step = swap(d_experts[3], "shard", 2)
        dn2_other = [swap(dn2_parts[3], "shard", 1), swap(dn2_parts[2], "shard", 1)][::-1]
        far_sums = add_low(dn2_parts[1], dn2_other[1])
        own_sums = add_low(dn2_parts[0], dn2_other[0])
        far_got = [swap(far_sums[r], "expert", r) for r in range(1, n_expert)]
        dn2_far = add_low(far_sums[0], *[after(got, own_sums, step) for got in far_got])
        dn2_got = swap(dn2_far, "shard", 4)
        own_got = [swap(after(own_sums[r], dn2_far), "expert", r) for r in range(1, n_expert)]
        d_far = add_low(d_experts[2], after(step, dn2_far))
        y_sum = add_low(y_parts[0], swap(after(y_parts[1], dn2_far), "shard", 1))
        y_sum = y_sum.reshape((2, n_expert) + y_sum.shape[1:])
        own_got = [after(got, d_far, y_sum) for got in own_got]
        dn2 = sum([g.astype(F32) for g in own_got + [dn2_got]], own_sums[0].astype(F32))
    else:
        c_own = jnp.stack([c_pack] + over_columns(c_pack))
        c_groups = [c_own, swap(c_own, "shard", 1)]
        gate_here, slots = places_of(c_groups)
        n2_own = jnp.stack([n2] + over_columns(n2))
        n2_groups = [n2_own, swap(n2_own, "shard", 1)]
        c_rows, gate_rows = gather_rows(ids, slots, c_groups, gate_here)
        (x_rows,) = gather_rows(ids, slots, n2_groups)
        flat = (experts, slots.shape[0] * CAP)
        y_rows, dx_rows, grad_rows, d_experts = run_experts(
            ids,
            x_rows.reshape(flat + (width,)),
            c_rows.reshape(flat + (width,)),
            gate_rows.reshape(flat + (LANES,)),
            expert_w,
        )
        split = (experts, slots.shape[0], CAP)
        dn2_parts = spread_rows(ids, slots, dx_rows.reshape(split + (width,)), 2)
        y_parts = spread_rows(
            ids, slots, y_rows.reshape(split + (width,)), 2, grad_rows.reshape(split + (LANES,))
        )
        own_sums = add_low(dn2_parts[0], swap(dn2_parts[1], "shard", 1))
        own_got = [swap(own_sums[r], "expert", r) for r in range(1, n_expert)]
        dn2 = sum([g.astype(F32) for g in own_got], own_sums[0].astype(F32))
        y_sum = add_low(y_parts[0], swap(y_parts[1], "shard", 1))[None]

    dx2, d_mixed, d_out_w = project_out_back(ids, c, x2, gain_two, dn2, mixed_low, attn_w)
    args = (mixed, lse, k, v, key_extra, query_extra, cosine, sine)
    if fast:
        far_a = swap(after(d_far[:, :2], dn2_got), "shard", 4)
        near_a = swap(after(d_experts[1][:, :1], dn2_got), "shard", 2)
        y_across_got = [swap(after(y_sum[1, r], dn2), "expert", r) for r in range(1, n_expert)]
        done = attend_back(ids, q, d_mixed, *args, 0, PAIRS // 2, None)
        y_across = add_low(y_sum[1, 0], *[after(got, done[0]) for got in y_across_got])
        far_b = swap(after(d_far[:, 2:], far_a, done[0]), "shard", 4)
        near_b = swap(after(d_experts[1][:, 1:], near_a, done[0]), "shard", 2)
        y_got = [swap(after(y_sum[0, r], y_across), "expert", r) for r in range(1, n_expert)]
        d_mixed = after(d_mixed, far_a, near_a, y_across)
        dq, *dkv = attend_back(ids, q, d_mixed, *args, PAIRS // 2, PAIRS // 2, done)
        y_got = [after(got, dq) for got in y_got]
        dkv[1] = after(dkv[1], far_b, near_b, *y_got)
        d_out_sums = add_low(d_out_w[0], swap(after(d_out_w[1], dkv[1]), "shard", 1))
        d_out_got = [swap(d_out_sums[r], "expert", r) for r in range(1, n_expert)]
    else:
        dq, *dkv = attend_back(ids, q, d_mixed, *args, 0, PAIRS, None)
        y_got = [swap(y_sum[0, r], "expert", r) for r in range(1, n_expert)]
    dkv_core = swap(dkv[1], "shard", 1)
    dkv_sums = add_low(dkv[0], dkv_core)
    dkv_parts = [dkv_sums[:, r * length : (r + 1) * length] for r in range(chips)]
    if fast:
        dkv_step, dkv_near = swap(dkv_parts[3], "shard", 2), swap(dkv_parts[1], "shard", 2)
        d_keys = keys_grads(ids, after(rows, dkv_sums, d_out_sums), gain_one, dkv, nr, nh)
        dq = after(dq, dkv_step, dkv_near, *d_out_got, *d_keys)
        d_queries = queries_grads(ids, scaled_rows, gain_one, dq, nr, nh)
        dkv_far = swap(after(add_low(dkv_parts[2], dkv_step), d_queries[0]), "shard", 4)
        y_far = swap(after(y_across, d_queries[0]), "shard", 4)
        d_halves = [swap(d_queries[1], "shard", 1), swap(d_keys[1], "shard", 1)]
        sums = jnp.concatenate(
            [add_low(d_queries[0], d_halves[0]), add_low(d_keys[0], d_halves[1])], axis=2
        )
        got = [swap(sums[r], "expert", r) for r in range(1, n_expert)]
        d_total = add_low(sums[0], *got)
        d_out_total = add_low(d_out_sums[0], *[after(g, sums) for g in d_out_got])
        dkv_own = sum([g.astype(F32) for g in (dkv_near, dkv_far)], dkv_parts[0].astype(F32))
        out_sum = sum([after(g, d_total).astype(F32) for g in y_got + [y_far]], y_sum[0, 0].astype(F32))
        parts, far_part = scatter_rows(jnp.concatenate([d_out_total, d_total], axis=1), z, core)
        dkv_own = after(dkv_own, far_part)
    else:
        out_sum = sum([g.astype(F32) for g in y_got], y_sum[0, 0].astype(F32))
        d_queries = queries_grads(ids, scaled_rows, gain_one, dq, nr, nh)
        d_keys = keys_grads(ids, rows, gain_one, dkv, nr, nh)
        dkv_own = scatter_z(dkv_parts)
        joined = jnp.concatenate([d_out_w[0][0], d_queries[0][0], d_keys[0][0]], axis=1)
        joined = lax.psum_scatter(joined, ("expert", "shard"), scatter_dimension=0, tiled=True)
        parts = [joined.astype(F32)]
    token_grad = rows_back(ids, dq, dkv_own, x, dx2, gain_one, attn_w)

    on, qn, kn = width // nh, H * HD // nh, KVH * HD // nh
    start = on + LANES
    d_out_full = jnp.concatenate([p[:, :on] for p in parts], axis=1)
    d_gain_two = parts[0][:, on]
    d_query_w = jnp.concatenate([p[:, start : start + qn] for p in parts], axis=1)
    d_key_w = jnp.concatenate([p[:, start + qn : start + qn + kn] for p in parts], axis=1)
    d_value_w = jnp.concatenate([p[:, start + qn + kn :] for p in parts], axis=1)
    row_sums = (
        jnp.sum(w_query.astype(BF).astype(F32) * d_query_w, axis=1)
        + jnp.sum(w_key.astype(BF).astype(F32) * d_key_w, axis=1)
        + jnp.sum(w_value.astype(BF).astype(F32) * d_value_w, axis=1)
    )
    d_gain_one = row_sums / attn_gain.astype(BF).astype(F32)

    output = x2 + out_sum[:length]
    gate_sums = out_sum[length : length + lines].reshape(EXPERTS, length)
    gate_grad = jnp.sum(jnp.where(named_experts(routes), gate_sums[:, :, None], 0.0), axis=0)

    if fast:
        there_sum = jnp.concatenate([far_a, far_b], axis=1).astype(F32)
        here_sum = d_experts[0].astype(F32)
        here_sum = here_sum + jnp.concatenate([near_a, near_b], axis=1).astype(F32)
        d_chip = jnp.where(
            side == 0,
            jnp.concatenate([here_sum, there_sum], axis=0),
            jnp.concatenate([there_sum, here_sum], axis=0),
        )
    else:
        d_chip = scatter_z(d_experts)
    half = d_chip.shape[2] // 2
    d_chip = d_chip.astype(BF)
    if fast:
        d_chip = after(d_chip, d_total)
    mine = lax.dynamic_slice_in_dim(d_chip, core * half, half, 2)
    other = swap(lax.dynamic_slice_in_dim(d_chip, (1 - core) * half, half, 2), "shard", 1)
    if fast:
        other = after(other, dkv_own)
    d_expert = in_order(mine, other, core, 0).astype(F32)

    return (
        output[None],
        token_grad[None],
        gate_grad[None],
        d_gain_one,
        d_query_w,
        d_key_w,
        d_value_w,
        d_out_full,
        d_gain_two,
        d_expert[:, 0],
        d_expert[:, 1],
        d_expert[:, 2],
    )


def solution(mesh):
    rows = P("expert", "shard", None)
    split = P(("expert", "shard"), None)
    gain = P(("expert", "shard"))
    in_specs = (
        rows, P("expert", None), rows, rows, gain, split, split, split, split, gain, rows, rows, rows, rows,
    )
    out_specs = (rows, rows, rows, gain, split, split, split, split, gain, rows, rows, rows)
    return jax.shard_map(body, mesh=mesh, in_specs=in_specs, out_specs=out_specs, check_vma=False)
```

time: 763 us -> 599 us (0.79)
  waiting for transfers between devices: 368 us -> 228 us
  Pallas kernels: 206 us -> 169 us
  local copies, waits for them, and re-layouts: 24.7 us -> 40.8 us
    ppermute x105 -> x78, waiting for transfers between devices: 368 us -> 228 us  [swap(): return lax.ppermute(value, axis, [(i, i ^ distance) for i in range(count)])]
    pallas_call x12 -> x10, Pallas kernels: 206 us -> 169 us  [call(): pl.pallas_call(kernel, grid_spec=pltpu.PrefetchScalarGridSpec(num_scalar_...]
    squeeze x1 -> x8, local copies, waits for them, and re-layouts: 0.07 us -> 8.42 us  [the longest x1 1.69 us: body(): y_sum[0, r]]
    ppermute x105 -> x78, starting transfers between devices: 83.2 us -> 77.2 us  [swap(): return lax.ppermute(value, axis, [(i, i ^ distance) for i in range(count)])]
    convert_element_type x25 -> x22, other arithmetic: 22.8 us -> 17.6 us  [the longest x14 14.3 us: add_low(): return total.astype(BF)]
    unnamed x172 -> x166, local copies, waits for them, and re-layouts: 14 us -> 16.2 us
  transfers between devices with their start and end apart: 105 -> 78, of which waited for: 44 -> 32; matrix products, arithmetic and copies ran while one was open for 11% -> 15% of each run, Pallas kernels for 21% -> 20%
where the time goes in v2:
time: 599 us; the launch traced here: 589 us
  waiting for transfers between devices  228 us (38%)
  Pallas kernels  169 us (28%)
  starting transfers between devices  77.2 us (13%)
  other arithmetic  70.9 us (12%)
  local copies, waits for them, and re-layouts  40.8 us (7%)
    ppermute x78, waiting for transfers between devices, swap(): return lax.ppermute(value, axis, [(i, i ^ distance) for i in range(count)])  228 us
    pallas_call x10, Pallas kernels, call(): pl.pallas_call(kernel, grid_spec=pltpu.PrefetchScalarGridSpec(num_scalar_...  169 us
    ppermute x78, starting transfers between devices, swap(): return lax.ppermute(value, axis, [(i, i ^ distance) for i in range(count)])  77.2 us
    unnamed x166, local copies, waits for them, and re-layouts  16.2 us
    convert_element_type x14, other arithmetic, add_low(): return total.astype(BF)  14.3 us
  transfers between devices with their start and end apart: 78, of which 32 were waited for; matrix products, arithmetic and copies ran while one was open for 15% of the time, Pallas kernels for 20%

profile of v2, /device:TPU:0, one launch (start us, length us, event | category | flops | bytes accessed | tf_op | source)
XLA Modules:
  0.0 588.8 jit_solution(14615424732363772294)
XLA Ops:
  22.4 5.3 fusion.33
  35.7 7.4 %collective-permute-done.7 = bf16[64,1664]{1,0:T(8,128)(2,1)S(1)} collective-permute-done((bf16[64,1664]{1,0:T(8,128)(2,1)}, bf16[64,1664]{1,0:T(8,128)(2,1)S(1)}, u32[]{:S(2)}, u32[]{:S(2)}) %collective-permute-start.7) | collective-permute-done | bytes 213024 | tf_op jit(solution)/shard_map/ppermute | solution.py:901
  54.8 6.9 %collective-permute-done.3 = bf16[256,1024]{1,0:T(8,128)(2,1)S(1)} collective-permute-done((bf16[256,1024]{1,0:T(8,128)(2,1)}, bf16[256,1024]{1,0:T(8,128)(2,1)S(1)}, u32[]{:S(2)}, u32[]{:S(2)}) %collective-permute-start.3) | collective-permute-done | bytes 524320 | tf_op jit(solution)/shard_map/ppermute | solution.py:901
  64.4 19.4 %collective-permute-done.4 = bf16[256,1024]{1,0:T(8,128)(2,1)S(1)} collective-permute-done((bf16[256,1024]{1,0:T(8,128)(2,1)S(1)}, bf16[256,1024]{1,0:T(8,128)(2,1)S(1)}, u32[]{:S(2)}, u32[]{:S(2)}) %collective-permute-start.4) | collective-permute-done | bytes 524320 | tf_op jit(solution)/shard_map/ppermute | solution.py:901
  111.3 15.3 %shard_map.229 = (bf16[256,1024]{1,0:T(8,128)(2,1)}, bf16[2048,512]{1,0:T(8,128)(2,1)}, bf16[2048,512]{1,0:T(8,128)(2,1)}) custom-call(s32[4]{0:T(128)} %pad_add_fusion.ids.refs_0_, bf16[8,256,1024]{2,1,0:T(8,128)(2,1)} %copy-done.3, f32[1,1024]{1,0:T(1,128)} %bitcast.285, f32[2048,128]{1,0:T(8,128)} %pad_maximum_fusion.8.cos_ref.refs_9_, ...), custom_call_target="tpu_custom_call" | custom-call | tf_op jit(solution)/shard_map/pallas_call | solution.py:39
  136.7 16.8 %shard_map.230 = (f32[256,1024]{1,0:T(8,128)}, bf16[256,1024]{1,0:T(8,128)(2,1)}, f32[4,256,128]{2,1,0:T(8,128)}) custom-call(s32[4]{0:T(128)} %pad_add_fusion.ids.refs_0_, bf16[256,1024]{1,0:T(8,128)(2,1)} %get-tuple-element.138.q_ref.refs_1_, bf16[2048,512]{1,0:T(8,128)(2,1)} %get-tuple-element.139.k_ref.refs_5_, ...), custom_call_target="tpu_custom_call" | custom-call | tf_op jit(solution)/shard_map/pallas_call | solution.py:39
  163.1 22.4 %collective-permute-done.27 = bf16[256,1024]{1,0:T(8,128)(2,1)S(1)} collective-permute-done((bf16[256,1024]{1,0:T(8,128)(2,1)}, bf16[256,1024]{1,0:T(8,128)(2,1)S(1)}, u32[]{:S(2)}, u32[]{:S(2)}) %collective-permute-start.27) | collective-permute-done | bytes 524320 | tf_op jit(solution)/shard_map/ppermute | solution.py:901
  190.2 12.2 %collective-permute-done.26 = bf16[256,1024]{1,0:T(8,128)(2,1)S(1)} collective-permute-done((bf16[256,1024]{1,0:T(8,128)(2,1)S(1)}, bf16[256,1024]{1,0:T(8,128)(2,1)S(1)}, u32[]{:S(2)}, u32[]{:S(2)}) %collective-permute-start.26) | collective-permute-done | bytes 524320 | tf_op jit(solution)/shard_map/ppermute | solution.py:901
  204.4 8.8 %collective-permute-done.25 = bf16[256,1024]{1,0:T(8,128)(2,1)S(1)} collective-permute-done((bf16[256,1024]{1,0:T(8,128)(2,1)S(1)}, bf16[256,1024]{1,0:T(8,128)(2,1)S(1)}, u32[]{:S(2)}, u32[]{:S(2)}) %collective-permute-start.25) | collective-permute-done | bytes 524320 | tf_op jit(solution)/shard_map/ppermute | solution.py:901
  229.2 10.1 %collective-permute-done.32 = bf16[256,1024]{1,0:T(8,128)(2,1)S(1)} collective-permute-done((bf16[256,1024]{1,0:T(8,128)(2,1)S(1)}, bf16[256,1024]{1,0:T(8,128)(2,1)S(1)}, u32[]{:S(2)}, u32[]{:S(2)}) %collective-permute-start.32) | collective-permute-done | bytes 524320 | tf_op jit(solution)/shard_map/ppermute | solution.py:901
  249.0 9.9 %collective-permute-done.37.rest_19_ = bf16[2,256,512]{2,1,0:T(8,128)(2,1)S(1)} collective-permute-done((bf16[2,256,512]{2,1,0:T(8,128)(2,1)S(1)}, bf16[2,256,512]{2,1,0:T(8,128)(2,1)S(1)}, u32[]{:S(2)}, u32[]{:S(2)}) %collective-permute-start.37) | collective-permute-done | bytes 524320 | tf_op jit(solution)/shard_map/ppermute | solution.py:901
  259.7 52.7 %shard_map.232 = (bf16[4,256,1024]{2,1,0:T(8,128)(2,1)}, bf16[4,256,1024]{2,1,0:T(8,128)(2,1)}, bf16[4,256,1024]{2,1,0:T(8,128)(2,1)}, bf16[4,256,1024]{2,1,0:T(...) custom-call(s32[4]{0:T(128)} %pad_add_fusion.ids.refs_0_, ...), custom_call_target="tpu_custom_call" | custom-call | tf_op jit(solution)/shard_map/pallas_call | solution.py:39
  324.2 25.3 %collective-permute-done.41 = bf16[2,3,256,512]{3,2,1,0:T(8,128)(2,1)S(1)} collective-permute-done((bf16[2,3,256,512]{3,2,1,0:T(8,128)(2,1)}, bf16[2,3,256,512]{3,2,1,0:T(8,128)(2,1)S(1)}, u32[]{:S(2)}, u32[]{:S(2)}) %collective-permute-start.41) | collective-permute-done | bytes 1572896 | tf_op jit(solution)/shard_map/ppermute | solution.py:901
  357.7 19.7 %collective-permute-done.48 = bf16[256,1024]{1,0:T(8,128)(2,1)S(1)} collective-permute-done((bf16[256,1024]{1,0:T(8,128)(2,1)S(1)}, bf16[256,1024]{1,0:T(8,128)(2,1)S(1)}, u32[]{:S(2)}, u32[]{:S(2)}) %collective-permute-start.48) | collective-permute-done | bytes 524320 | tf_op jit(solution)/shard_map/ppermute | solution.py:901
  392.0 7.0 %shard_map.233 = (f32[256,1024]{1,0:T(8,128)}, bf16[256,1024]{1,0:T(8,128)(2,1)}, bf16[4,256,640]{2,1,0:T(8,128)(2,1)}, bf16[4,256,640]{2,1,0:T(8,128)(2,1)}) custom-call(s32[4]{0:T(128)} %pad_add_fusion.ids.refs_0_, f32[256,1024]{1,0:T(8,128)} %bitcast.246, f32[256,1024]{1,0:T(8,128)} %get-tuple-element.142.x2_ref, f32[1,1024]{1,0:T(1,128)} %bitcast.290, ...), custom_call_target="tpu_custom_call" | custom-call | tf_op jit(solution)/shard_map/pallas_call | solution.py:39
  399.0 24.4 %shard_map.234 = (bf16[256,1024]{1,0:T(8,128)(2,1)}, bf16[2,1024,512]{2,1,0:T(8,128)(2,1)}, bf16[2,1024,512]{2,1,0:T(8,128)(2,1)}) custom-call(s32[4]{0:T(128)} %pad_add_fusion.ids.refs_0_, bf16[256,1024]{1,0:T(8,128)(2,1)} %get-tuple-element.138.q_ref.refs_1_, bf16[256,1024]{1,0:T(8,128)(2,1)} %get-tuple-element.193.do_ref.refs_2_, ...), custom_call_target="tpu_custom_call" | custom-call | tf_op jit(solution)/shard_map/pallas_call | solution.py:39
  432.7 24.3 %shard_map.235 = (bf16[256,1024]{1,0:T(8,128)(2,1)}, bf16[2,1024,512]{2,1,0:T(8,128)(2,1)}, bf16[2,1024,512]{2,1,0:T(8,128)(2,1)}) custom-call(s32[4]{0:T(128)} %pad_add_fusion.ids.refs_0_, bf16[256,1024]{1,0:T(8,128)(2,1)} %get-tuple-element.138.q_ref.refs_1_, ...), custom_call_target="tpu_custom_call", output_to_operand_aliasing={{0}: (11, {}), {1}: (12, {}), {2}: (13, {})} | custom-call | tf_op jit(solution)/shard_map/pallas_call | solution.py:39
  460.0 5.2 collective-permute-done.62
  475.0 12.3 %shard_map.236 = (bf16[4,256,512]{2,1,0:T(8,128)(2,1)}, bf16[4,256,512]{2,1,0:T(8,128)(2,1)}) custom-call(s32[4]{0:T(128)} %pad_add_fusion.ids.refs_0_, bf16[8,256,1024]{2,1,0:T(8,128)(2,1)} %copy-done.3, f32[1,1024]{1,0:T(1,128)} %bitcast.286, bf16[2,1024,512]{2,1,0:T(8,128)(2,1)} %get-tuple-element.198.own_ref, ...), custom_call_target="tpu_custom_call" | custom-call | tf_op jit(solution)/shard_map/pallas_call | solution.py:39
  488.7 5.2 collective-permute-done.60
  510.4 29.5 %collective-permute-done.72 = bf16[2,256,512]{2,1,0:T(8,128)(2,1)S(1)} collective-permute-done((bf16[2,256,512]{2,1,0:T(8,128)(2,1)S(1)}, bf16[2,256,512]{2,1,0:T(8,128)(2,1)S(1)}, u32[]{:S(2)}, u32[]{:S(2)}) %collective-permute-start.72) | collective-permute-done | bytes 524320 | tf_op jit(solution)/shard_map/ppermute | solution.py:901
  542.9 8.9 %collective-permute-done.71 = bf16[272,1024]{1,0:T(8,128)(2,1)S(1)} collective-permute-done((bf16[272,1024]{1,0:T(8,128)(2,1)S(1)}, bf16[272,1024]{1,0:T(8,128)(2,1)S(1)}, u32[]{:S(2)}, u32[]{:S(2)}) %collective-permute-start.71) | collective-permute-done | bytes 557088 | tf_op jit(solution)/shard_map/ppermute | solution.py:901
  566.6 5.8 collective-permute-done.75
  573.2 7.5 %shard_map.238 = f32[256,1024]{1,0:T(8,128)} custom-call(s32[4]{0:T(128)} %pad_add_fusion.ids.refs_0_, bf16[256,1024]{1,0:T(8,128)(2,1)} %get-tuple-element.213.dq_ref, f32[2,256,512]{2,1,0:T(8,128)} %convert_add_fusion.6.dkv_ref, f32[256,1024]{1,0:T(8,128)} %bitcast.236, f32[256,1024]{1,0:T(8,128)} %get-tuple-element.226.dx2_ref, f32[1,1024]{1,0:T(1,128)} %bitcast.288, ...), custom_call_target="tpu_custom_call" | custom-call | tf_op jit(solution)/shard_map/pallas_call | solution.py:39
  (441 shorter events, 223.9 us)
Async XLA Ops:
  7.5 43.7 %collective-permute-start = (bf16[256,1024]{1,0:T(8,128)(2,1)}, bf16[256,1024]{1,0:T(8,128)(2,1)}, u32[]{:S(2)}, u32[]{:S(2)}) collective-permute-start(bf16[256,1024]{1,0:T(8,128)(2,1)} %multiply_convert_fusion.rows_ref), channel_id=1, source_target_pairs={{0,2},{1,3},{2,0},{3,1},{4,6},{5,7},{6,4},{7,5},{8,10},{9,11},{10,... | collective-permute-start | bytes 1572872 | tf_op jit(solution)/shard_map/ppermute | solution.py:901
  51.3 37.2 %collective-permute-start.12 = (bf16[256,1664]{1,0:T(8,128)(2,1)S(1)}, bf16[256,1664]{1,0:T(8,128)(2,1)S(1)}, u32[]{:S(2)}, u32[]{:S(2)}) collective-permute-start(bf16[256,1664]{1,0:T(8,128)(2,1)S(1)} %get-tuple-element.125), channel_id=1, source_target_pairs={{0,24},{8,16},{16,8},{24,0},{1,25},{9,17},{17,9},{25,1},{2,26},{10... | collective-permute-start | bytes 2555912 | tf_op jit(solution)/shard_map/ppermute | solution.py:901
  53.7 37.1 %collective-permute-start.11 = (bf16[256,1664]{1,0:T(8,128)(2,1)S(1)}, bf16[256,1664]{1,0:T(8,128)(2,1)S(1)}, u32[]{:S(2)}, u32[]{:S(2)}) collective-permute-start(bf16[256,1664]{1,0:T(8,128)(2,1)S(1)} %get-tuple-element.125), channel_id=1, source_target_pairs={{0,16},{8,24},{16,0},{24,8},{1,17},{9,25},{17,1},{25,9},{2,18},{10... | collective-permute-start | bytes 2555912 | tf_op jit(solution)/shard_map/ppermute | solution.py:901
  54.2 36.7 %collective-permute-start.9 = (bf16[256,1664]{1,0:T(8,128)(2,1)S(1)}, bf16[256,1664]{1,0:T(8,128)(2,1)S(1)}, u32[]{:S(2)}, u32[]{:S(2)}) collective-permute-start(bf16[256,1664]{1,0:T(8,128)(2,1)S(1)} %get-tuple-element.125), channel_id=1, source_target_pairs={{0,8},{8,0},{16,24},{24,16},{1,9},{9,1},{17,25},{25,17},{2,10},{10... | collective-permute-start | bytes 2555912 | tf_op jit(solution)/shard_map/ppermute | solution.py:901
  126.6 35.1 %collective-permute-start.19 = (bf16[2,2,256,512]{3,2,0,1:T(8,128)(2,1)}, bf16[2,2,256,512]{3,2,0,1:T(8,128)(2,1)S(1)}, u32[]{:S(2)}, u32[]{:S(2)}) collective-permute-start(bf16[2,2,256,512]{3,2,0,1:T(8,128)(2,1)} %stack.222), channel_id=1, source_target_pairs={{0,2},{1,3},{2,0},{3,1},{4,6},{5,7},{6,4},{7,5},{8,10},{9,11},{10,... | collective-permute-start | bytes 3145736 | tf_op jit(solution)/shard_map/ppermute | solution.py:901
  126.8 32.9 %collective-permute-start.23 = (bf16[272,1024]{1,0:T(8,128)(2,1)S(1)}, bf16[272,1024]{1,0:T(8,128)(2,1)S(1)}, u32[]{:S(2)}, u32[]{:S(2)}) collective-permute-start(bf16[272,1024]{1,0:T(8,128)(2,1)S(1)} %copy-done.40), channel_id=1, source_target_pairs={{0,24},{8,16},{16,8},{24,0},{1,25},{9,17},{17,9},{25,1},{2,26},{10... | collective-permute-start | bytes 1671176 | tf_op jit(solution)/shard_map/ppermute | solution.py:901
  128.5 31.2 %collective-permute-start.22 = (bf16[272,1024]{1,0:T(8,128)(2,1)S(1)}, bf16[272,1024]{1,0:T(8,128)(2,1)S(1)}, u32[]{:S(2)}, u32[]{:S(2)}) collective-permute-start(bf16[272,1024]{1,0:T(8,128)(2,1)S(1)} %copy-done.40), channel_id=1, source_target_pairs={{0,16},{8,24},{16,0},{24,8},{1,17},{9,25},{17,1},{25,9},{2,18},{10... | collective-permute-start | bytes 1671176 | tf_op jit(solution)/shard_map/ppermute | solution.py:901
  185.4 43.7 %collective-permute-start.28 = (bf16[4,272,1024]{2,1,0:T(8,128)(2,1)S(1)}, bf16[4,272,1024]{2,1,0:T(8,128)(2,1)S(1)}, u32[]{:S(2)}, u32[]{:S(2)}) collective-permute-start(bf16[4,272,1024]{2,1,0:T(8,128)(2,1)S(1)} %pad_maximum_fusion.3.rest_4_), channel_id=1, source_target_pairs={{0,1},{1,0},{2,3},{3,2},{4,5},{5,4},{6,7},{7,6},{8,9},{9,8},{10,11... | collective-permute-start | bytes 6684680 | tf_op jit(solution)/shard_map/ppermute | solution.py:901
  186.6 32.4 %collective-permute-start.31 = (bf16[2,2,256,512]{3,2,0,1:T(8,128)(2,1)S(1)}, bf16[2,2,256,512]{3,2,0,1:T(8,128)(2,1)S(1)}, u32[]{:S(2)}, u32[]{:S(2)}) collective-permute-start(bf16[2,2,256,512]{3,2,0,1:T(8,128)(2,1)S(1)} %pad_maximum_fusion.10), channel_id=1, source_target_pairs={{0,2},{1,3},{2,0},{3,1},{4,6},{5,7},{6,4},{7,5},{8,10},{9,11},{10,... | collective-permute-start | bytes 3145736 | tf_op jit(solution)/shard_map/ppermute | solution.py:901
  313.0 36.6 %collective-permute-start.41 = (bf16[2,3,256,512]{3,2,1,0:T(8,128)(2,1)}, bf16[2,3,256,512]{3,2,1,0:T(8,128)(2,1)S(1)}, u32[]{:S(2)}, u32[]{:S(2)}) collective-permute-start(bf16[2,3,256,512]{3,2,1,0:T(8,128)(2,1)} %get-tuple-element.166), channel_id=1, source_target_pairs={{0,2},{1,3},{2,0},{3,1},{4,6},{5,7},{6,4},{7,5},{8,10},{9,11},{10,... | collective-permute-start | bytes 4718600 | tf_op jit(solution)/shard_map/ppermute | solution.py:901
  319.7 29.9 %collective-permute-start.43 = (bf16[256,1024]{1,0:T(8,128)(2,1)S(1)}, bf16[256,1024]{1,0:T(8,128)(2,1)S(1)}, u32[]{:S(2)}, u32[]{:S(2)}) collective-permute-start(bf16[256,1024]{1,0:T(8,128)(2,1)S(1)} %get-tuple-element.266), channel_id=1, source_target_pairs={{0,24},{8,16},{16,8},{24,0},{1,25},{9,17},{17,9},{25,1},{2,26},{10... | collective-permute-start | bytes 1572872 | tf_op jit(solution)/shard_map/ppermute | solution.py:901
  377.4 46.0 %collective-permute-start.54 = (bf16[2,1,256,512]{3,2,1,0:T(8,128)(2,1)}, bf16[2,1,256,512]{3,2,1,0:T(8,128)(2,1)}, u32[]{:S(2)}, u32[]{:S(2)}) collective-permute-start(bf16[2,1,256,512]{3,2,1,0:T(8,128)(2,1)} %slice.230), channel_id=1, source_target_pairs={{0,2},{1,3},{2,0},{3,1},{4,6},{5,7},{6,4},{7,5},{8,10},{9,11},{10,... | collective-permute-start | bytes 1572872 | tf_op jit(solution)/shard_map/ppermute | solution.py:901
  377.4 52.3 %collective-permute-start.53 = (bf16[2,2,256,512]{3,2,1,0:T(8,128)(2,1)S(1)}, bf16[2,2,256,512]{3,2,1,0:T(8,128)(2,1)S(1)}, u32[]{:S(2)}, u32[]{:S(2)}) collective-permute-start(bf16[2,2,256,512]{3,2,1,0:T(8,128)(2,1)S(1)} %slice.294), channel_id=1, source_target_pairs={{0,4},{1,5},{2,6},{3,7},{4,0},{5,1},{6,2},{7,3},{8,12},{9,13},{10,... | collective-permute-start | bytes 3145736 | tf_op jit(solution)/shard_map/ppermute | solution.py:901
  387.4 36.2 %collective-permute-start.51 = (bf16[272,1024]{1,0:T(8,128)(2,1)}, bf16[272,1024]{1,0:T(8,128)(2,1)}, u32[]{:S(2)}, u32[]{:S(2)}) collective-permute-start(bf16[272,1024]{1,0:T(8,128)(2,1)} %get-tuple-element.187), channel_id=1, source_target_pairs={{0,24},{8,16},{16,8},{24,0},{1,25},{9,17},{17,9},{25,1},{2,26},{10... | collective-permute-start | bytes 1671176 | tf_op jit(solution)/shard_map/ppermute | solution.py:901
  388.9 34.6 %collective-permute-start.50 = (bf16[272,1024]{1,0:T(8,128)(2,1)}, bf16[272,1024]{1,0:T(8,128)(2,1)}, u32[]{:S(2)}, u32[]{:S(2)}) collective-permute-start(bf16[272,1024]{1,0:T(8,128)(2,1)} %get-tuple-element.185), channel_id=1, source_target_pairs={{0,16},{8,24},{16,0},{24,8},{1,17},{9,25},{17,1},{25,9},{2,18},{10... | collective-permute-start | bytes 1671176 | tf_op jit(solution)/shard_map/ppermute | solution.py:901
  390.2 33.3 %collective-permute-start.49 = (bf16[272,1024]{1,0:T(8,128)(2,1)}, bf16[272,1024]{1,0:T(8,128)(2,1)}, u32[]{:S(2)}, u32[]{:S(2)}) collective-permute-start(bf16[272,1024]{1,0:T(8,128)(2,1)} %get-tuple-element.179), channel_id=1, source_target_pairs={{0,8},{8,0},{16,24},{24,16},{1,9},{9,1},{17,25},{25,17},{2,10},{10... | collective-permute-start | bytes 1671176 | tf_op jit(solution)/shard_map/ppermute | solution.py:901
  423.4 36.0 %collective-permute-start.56 = (bf16[2,2,256,512]{3,2,1,0:T(8,128)(2,1)}, bf16[2,2,256,512]{3,2,1,0:T(8,128)(2,1)}, u32[]{:S(2)}, u32[]{:S(2)}) collective-permute-start(bf16[2,2,256,512]{3,2,1,0:T(8,128)(2,1)} %slice.232), channel_id=1, source_target_pairs={{0,2},{1,3},{2,0},{3,1},{4,6},{5,7},{6,4},{7,5},{8,10},{9,11},{10,... | collective-permute-start | bytes 3145736 | tf_op jit(solution)/shard_map/ppermute | solution.py:901
  426.2 30.8 %collective-permute-start.52 = (bf16[272,1024]{1,0:T(8,128)(2,1)}, bf16[272,1024]{1,0:T(8,128)(2,1)S(1)}, u32[]{:S(2)}, u32[]{:S(2)}) collective-permute-start(bf16[272,1024]{1,0:T(8,128)(2,1)} %get-tuple-element.189), channel_id=1, source_target_pairs={{0,8},{8,0},{16,24},{24,16},{1,9},{9,1},{17,25},{25,17},{2,10},{10... | collective-permute-start | bytes 1671176 | tf_op jit(solution)/shard_map/ppermute | solution.py:901
  427.6 29.4 %collective-permute-start.57 = (bf16[272,1024]{1,0:T(8,128)(2,1)}, bf16[272,1024]{1,0:T(8,128)(2,1)S(1)}, u32[]{:S(2)}, u32[]{:S(2)}) collective-permute-start(bf16[272,1024]{1,0:T(8,128)(2,1)} %get-tuple-element.202), channel_id=1, source_target_pairs={{0,16},{8,24},{16,0},{24,8},{1,17},{9,25},{17,1},{25,9},{2,18},{10... | collective-permute-start | bytes 1671176 | tf_op jit(solution)/shard_map/ppermute | solution.py:901
  501.7 38.2 %collective-permute-start.72 = (bf16[2,256,512]{2,1,0:T(8,128)(2,1)S(1)}, bf16[2,256,512]{2,1,0:T(8,128)(2,1)S(1)}, u32[]{:S(2)}, u32[]{:S(2)}) collective-permute-start(bf16[2,256,512]{2,1,0:T(8,128)(2,1)S(1)} %add_convert_fusion.8), channel_id=1, source_target_pairs={{0,4},{1,5},{2,6},{3,7},{4,0},{5,1},{6,2},{7,3},{8,12},{9,13},{10,... | collective-permute-start | bytes 1572872 | tf_op jit(solution)/shard_map/ppermute | solution.py:901
  502.1 49.7 %collective-permute-start.71 = (bf16[272,1024]{1,0:T(8,128)(2,1)S(1)}, bf16[272,1024]{1,0:T(8,128)(2,1)S(1)}, u32[]{:S(2)}, u32[]{:S(2)}) collective-permute-start(bf16[272,1024]{1,0:T(8,128)(2,1)S(1)} %copy-done.48), channel_id=1, source_target_pairs={{0,4},{1,5},{2,6},{3,7},{4,0},{5,1},{6,2},{7,3},{8,12},{9,13},{10,... | collective-permute-start | bytes 1671176 | tf_op jit(solution)/shard_map/ppermute | solution.py:901
  506.8 35.7 %collective-permute-start.68 = (bf16[256,1024]{1,0:T(8,128)(2,1)S(1)}, bf16[256,1024]{1,0:T(8,128)(2,1)S(1)}, u32[]{:S(2)}, u32[]{:S(2)}) collective-permute-start(bf16[256,1024]{1,0:T(8,128)(2,1)S(1)} %get-tuple-element.257), channel_id=1, source_target_pairs={{0,8},{8,0},{16,24},{24,16},{1,9},{9,1},{17,25},{25,17},{2,10},{10... | collective-permute-start | bytes 1572872 | tf_op jit(solution)/shard_map/ppermute | solution.py:901
  508.2 34.3 %collective-permute-start.69 = (bf16[256,1024]{1,0:T(8,128)(2,1)S(1)}, bf16[256,1024]{1,0:T(8,128)(2,1)S(1)}, u32[]{:S(2)}, u32[]{:S(2)}) collective-permute-start(bf16[256,1024]{1,0:T(8,128)(2,1)S(1)} %get-tuple-element.258), channel_id=1, source_target_pairs={{0,16},{8,24},{16,0},{24,8},{1,17},{9,25},{17,1},{25,9},{2,18},{10... | collective-permute-start | bytes 1572872 | tf_op jit(solution)/shard_map/ppermute | solution.py:901
  508.8 33.7 %collective-permute-start.70 = (bf16[256,1024]{1,0:T(8,128)(2,1)S(1)}, bf16[256,1024]{1,0:T(8,128)(2,1)S(1)}, u32[]{:S(2)}, u32[]{:S(2)}) collective-permute-start(bf16[256,1024]{1,0:T(8,128)(2,1)S(1)} %get-tuple-element.259), channel_id=1, source_target_pairs={{0,24},{8,16},{16,8},{24,0},{1,25},{9,17},{17,9},{25,1},{2,26},{10... | collective-permute-start | bytes 1572872 | tf_op jit(solution)/shard_map/ppermute | solution.py:901
  (132 other events, 2086.7 us)

commit v3 on v2

--- a/solution.py
+++ b/solution.py
@@ -16,6 +16,7 @@
 EPSILON = 1e-06
 LANES = 128
 PAIRS = KVH // 2
+BLOCKS = 2
 GATE_ROWS = 16
 
 BF = jnp.bfloat16
@@ -94,14 +95,14 @@
     return on, on + qn, on + qn + kn, on + qn + 2 * kn
 
 
-def qkv_kernel(nr, nh, ids, rows_ref, gain_ref, cos_ref, sin_ref, *rest):
+def qkv_kernel(nr, nh, ids, own_ref, other_ref, gain_ref, cos_ref, sin_ref, *rest):
     weights = rest[:nh]
     q_ref, k_ref, v_ref, normed_ref = rest[nh:]
-    width = rows_ref.shape[-1]
+    width = own_ref.shape[-1]
     chunk = width // nr
     qn, kn = H * HD // nh, KVH * HD // nh
     at_q, at_k, _, at_end = columns(nh, width)
-    normed_ref[...] = (rows_ref[0].astype(F32) * gain_ref[...]).astype(BF)
+    normalize(own_ref, other_ref, gain_ref, normed_ref)
     cosine, sine = cos_ref[...], sin_ref[...]
     for h in range(nh):
         total = None
@@ -115,34 +116,54 @@
         k_ref[:, here] = turn(total[:, :kn], cosine, sine, 1.0).astype(BF)
         v_ref[:, here] = total[:, kn:].astype(BF)
 
+    rows = q_ref.shape[0]
+
     @pl.when(pl.program_id(0) == 0)
     def _():
         for h in range(nh):
             total = None
             for r in range(nr):
                 part = dot(
-                    normed_ref[:, span(row_chunk(ids, r, nr), chunk)], weights[h][r, :, at_q:at_k]
+                    normed_ref[:rows, span(row_chunk(ids, r, nr), chunk)], weights[h][r, :, at_q:at_k]
                 )
                 total = part if total is None else total + part
-            turned = turn(total, cosine, sine, 1.0).astype(BF).astype(F32) * HD**-0.5
+            turned = turn(total, cosine[:rows], sine[:rows], 1.0).astype(BF).astype(F32) * HD**-0.5
             q_ref[:, span(half_chunk(ids, h, nh), qn)] = turned.astype(BF)
 
 
+def normalize(own_ref, other_ref, gain_ref, normed_ref):
+    own = pl.program_id(0) < pl.num_programs(0) // 2
+    rows = jnp.where(own, own_ref[...], other_ref[...])
+    normed_ref[...] = (rows.astype(F32) * gain_ref[...]).astype(BF)
+
+
+def rows_specs(steps, shape):
+    half = steps // 2
+    return [
+        pl.BlockSpec(shape, lambda i, _: (jnp.minimum(i, half - 1), 0)),
+        pl.BlockSpec(shape, lambda i, _: (jnp.maximum(i - half, 0), 0)),
+    ]
+
+
+def flat_rows(rows):
+    return [part.reshape(-1, part.shape[-1]) for part in rows]
+
+
 def project(ids, rows, gain, cosine, sine, weights):
-    slots, length, width = rows.shape
+    slots, (length, width) = 2 * rows[0].shape[0], rows[0].shape[1:]
     nr, nh = weights[0].shape[0], len(weights)
-    flat = weights
+    tile, steps = BLOCKS * length, slots // BLOCKS
     return call(
         functools.partial(qkv_kernel, nr, nh),
-        (slots,),
+        (steps,),
         ids,
-        [rows, gain, cosine, sine, *flat],
+        [*flat_rows(rows), gain, cosine, sine, *weights],
         [
-            pl.BlockSpec((1, length, width), lambda i, _: (i, 0, 0)),
+            *rows_specs(steps, (tile, width)),
             whole_spec(gain.shape),
-            pl.BlockSpec((length, LANES), lambda i, _: (i, 0)),
-            pl.BlockSpec((length, LANES), lambda i, _: (i, 0)),
-            *[whole_spec(w.shape) for w in flat],
+            pl.BlockSpec((tile, LANES), lambda i, _: (i, 0)),
+            pl.BlockSpec((tile, LANES), lambda i, _: (i, 0)),
+            *[whole_spec(w.shape) for w in weights],
         ],
         [
             jax.ShapeDtypeStruct((length, H * HD), BF),
@@ -151,10 +172,10 @@
         ],
         [
             whole_spec((length, H * HD)),
-            pl.BlockSpec((length, KVH * HD), lambda i, _: (i, 0)),
-            pl.BlockSpec((length, KVH * HD), lambda i, _: (i, 0)),
+            pl.BlockSpec((tile, KVH * HD), lambda i, _: (i, 0)),
+            pl.BlockSpec((tile, KVH * HD), lambda i, _: (i, 0)),
         ],
-        [pltpu.VMEM((length, width), BF)],
+        [pltpu.VMEM((tile, width), BF)],
     )
 
 
@@ -246,6 +267,8 @@
             pads_q.append(q_pad)
             pads_o.append(o_pad)
     all_q = jnp.concatenate(pads_q, axis=0)
+    every_q = jnp.concatenate(queries, axis=0)
+    every_o = jnp.concatenate(outs, axis=0)
     all_o = jnp.concatenate(pads_o, axis=0)
     sum_ref[...] = jnp.zeros_like(sum_ref)
 
@@ -258,15 +281,11 @@
         k_here, x_here = k_ref[at, :], kx_ref[at, :]
         keys = jnp.concatenate([k_here, x_here], axis=1)
         values = jnp.concatenate([v_ref[at, :], x_here], axis=1)
-        probs, d_scores = [], []
-        for n in range(4):
-            prob = jnp.exp(dot_nt(keys, queries[n]))
-            d_score = (prob * dot_nt(values, outs[n])).astype(BF)
-            probs.append(prob.astype(BF))
-            d_scores.append(d_score)
-            sum_ref[n] += dot_tn(d_score, k_here)
-        out_ref[1, put, :] = dot(jnp.concatenate(probs, axis=1), all_o).astype(BF)
-        d_key = dot(jnp.concatenate(d_scores, axis=1), all_q)
+        probs = jnp.exp(dot_nt(keys, every_q))
+        d_scores = (probs * dot_nt(values, every_o)).astype(BF)
+        sum_ref[...] += dot_tn(k_here, d_scores)
+        out_ref[1, put, :] = dot(probs.astype(BF), all_o).astype(BF)
+        d_key = dot(d_scores, all_q)
         d_key = turn(d_key, cos_ref[at, :], sin_ref[at, :], -1.0)
         out_ref[0, put, :] = d_key.astype(BF)
         return 0
@@ -275,25 +294,31 @@
         lax.fori_loop(0, spans, functools.partial(one_span, part=part, out_ref=out_ref), 0)
     cosine, sine = cos_ref[:rows, :], sin_ref[:rows, :]
     for t in range(2):
-        tile = to_half(sum_ref[2 * t], t, 0) + to_half(sum_ref[2 * t + 1], t, 1)
+        d_query = [sum_ref[:, n * rows : (n + 1) * rows].T for n in (2 * t, 2 * t + 1)]
+        tile = to_half(d_query[0], t, 0) + to_half(d_query[1], t, 1)
         turned = turn(tile * HD**-0.5, cosine, sine, -1.0)
         dq_ref[:, t * LANES : (t + 1) * LANES] = turned.astype(BF)
 
 
 def attend_back_part(*refs):
-    attend_back_kernel(512, *refs[:11], *refs[14:])
-
-
-def attend_back(ids, q, d_out, out, lse, k, v, key_extra, query_extra, cosine, sine, first, count, done):
+    attend_back_kernel(1024, *refs[:11], *refs[14:])
+
+
+def attend_back(ids, q, d_out, out, lse, k, v, key_extra, query_extra, cosine, sine, half=None, done=None):
     length, keys = q.shape[0], k.shape[0]
-    quad = pl.BlockSpec((length, 2 * LANES), lambda p, _: (0, first + p))
-    pair = pl.BlockSpec((keys, LANES), lambda p, _: (0, first + p))
+    count = PAIRS if half is None else PAIRS // 2
+
+    def at(p, ids):
+        return p if half is None else (ids[2] ^ half) * count + p
+
+    quad = pl.BlockSpec((length, 2 * LANES), lambda p, ids: (0, at(p, ids)))
+    pair = pl.BlockSpec((keys, LANES), lambda p, ids: (0, at(p, ids)))
     ins = [q, d_out, out, lse, k, v, key_extra, query_extra, cosine, sine]
     specs = [
         quad,
         quad,
         quad,
-        pl.BlockSpec((1, length, LANES), lambda p, _: (first + p, 0, 0)),
+        pl.BlockSpec((1, length, LANES), lambda p, ids: (at(p, ids), 0, 0)),
         pair,
         pair,
         whole_spec(key_extra.shape),
@@ -305,7 +330,7 @@
         ins += done
         specs += [pl.BlockSpec(memory_space=pl.ANY)] * 3
     return call(
-        attend_back_part if done is not None else functools.partial(attend_back_kernel, 512),
+        attend_back_part if done is not None else functools.partial(attend_back_kernel, 1024),
         (count,),
         ids,
         ins,
@@ -315,8 +340,8 @@
             jax.ShapeDtypeStruct((2, keys // 2, KVH * HD), BF),
             jax.ShapeDtypeStruct((2, keys // 2, KVH * HD), BF),
         ],
-        [quad] + [pl.BlockSpec((2, keys // 2, LANES), lambda p, _: (0, 0, first + p))] * 2,
-        [pltpu.VMEM((4, length, LANES), F32)],
+        [quad] + [pl.BlockSpec((2, keys // 2, LANES), lambda p, ids: (0, 0, at(p, ids)))] * 2,
+        [pltpu.VMEM((LANES, 4 * length), F32)],
         aliases={11: 0, 12: 1, 13: 2} if done is not None else None,
     )
 
@@ -372,19 +397,23 @@
     d_middle = c_ref[...] + inverse * scaled - middle * (inverse * inverse * inverse * inner)
     dx2_ref[...] = d_middle
     dr_ref[...] = d_middle.astype(BF)
-    term_ref[...] = (d_normed * middle * inverse).astype(BF)
-    ones = jnp.ones((middle.shape[0], LANES), BF)
+    term_ref[...] = d_normed * middle * inverse
+    fold = width // cols
+    rows = chunk // fold
     for r in range(nr):
         at = span(row_chunk(ids, r, nr), chunk)
         low = low_ref[:, at]
-        gain_grad = dot_tn(term_ref[:, at], ones).astype(BF)
+        gain_grad = jnp.sum(term_ref[:, at], axis=0, keepdims=True)
+        gain_grad = jnp.concatenate([gain_grad] * (width // chunk), axis=1)
         total = None
         for h in range(nh):
             branch = dr_ref[:, span(half_chunk(ids, h, nh), cols)]
             part = dot_nt(branch, weights[h][r])
             total = part if total is None else total + part
-            grads[h][r, :, :cols] = dot_tn(low, branch).astype(BF)
-            grads[h][r, :, cols:] = gain_grad
+            grad = dot_tn(low, branch).astype(BF)
+            for f in range(fold):
+                grads[h][r, :rows, f * cols : (f + 1) * cols] = grad[f * rows : (f + 1) * rows]
+            grads[h][r, rows:] = jnp.broadcast_to(gain_grad, (GATE_ROWS, width)).astype(BF)
         do_ref[:, at] = total.astype(BF)
 
 
@@ -393,7 +422,8 @@
     ins = [c, x2, gain, dn2, low, *weights]
     rows, cols = H * HD // nr, c.shape[1] // nh
     outs = [jax.ShapeDtypeStruct(c.shape, F32), jax.ShapeDtypeStruct((c.shape[0], H * HD), BF)]
-    outs += [jax.ShapeDtypeStruct((nr, rows, cols + LANES), BF)] * nh
+    high = rows * cols // c.shape[1] + GATE_ROWS
+    outs += [jax.ShapeDtypeStruct((nr, high, c.shape[1]), BF)] * nh
     got = call(
         functools.partial(out_back_kernel, nr, nh),
         (1,),
@@ -402,7 +432,7 @@
         [whole_spec(i.shape) for i in ins[:5]] + [out_spec(w, cols) for w in weights],
         outs,
         [whole_spec(o.shape) for o in outs],
-        [pltpu.VMEM(c.shape, BF), pltpu.VMEM(c.shape, BF)],
+        [pltpu.VMEM(c.shape, BF), pltpu.VMEM(c.shape, F32)],
     )
     return got[0], got[1], got[2:]
 
@@ -594,10 +624,10 @@
     )
 
 
-def mixture_kernel(nz, groups, per, experts, tile, ids, slot_ref, gate_ref, *rest):
+def mixture_kernel(nz, w_parts, groups, per, experts, tile, ids, slot_ref, gate_ref, *rest):
     n2_in, rest = rest[:groups], rest[groups:]
     c_in, rest = rest[:groups], rest[groups:]
-    w_in, rest = rest[: 3 * nz], rest[3 * nz :]
+    w_in, rest = rest[: len(w_parts)], rest[len(w_parts) :]
     dn2_out, rest = rest[:groups], rest[groups:]
     y_out, rest = rest[: groups // 2], rest[groups // 2 :]
     dw_out, rest = rest[:nz], rest[nz:]
@@ -614,15 +644,16 @@
     def c_copy(g):
         return pltpu.make_async_copy(c_in[g], c_ref.at[pl.ds(g * per, per)], c_sem.at[g])
 
-    def w_copy(r, k):
-        return pltpu.make_async_copy(w_in[3 * r + k], w_ref.at[r, :, k], w_sem.at[r, k])
+    def w_copy(n):
+        r, first, count = w_parts[n]
+        to = w_ref.at[:, pl.ds(first, count), span(z_chunk(ids, r, nz), chunk)]
+        return pltpu.make_async_copy(w_in[n], to, w_sem.at[n])
 
     for g in range(groups):
         c_copy(g).start()
         n2_copy(g).start()
-    for r in range(nz):
-        for k in range(3):
-            w_copy(r, k).start()
+    for n in range(len(w_parts)):
+        w_copy(n).start()
 
     def chosen_rows(i):
         places = lax.broadcasted_iota(jnp.int32, (CAP, length), 0).astype(F32)
@@ -649,23 +680,19 @@
         c_copy(g).wait()
         n2_copy(g).wait()
         lax.fori_loop(g * per, (g + 1) * per, gather, 0)
-    for r in range(nz):
-        for k in range(3):
-            w_copy(r, k).wait()
+    for n in range(len(w_parts)):
+        w_copy(n).wait()
 
     def dw_copy(j, r):
-        return pltpu.make_async_copy(dw_ref.at[j, r], dw_out[r].at[j], dw_sem.at[j, r])
+        rows = span(z_chunk(ids, r, nz), chunk)
+        return pltpu.make_async_copy(dw_ref.at[j, :, rows], dw_out[r].at[j], dw_sem.at[j, r])
 
     for j in range(experts):
 
         def one_tile(i, _, j=j):
             at = pl.ds(pl.multiple_of(i * tile, tile), tile)
-            a = b = ch = None
-            for r in range(nz):
-                cols = span(z_chunk(ids, r, nz), chunk)
-                x, c = x_rows[j, at, cols], c_rows[j, at, cols]
-                parts = (dot(x, w_ref[r, j, 0]), dot(x, w_ref[r, j, 1]), dot(c, w_ref[r, j, 2]))
-                a, b, ch = parts if a is None else (a + parts[0], b + parts[1], ch + parts[2])
+            x, c = x_rows[j, at], c_rows[j, at]
+            a, b, ch = dot(x, w_ref[j, 0]), dot(x, w_ref[j, 1]), dot(c, w_ref[j, 2])
             gate = gate_rows[j, at][:, :1]
             sig = 1.0 / (1.0 + jnp.exp(-a))
             act = a * sig
@@ -680,20 +707,19 @@
             return 0
 
         lax.fori_loop(0, blocks * CAP // tile, one_tile, 0)
+        for part in range(width // chunk):
+            cols = slice(part * chunk, (part + 1) * chunk)
+            for k in range(3):
+                x = (c_rows if k == 2 else x_rows)[j, :, cols]
+                dw_ref[j, k, cols] = dot_tn(x, inner_ref[k]).astype(BF)
         for r in range(nz):
-            cols = span(z_chunk(ids, r, nz), chunk)
-            x, c = x_rows[j, :, cols], c_rows[j, :, cols]
-            for k in range(3):
-                dw_ref[j, r, k] = dot_tn(c if k == 2 else x, inner_ref[k]).astype(BF)
             dw_copy(j, r).start()
 
         def back_tile(i, _, j=j):
             at = pl.ds(pl.multiple_of(i * tile, tile), tile)
             da, db, hg = inner_ref[0, at], inner_ref[1, at], inner_ref[2, at]
-            for r in range(nz):
-                cols = span(z_chunk(ids, r, nz), chunk)
-                c_rows[j, at, cols] = dot_nt(hg, w_ref[r, j, 2]).astype(BF)
-                x_rows[j, at, cols] = (dot_nt(da, w_ref[r, j, 0]) + dot_nt(db, w_ref[r, j, 1])).astype(BF)
+            c_rows[j, at] = dot_nt(hg, w_ref[j, 2]).astype(BF)
+            x_rows[j, at] = (dot_nt(da, w_ref[j, 0]) + dot_nt(db, w_ref[j, 1])).astype(BF)
             return 0
 
         lax.fori_loop(0, blocks * CAP // tile, back_tile, 0)
@@ -747,33 +773,40 @@
     per, length, width = n2_groups[0].shape
     blocks, experts, _ = slots.shape
     high, rows = c_groups[0].shape[1], blocks * CAP
-    part = weights[0][0].shape
-    matrices = (part[0], 3) + part[1:]
+    flat = [w for row in weights for w in row]
+    w_parts = []
+    for r, row in enumerate(weights):
+        first = 0
+        for w in row:
+            w_parts.append((r, first, w.shape[1]))
+            first += w.shape[1]
+    part = flat[0].shape
+    matrices = (part[0], 3) + part[2:]
     anywhere = pl.BlockSpec(memory_space=pl.ANY)
     outs = [jax.ShapeDtypeStruct((per, length, width), BF)] * groups
     outs += [jax.ShapeDtypeStruct((groups // 2 * per, high, width), BF)] * 2
     outs += [jax.ShapeDtypeStruct(matrices, BF)] * nz
     got = call(
-        functools.partial(mixture_kernel, nz, groups, per, experts, 256),
+        functools.partial(mixture_kernel, nz, tuple(w_parts), groups, per, experts, 256),
         (1,),
         ids,
-        [slots, gates, *n2_groups, *c_groups, *[w for row in weights for w in row]],
-        [whole_spec(slots.shape), whole_spec(gates.shape)] + [anywhere] * (2 * groups + 3 * nz),
+        [slots, gates, *n2_groups, *c_groups, *flat],
+        [whole_spec(slots.shape), whole_spec(gates.shape)] + [anywhere] * (2 * groups + len(flat)),
         outs,
         [anywhere] * len(outs),
         [
             pltpu.VMEM((blocks, length, width), BF),
             pltpu.VMEM((blocks, high, width), BF),
-            pltpu.VMEM((nz,) + matrices, BF),
+            pltpu.VMEM(matrices[:2] + (width,) + matrices[3:], BF),
             pltpu.VMEM((experts, rows, width), BF),
             pltpu.VMEM((experts, rows, width), BF),
             pltpu.VMEM((experts, rows, LANES), F32),
             pltpu.VMEM((experts, rows, LANES), F32),
             pltpu.VMEM((3, rows, part[-1]), BF),
-            pltpu.VMEM((experts, nz) + matrices[1:], BF),
+            pltpu.VMEM(matrices[:2] + (width,) + matrices[3:], BF),
             pltpu.SemaphoreType.DMA((groups,)),
             pltpu.SemaphoreType.DMA((groups,)),
-            pltpu.SemaphoreType.DMA((nz, 3)),
+            pltpu.SemaphoreType.DMA((len(flat),)),
             pltpu.SemaphoreType.DMA((groups,)),
             pltpu.SemaphoreType.DMA((groups,)),
             pltpu.SemaphoreType.DMA((experts, nz)),
@@ -782,77 +815,62 @@
     return got[:groups], got[groups : groups + 2], got[groups + 2 :]
 
 
-def keys_grad_kernel(nr, nh, ids, rows_ref, gain_ref, own_ref, other_ref, *rest):
-    grads, (normed_ref, acc_ref) = rest[:nh], rest[nh:]
-    chunk, kn = rows_ref.shape[-1] // nr, KVH * HD // nh
-    step, last = pl.program_id(0), pl.num_programs(0) - 1
-    normed_ref[...] = (rows_ref[0].astype(F32) * gain_ref[...]).astype(BF)
+def half_grads_kernel(nr, ids, own_rows, other_rows, gain_ref, dq_ref, own_ref, other_ref, grad_ref, normed_ref, acc_ref):
+    chunk, qn, kn = grad_ref.shape[1], dq_ref.shape[1], own_ref.shape[2]
+    step, count = pl.program_id(0), pl.num_programs(0)
+    normalize(own_rows, other_rows, gain_ref, normed_ref)
 
     @pl.when(step == 0)
     def _():
-        acc_ref[...] = jnp.zeros_like(acc_ref)
-
-    def add(dkv_ref):
         for r in range(nr):
             x = normed_ref[:, span(row_chunk(ids, r, nr), chunk)]
-            for h in range(nh):
-                here = span(half_chunk(ids, h, nh), kn)
-                acc_ref[r * nh + h, :, :kn] += dot_tn(x, dkv_ref[0, :, here])
-                acc_ref[r * nh + h, :, kn:] += dot_tn(x, dkv_ref[1, :, here])
-
-    half = pl.num_programs(0) // 2
-    pl.when(step < half)(lambda: add(own_ref))
-    pl.when(step >= half)(lambda: add(other_ref))
-
-    @pl.when(step == last)
+            grad_ref[r, :, :qn] = dot_tn(x[: dq_ref.shape[0]], dq_ref[...]).astype(BF)
+        acc_ref[...] = jnp.zeros_like(acc_ref)
+
+    def add(dkv_ref):
+        grad = jnp.concatenate([dkv_ref[0], dkv_ref[1]], axis=1)
+        for r in range(nr):
+            acc_ref[r] += dot_tn(normed_ref[:, span(row_chunk(ids, r, nr), chunk)], grad)
+
+    pl.when(step < count // 2)(lambda: add(own_ref))
+    pl.when(step >= count // 2)(lambda: add(other_ref))
+
+    @pl.when(step == count - 1)
     def _():
-        for n in range(nr * nh):
-            grads[n % nh][n // nh] = acc_ref[n].astype(BF)
-
-
-def keys_grads(ids, rows, gain, dkv, nr, nh):
-    slots, length, width = rows.shape
-    cols, half = 2 * KVH * HD // nh, slots // 2
-    outs = [jax.ShapeDtypeStruct((nr, width // nr, cols), BF)] * nh
+        for r in range(nr):
+            grad_ref[r, :, qn:] = acc_ref[r].astype(BF)
+
+
+def half_grads(ids, rows, gain, dq, dkv, half, nr, nh):
+    slots, (length, width) = 2 * rows[0].shape[0], rows[0].shape[1:]
+    qn, kn = H * HD // nh, KVH * HD // nh
+
+    def body(ids, own_rows, other_rows, gain_ref, dq_ref, own_ref, other_ref, grad_ref, normed_ref, acc_ref):
+        half_grads_kernel(
+            nr, ids, own_rows, other_rows, gain_ref, dq_ref, own_ref, other_ref, grad_ref, normed_ref, acc_ref
+        )
+
+    def at(ids):
+        return half_chunk(ids, half, nh)
+
+    out = jax.ShapeDtypeStruct((nr, width // nr, qn + 2 * kn), BF)
+    tile, steps = BLOCKS * length, slots // BLOCKS
+    middle = steps // 2
     return call(
-        functools.partial(keys_grad_kernel, nr, nh),
-        (slots,),
+        body,
+        (steps,),
         ids,
-        [rows, gain, *dkv],
+        [*flat_rows(rows), gain, dq, *dkv],
         [
-            pl.BlockSpec((1, length, width), lambda i, _: (i, 0, 0)),
+            *rows_specs(steps, (tile, width)),
             whole_spec(gain.shape),
-            pl.BlockSpec((2, length, KVH * HD), lambda i, _: (0, jnp.minimum(i, half - 1), 0)),
-            pl.BlockSpec((2, length, KVH * HD), lambda i, _: (0, jnp.maximum(i - half, 0), 0)),
+            pl.BlockSpec((length, qn), lambda i, ids: (0, at(ids))),
+            pl.BlockSpec((2, tile, kn), lambda i, ids: (0, jnp.minimum(i, middle - 1), at(ids))),
+            pl.BlockSpec((2, tile, kn), lambda i, ids: (0, jnp.maximum(i - middle, 0), at(ids))),
         ],
-        outs,
-        [whole_spec(o.shape) for o in outs],
-        [pltpu.VMEM((length, width), BF), pltpu.VMEM((nr * nh, width // nr, cols), F32)],
-    )
-
-
-def queries_grad_kernel(nr, nh, ids, rows_ref, gain_ref, dq_ref, *rest):
-    grads, normed_ref = rest[:nh], rest[nh]
-    chunk, qn = rows_ref.shape[-1] // nr, H * HD // nh
-    normed_ref[...] = (rows_ref[...].astype(F32) * gain_ref[...]).astype(BF)
-    for r in range(nr):
-        x = normed_ref[:, span(row_chunk(ids, r, nr), chunk)]
-        for h in range(nh):
-            grads[h][r] = dot_tn(x, dq_ref[:, span(half_chunk(ids, h, nh), qn)]).astype(BF)
-
-
-def queries_grads(ids, rows, gain, dq, nr, nh):
-    ins = [rows, gain, dq]
-    outs = [jax.ShapeDtypeStruct((nr, rows.shape[1] // nr, H * HD // nh), BF)] * nh
-    return call(
-        functools.partial(queries_grad_kernel, nr, nh),
-        (1,),
-        ids,
-        ins,
-        [whole_spec(i.shape) for i in ins],
-        outs,
-        [whole_spec(o.shape) for o in outs],
-        [pltpu.VMEM(rows.shape, BF)],
+        out,
+        whole_spec(out.shape),
+        [pltpu.VMEM((tile, width), BF), pltpu.VMEM((nr, width // nr, 2 * kn), F32)],
     )
 
 
@@ -905,6 +923,10 @@
     return lax.optimization_barrier((value,) + done)[0]
 
 
+def together(*values):
+    return lax.optimization_barrier(values)
+
+
 def pick(array, index):
     return lax.dynamic_index_in_dim(array, index, 0, keepdims=False)
 
@@ -937,19 +959,6 @@
     for value in values[1:]:
         total = total + value.astype(F32)
     return total.astype(BF)
-
-
-def scatter_rows(total, z, core):
-    chips = lax.axis_size("shard") // 2
-    parts = total.reshape(chips, total.shape[0] // chips, total.shape[1])
-    parts = [pick(parts, z ^ r) for r in range(chips)]
-    step, near = swap(parts[3], "shard", 2), swap(parts[1], "shard", 2)
-    far = add_low(parts[2], step)
-    rows = parts[0].astype(F32) + near.astype(F32) + swap(far, "shard", 4).astype(F32)
-    rows = rows.reshape(2, rows.shape[0] // 2, rows.shape[1])
-    mine = pick(rows, core)
-    other = swap(pick(rows, 1 - core).astype(BF), "shard", 1).astype(F32)
-    return (jnp.where(core == 0, mine, other), jnp.where(core == 0, other, mine)), far
 
 
 def body(
@@ -1004,6 +1013,25 @@
     numbers = jnp.arange(EXPERTS, dtype=jnp.int32)
     lines = EXPERTS * length // width
 
+    def positions(start):
+        s_late = after(s, start)
+        owners = jnp.stack([s_late ^ (2 * r + k) for k in range(2) for r in range(chips)])
+        places = (owners[:, None] * length + jnp.arange(length)[None, :]).reshape(n_shard * length)
+        freqs = 10000.0 ** (-(jnp.arange(HD // 2, dtype=F32) * 2.0 / HD))
+        angles = places.astype(F32)[:, None] * freqs[None, :]
+        cosine, sine = jnp.cos(angles), jnp.sin(angles)
+        cosine = jnp.concatenate([cosine] * 4, axis=1)
+        sine = jnp.concatenate([-sine, sine] * 2, axis=1)
+        every = block_ids[0].reshape(n_shard, length)
+        key_blocks = jnp.concatenate(
+            [pick(every, s_late ^ (2 * r + k)) for k in range(2) for r in range(chips)]
+        )
+        own_blocks = pick(every, s_late)
+        lanes = jnp.arange(LANES, dtype=jnp.int32)[None, :]
+        key_extra = ((lanes == key_blocks[:, None]) | ((lanes >= 16) & (lanes < 19))).astype(BF)
+        query_extra = jnp.where((lanes < 16) & (lanes > own_blocks[:, None]), -1e30, 0.0).astype(BF)
+        return cosine, sine, key_extra, query_extra
+
     def named_experts(routed):
         return routed[0][None, :, :] == numbers[:, None, None]
 
@@ -1018,7 +1046,7 @@
     def own_experts(start):
         low = jnp.stack([m.astype(BF) for m in after((w_gate, w_up, w_down), start)], axis=1)
         low = low.reshape((2, local // 2) + low.shape[1:])
-        return in_order(pick(low, core), swap(pick(low, 1 - core), "shard", 1), core, 2)
+        return pick(low, core), swap(pick(low, 1 - core), "shard", 1)
 
     def over_columns(value):
         return [swap(value, "expert", r) for r in range(1, n_expert)]
@@ -1026,23 +1054,6 @@
     if fast:
         mine, other = pick(packed, core), pick(packed, 1 - core)
         chip = in_order(mine, swap(other, "shard", 1), core, 0)
-
-    s_late = after(s, chip) if fast else s
-    owners = jnp.stack([s_late ^ (2 * r + k) for k in range(2) for r in range(chips)])
-    places = (owners[:, None] * length + jnp.arange(length)[None, :]).reshape(n_shard * length)
-    freqs = 10000.0 ** (-(jnp.arange(HD // 2, dtype=F32) * 2.0 / HD))
-    angles = places.astype(F32)[:, None] * freqs[None, :]
-    cosine, sine = jnp.cos(angles), jnp.sin(angles)
-    cosine = jnp.concatenate([cosine] * 4, axis=1)
-    sine = jnp.concatenate([-sine, sine] * 2, axis=1)
-    every = block_ids[0].reshape(n_shard, length)
-    key_blocks = jnp.concatenate(
-        [pick(every, s_late ^ (2 * r + k)) for k in range(2) for r in range(chips)]
-    )
-    own_blocks = pick(every, s_late)
-    lanes = jnp.arange(LANES, dtype=jnp.int32)[None, :]
-    key_extra = ((lanes == key_blocks[:, None]) | ((lanes >= 16) & (lanes < 19))).astype(BF)
-    query_extra = jnp.where((lanes < 16) & (lanes > own_blocks[:, None]), -1e30, 0.0).astype(BF)
 
     if fast:
         w_near, w_far = swap(chip, "shard", 2), swap(chip, "shard", 4)
@@ -1051,31 +1062,36 @@
         stacked = jnp.stack([chip, w_near, w_far, swap(w_far, "shard", 2)])
         block = jnp.concatenate([pick(stacked, z ^ i) for i in range(chips)], axis=0)
         c_pack = cotangent_rows(chip)
-        chip_w = own_experts(chip).reshape((2, experts, 3, 2 * w_gate.shape[1], w_gate.shape[2]))
-        here = [pick(chip_w, side)[:, k] for k in range(3)]
-        there = [pick(chip_w, 1 - side)[:, k] for k in range(3)]
-        w_got = over_columns(after(block, x_near, *here, *there))
+        w_mine, w_other = own_experts(chip)
+        cosine, sine, key_extra, query_extra = positions(chip)
+        w_got = over_columns(after(block, x_near, w_other))
         x_cross = swap(x_far, "shard", 2)
         c_far = swap(after(c_pack, x_far), "shard", 4)
+        chip_w = in_order(after(w_mine, x_cross), w_other, core, 2)
+        chip_w = chip_w.reshape((2, experts, 3, 2 * w_gate.shape[1], w_gate.shape[2]))
+        here, there = pick(chip_w, side), pick(chip_w, 1 - side)
+        there = [there[:, k : k + 1] for k in range(3)]
         own_core = jnp.stack([scaled_rows, x_near, x_far, x_cross])
         x_other = swap(own_core, "shard", 1)
-        rows = jnp.concatenate([own_core, x_other], axis=0)
-        w_got = [after(got, own_core, c_far, cosine, sine, key_extra, query_extra) for got in w_got]
+        rows = [own_core, x_other]
+        early = (own_core, c_far, cosine, sine, key_extra, query_extra)
+        w_got = [after(got, *early) for got in w_got]
         blocks = jnp.stack([block] + w_got)
         attn_w = [blocks, swap(blocks, "shard", 1)]
         gain_cols = blocks[:, :, at_end:]
         gain_cols = jnp.concatenate([pick(gain_cols, e ^ i) for i in range(n_expert)], axis=0)
-        near_a = swap(after(here[0], blocks), "shard", 2)
+        near_a = swap(after(here[:, :1], blocks), "shard", 2)
         far_a = swap(after(there[0], blocks), "shard", 4)
         c_own_got = over_columns(after(c_pack, attn_w[1]))
     else:
         c_pack = cotangent_rows(packed)
         own_core = jnp.stack(gather_z(scaled_rows))
-        rows = jnp.concatenate([own_core, swap(own_core, "shard", 1)], axis=0)
+        rows = [own_core, swap(own_core, "shard", 1)]
+        cosine, sine, key_extra, query_extra = positions(packed)
         blocks = lax.all_gather(packed[0], ("expert", "shard"), axis=0, tiled=True)
         attn_w = [blocks[None]]
         gain_cols = blocks[:, at_end:]
-        expert_w = gather_z(own_experts(packed))
+        expert_w = gather_z(in_order(*own_experts(packed), core, 2))
     gain_one = gain_cols[:, 0].astype(F32)[None]
     gain_two = gain_cols[:, LANES // 2].astype(F32)[None]
     nr = attn_w[0].shape[0]
@@ -1083,10 +1099,10 @@
     q, k, v = project(ids, rows, gain_one, cosine, sine, attn_w)
     if fast:
         c_far_got = over_columns(after(c_far, q))
-        near_b = swap(after(jnp.stack(here[1:], axis=1), near_a, q), "shard", 2)
-        far_b = swap(after(there[1], far_a, q), "shard", 4)
+        q, near_a, far_a, *c_own_got = together(q, near_a, far_a, *c_own_got)
+        near_b = swap(after(here[:, 1:], q), "shard", 2)
+        far_b = swap(after(there[1], q), "shard", 4)
         c_own = jnp.stack([c_pack] + c_own_got)
-        q = after(q, near_a, far_a, c_own)
     mixed, mixed_low, lse = attend(ids, q, k, v, key_extra, query_extra)
     x2, n2 = project_out(ids, x, mixed_low, gain_two, attn_w)
 
@@ -1100,23 +1116,25 @@
         return gate_here, jnp.where(chosen, ranks, -1.0)
 
     if fast:
-        n2 = after(n2, near_b, far_b, *c_far_got)
+        n2, near_b, far_b, *c_far_got = together(n2, near_b, far_b, *c_far_got)
         n2_far = swap(n2, "shard", 4)
         n2_own_got = over_columns(n2)
-        cross_b = swap(after(jnp.stack([far_a, far_b], axis=1), n2), "shard", 2)
-        n2_far_got = over_columns(after(n2_far, *n2_own_got))
-        c_across = jnp.stack([after(piece, *n2_own_got) for piece in [c_far, *c_far_got]])
-        c_own_other = swap(after(c_own, n2_far), "shard", 1)
+        cross_a = swap(after(far_a, n2), "shard", 2)
+        n2_far, cross_a, *n2_own_got = together(n2_far, cross_a, *n2_own_got)
+        cross_b = swap(after(far_b, n2_far), "shard", 2)
+        n2_far_got = over_columns(n2_far)
         far_c = swap(after(there[2], n2_far), "shard", 4)
+        n2_own = jnp.stack([n2] + n2_own_got)
+        c_across = jnp.stack([after(piece, n2_far) for piece in [c_far, *c_far_got]])
+        far_c, cross_b, n2_own, c_across, *n2_far_got = together(
+            far_c, cross_b, n2_own, c_across, *n2_far_got
+        )
+        n2_across = jnp.stack([n2_far] + n2_far_got)
         cross_c = swap(far_c, "shard", 2)
-        n2_own = jnp.stack([n2] + n2_own_got)
-        n2_own_other = swap(n2_own, "shard", 1)
-        n2_far_got = [after(got, far_c, cross_b, n2_own, c_own_other, c_across) for got in n2_far_got]
-        n2_across = jnp.stack([n2_far] + n2_far_got)
-        c_groups = [c_own, c_across, c_own_other, swap(after(c_across, n2_across), "shard", 1)]
+        n2_groups = [n2_own, n2_across, swap(n2_own, "shard", 1), swap(n2_across, "shard", 1)]
+        c_groups = [c_own, c_across] + [swap(after(g, far_c), "shard", 1) for g in (c_own, c_across)]
         gate_here, slots = places_of(c_groups)
-        n2_groups = [n2_own, n2_across, n2_own_other, swap(n2_across, "shard", 1)]
-        expert_w = [here, [near_a, near_b[:, 0], near_b[:, 1]], [far_a, far_b, far_c], [cross_b[:, 0], cross_b[:, 1], cross_c]]
+        expert_w = [[here], [near_a, near_b], [far_a, far_b, far_c], [cross_a, cross_b, cross_c]]
         dn2_parts, y_parts, d_experts = mixture(
             ids, slots, gate_here, n2_groups, c_groups, expert_w
         )
@@ -1131,7 +1149,8 @@
         d_far = add_low(d_experts[2], after(step, dn2_far))
         y_sum = add_low(y_parts[0], swap(after(y_parts[1], dn2_far), "shard", 1))
         y_sum = y_sum.reshape((2, n_expert) + y_sum.shape[1:])
-        own_got = [after(got, d_far, y_sum) for got in own_got]
+        far_early, near_early = after((d_far[:, :1], d_experts[1][:, :1]), dn2_got)
+        own_got = [after(got, far_early, near_early, y_sum) for got in own_got]
         dn2 = sum([g.astype(F32) for g in own_got + [dn2_got]], own_sums[0].astype(F32))
     else:
         c_own = jnp.stack([c_pack] + over_columns(c_pack))
@@ -1162,53 +1181,72 @@
     dx2, d_mixed, d_out_w = project_out_back(ids, c, x2, gain_two, dn2, mixed_low, attn_w)
     args = (mixed, lse, k, v, key_extra, query_extra, cosine, sine)
     if fast:
-        far_a = swap(after(d_far[:, :2], dn2_got), "shard", 4)
-        near_a = swap(after(d_experts[1][:, :1], dn2_got), "shard", 2)
-        y_across_got = [swap(after(y_sum[1, r], dn2), "expert", r) for r in range(1, n_expert)]
-        done = attend_back(ids, q, d_mixed, *args, 0, PAIRS // 2, None)
-        y_across = add_low(y_sum[1, 0], *[after(got, done[0]) for got in y_across_got])
-        far_b = swap(after(d_far[:, 2:], far_a, done[0]), "shard", 4)
-        near_b = swap(after(d_experts[1][:, 1:], near_a, done[0]), "shard", 2)
-        y_got = [swap(after(y_sum[0, r], y_across), "expert", r) for r in range(1, n_expert)]
-        d_mixed = after(d_mixed, far_a, near_a, y_across)
-        dq, *dkv = attend_back(ids, q, d_mixed, *args, PAIRS // 2, PAIRS // 2, done)
-        y_got = [after(got, dq) for got in y_got]
-        dkv[1] = after(dkv[1], far_b, near_b, *y_got)
-        d_out_sums = add_low(d_out_w[0], swap(after(d_out_w[1], dkv[1]), "shard", 1))
-        d_out_got = [swap(d_out_sums[r], "expert", r) for r in range(1, n_expert)]
+        d_out_sums = add_low(d_out_w[0], swap(d_out_w[1], "shard", 1))
+        far_a, near_a = swap(far_early, "shard", 4), swap(near_early, "shard", 2)
+        y_got = [swap(after(y_sum[1, r], dn2), "expert", r) for r in range(1, n_expert)]
+        done = attend_back(ids, q, after(d_mixed, d_out_sums), *args, 1)
+        y_across = add_low(y_sum[1, 0], *[after(g, done[0]) for g in y_got])
+        dq = after(done[0], y_across, far_a, near_a)
+        far_b = swap(after(d_far[:, 1:], dq), "shard", 4)
+        near_b = swap(after(d_experts[1][:, 1:], dq), "shard", 2)
+        both = jnp.concatenate([y_sum[0], after(d_out_sums, dq)], axis=1)
+        both_got = [swap(both[r], "expert", r) for r in range(1, n_expert)]
+        d_other = half_grads(ids, rows, gain_one, dq, done[1:], 1, nr, nh)
+        dq, *dkv = attend_back(ids, q, after(d_mixed, d_other), *args, 0, done)
+        dq, far_b, near_b, *parts = together(dq, far_b, near_b, *dkv, *both_got)
+        dkv, both_got = parts[:2], parts[2:]
+        d_other = swap(after(d_other, dq), "shard", 1)
+        y_far = swap(after(y_across, dq), "shard", 4)
     else:
-        dq, *dkv = attend_back(ids, q, d_mixed, *args, 0, PAIRS, None)
+        dq, *dkv = attend_back(ids, q, d_mixed, *args)
         y_got = [swap(y_sum[0, r], "expert", r) for r in range(1, n_expert)]
     dkv_core = swap(dkv[1], "shard", 1)
+    d_own = half_grads(ids, rows, gain_one, dq, dkv, 0, nr, nh)
+    if fast:
+        d_own, d_other, dkv_core = together(d_own, d_other, dkv_core)
     dkv_sums = add_low(dkv[0], dkv_core)
     dkv_parts = [dkv_sums[:, r * length : (r + 1) * length] for r in range(chips)]
     if fast:
-        dkv_step, dkv_near = swap(dkv_parts[3], "shard", 2), swap(dkv_parts[1], "shard", 2)
-        d_keys = keys_grads(ids, after(rows, dkv_sums, d_out_sums), gain_one, dkv, nr, nh)
-        dq = after(dq, dkv_step, dkv_near, *d_out_got, *d_keys)
-        d_queries = queries_grads(ids, scaled_rows, gain_one, dq, nr, nh)
-        dkv_far = swap(after(add_low(dkv_parts[2], dkv_step), d_queries[0]), "shard", 4)
-        y_far = swap(after(y_across, d_queries[0]), "shard", 4)
-        d_halves = [swap(d_queries[1], "shard", 1), swap(d_keys[1], "shard", 1)]
-        sums = jnp.concatenate(
-            [add_low(d_queries[0], d_halves[0]), add_low(d_keys[0], d_halves[1])], axis=2
+        sums = add_low(d_own, d_other)
+        dkv_step = swap(dkv_parts[3], "shard", 2)
+        dkv_far = add_low(dkv_parts[2], dkv_step)
+        sums, y_far, dkv_far = together(sums, y_far, dkv_far)
+        got = [swap(sums[r], "expert", r) for r in range(1, n_expert)]
+        dkv_far = swap(dkv_far, "shard", 4)
+        dkv_near = swap(after(dkv_parts[1], dkv_step), "shard", 2)
+        dkv_near, dkv_far, *got = together(dkv_near, dkv_far, *got)
+        both = sum([g.astype(F32) for g in both_got], both[0].astype(F32))
+        y_out, d_out_total = both[: y_sum.shape[2]], both[y_sum.shape[2] :].astype(BF)
+        cols = width // nh
+        high = d_out_total.shape[0] - GATE_ROWS
+        gain_grad = d_out_total[high, : width // n_expert]
+        d_out_total = jnp.concatenate(
+            [d_out_total[:high, f * cols : (f + 1) * cols] for f in range(nh)], axis=0
         )
-        got = [swap(sums[r], "expert", r) for r in range(1, n_expert)]
+        gain_grad = jnp.broadcast_to(gain_grad[:, None], (gain_grad.shape[0], LANES))
+        d_out_total = jnp.concatenate([d_out_total, gain_grad], axis=1)
+        dkv_own = sum([g.astype(F32) for g in (dkv_near, dkv_far)], dkv_parts[0].astype(F32))
         d_total = add_low(sums[0], *got)
-        d_out_total = add_low(d_out_sums[0], *[after(g, sums) for g in d_out_got])
-        dkv_own = sum([g.astype(F32) for g in (dkv_near, dkv_far)], dkv_parts[0].astype(F32))
-        out_sum = sum([after(g, d_total).astype(F32) for g in y_got + [y_far]], y_sum[0, 0].astype(F32))
-        parts, far_part = scatter_rows(jnp.concatenate([d_out_total, d_total], axis=1), z, core)
-        dkv_own = after(dkv_own, far_part)
+        total = jnp.concatenate([d_out_total, d_total], axis=1)
+        total = total.reshape(chips, total.shape[0] // chips, total.shape[1])
+        total = [pick(total, z ^ r) for r in range(chips)]
+        step, near = swap(total[3], "shard", 2), swap(total[1], "shard", 2)
+        far = swap(add_low(total[2], step), "shard", 4)
+        token_grad = rows_back(ids, dq, dkv_own, x, dx2, gain_one, attn_w)
+        summed = total[0].astype(F32) + near.astype(F32) + after(far, token_grad).astype(F32)
+        summed = summed.reshape(2, summed.shape[0] // 2, summed.shape[1])
+        mine = pick(summed, core)
+        other = swap(pick(summed, 1 - core).astype(BF), "shard", 1).astype(F32)
+        parts = (jnp.where(core == 0, mine, other), jnp.where(core == 0, other, mine))
+        out_sum = y_out + after(y_far, far).astype(F32)
     else:
         out_sum = sum([g.astype(F32) for g in y_got], y_sum[0, 0].astype(F32))
-        d_queries = queries_grads(ids, scaled_rows, gain_one, dq, nr, nh)
-        d_keys = keys_grads(ids, rows, gain_one, dkv, nr, nh)
         dkv_own = scatter_z(dkv_parts)
-        joined = jnp.concatenate([d_out_w[0][0], d_queries[0][0], d_keys[0][0]], axis=1)
+        token_grad = rows_back(ids, dq, dkv_own, x, dx2, gain_one, attn_w)
+        gain_grad = jnp.broadcast_to(d_out_w[0][0, width][:, None], (width, LANES))
+        joined = jnp.concatenate([d_out_w[0][0, :width], gain_grad, d_own[0]], axis=1)
         joined = lax.psum_scatter(joined, ("expert", "shard"), scatter_dimension=0, tiled=True)
         parts = [joined.astype(F32)]
-    token_grad = rows_back(ids, dq, dkv_own, x, dx2, gain_one, attn_w)
 
     on, qn, kn = width // nh, H * HD // nh, KVH * HD // nh
     start = on + LANES
@@ -1242,7 +1280,7 @@
     half = d_chip.shape[2] // 2
     d_chip = d_chip.astype(BF)
     if fast:
-        d_chip = after(d_chip, d_total)
+        d_chip = after(d_chip, *got)
     mine = lax.dynamic_slice_in_dim(d_chip, core * half, half, 2)
     other = swap(lax.dynamic_slice_in_dim(d_chip, (1 - core) * half, half, 2), "shard", 1)
     if fast:

time: 599 us -> 557 us (0.930)
  Pallas kernels: 169 us -> 150 us
  local copies, waits for them, and re-layouts: 40.8 us -> 27.2 us
  starting transfers between devices: 77.2 us -> 70.3 us
    pallas_call x10, Pallas kernels: 169 us -> 150 us  [call(): pl.pallas_call(kernel, grid_spec=pltpu.PrefetchScalarGridSpec(num_scalar_...]
    unnamed x166 -> x97, local copies, waits for them, and re-layouts: 16.2 us -> 3.77 us
    ppermute x78 -> x75, starting transfers between devices: 77.2 us -> 70.3 us  [swap(): return lax.ppermute(value, axis, [(i, i ^ distance) for i in range(count)])]
    ppermute x78 -> x75, waiting for transfers between devices: 228 us -> 225 us  [swap(): return lax.ppermute(value, axis, [(i, i ^ distance) for i in range(count)])]
    convert_element_type x14 -> x12, other arithmetic: 14.3 us -> 15.1 us  [add_low(): return total.astype(BF)]
  transfers between devices with their start and end apart: 78 -> 75, of which waited for: 32 -> 37; matrix products, arithmetic and copies ran while one was open for 15% -> 15% of each run, Pallas kernels for 20% -> 17%
where the time goes in v3:
time: 557 us; the launch traced here: 549 us
  waiting for transfers between devices  225 us (40%)
  Pallas kernels  150 us (27%)
  other arithmetic  73.5 us (13%)
  starting transfers between devices  70.3 us (13%)
  local copies, waits for them, and re-layouts  27.2 us (5%)
    ppermute x75, waiting for transfers between devices, swap(): return lax.ppermute(value, axis, [(i, i ^ distance) for i in range(count)])  225 us
    pallas_call x10, Pallas kernels, call(): pl.pallas_call(kernel, grid_spec=pltpu.PrefetchScalarGridSpec(num_scalar_...  150 us
    ppermute x75, starting transfers between devices, swap(): return lax.ppermute(value, axis, [(i, i ^ distance) for i in range(count)])  70.3 us
    convert_element_type x12, other arithmetic, add_low(): return total.astype(BF)  15.1 us
  transfers between devices with their start and end apart: 75, of which 37 were waited for; matrix products, arithmetic and copies ran while one was open for 15% of the time, Pallas kernels for 17%

profile of v3, /device:TPU:0, one launch (start us, length us, event | category | flops | bytes accessed | tf_op | source)
XLA Modules:
  0.0 548.8 jit_solution(10915933917259749632)
XLA Ops:
  35.7 7.2 %collective-permute-done.7 = bf16[64,1664]{1,0:T(8,128)(2,1)S(1)} collective-permute-done((bf16[64,1664]{1,0:T(8,128)(2,1)}, bf16[64,1664]{1,0:T(8,128)(2,1)S(1)}, u32[]{:S(2)}, u32[]{:S(2)}) %collective-permute-start.7) | collective-permute-done | bytes 213024 | tf_op jit(solution)/shard_map/ppermute | solution.py:919
  47.8 13.5 %collective-permute-done.3 = bf16[256,1024]{1,0:T(8,128)(2,1)S(1)} collective-permute-done((bf16[256,1024]{1,0:T(8,128)(2,1)}, bf16[256,1024]{1,0:T(8,128)(2,1)S(1)}, u32[]{:S(2)}, u32[]{:S(2)}) %collective-permute-start.3) | collective-permute-done | bytes 524320 | tf_op jit(solution)/shard_map/ppermute | solution.py:919
  64.4 19.0 %collective-permute-done.4 = bf16[256,1024]{1,0:T(8,128)(2,1)S(1)} collective-permute-done((bf16[256,1024]{1,0:T(8,128)(2,1)S(1)}, bf16[256,1024]{1,0:T(8,128)(2,1)S(1)}, u32[]{:S(2)}, u32[]{:S(2)}) %collective-permute-start.4) | collective-permute-done | bytes 524320 | tf_op jit(solution)/shard_map/ppermute | solution.py:919
  108.5 14.4 %shard_map.229 = (bf16[256,1024]{1,0:T(8,128)(2,1)}, bf16[2048,512]{1,0:T(8,128)(2,1)}, bf16[2048,512]{1,0:T(8,128)(2,1)}) custom-call(s32[4]{0:T(128)} %pad_add_fusion.ids.refs_0_, bf16[1024,1024]{1,0:T(8,128)(2,1)} %bitcast.14.own_ref.own_rows, bf16[1024,1024]{1,0:T(8,128)(2,1)} %bitcast.15.other_ref.other_rows, f32[1,1024]{1,0:T(1,128)} %bitcast.242, ...), custom_call_target="tpu_custom_call" | custom-call | tf_op jit(solution)/shard_map/pallas_call | solution.py:40
  134.8 16.8 %shard_map.230 = (f32[256,1024]{1,0:T(8,128)}, bf16[256,1024]{1,0:T(8,128)(2,1)}, f32[4,256,128]{2,1,0:T(8,128)}) custom-call(s32[4]{0:T(128)} %pad_add_fusion.ids.refs_0_, bf16[256,1024]{1,0:T(8,128)(2,1)} %get-tuple-element.162.q_ref.refs_1_, bf16[2048,512]{1,0:T(8,128)(2,1)} %get-tuple-element.163.k_ref.refs_5_, ...), custom_call_target="tpu_custom_call" | custom-call | tf_op jit(solution)/shard_map/pallas_call | solution.py:40
  151.6 4.7 shard_map.231
  156.3 4.8 collective-permute-done.20.rest_12_
  169.2 12.3 %collective-permute-done.25.rest_14_ = bf16[2,1,256,512]{3,2,1,0:T(8,128)(2,1)S(1)} collective-permute-done((bf16[2,1,256,512]{3,2,1,0:T(8,128)(2,1)}, bf16[2,1,256,512]{3,2,1,0:T(8,128)(2,1)S(1)}, u32[]{:S(2)}, u32[]{:S(2)}) %collective-permute-start.25) | collective-permute-done | bytes 524320 | tf_op jit(solution)/shard_map/ppermute | solution.py:919
  181.5 6.7 %collective-permute-done.27 = bf16[256,1024]{1,0:T(8,128)(2,1)S(1)} collective-permute-done((bf16[256,1024]{1,0:T(8,128)(2,1)}, bf16[256,1024]{1,0:T(8,128)(2,1)S(1)}, u32[]{:S(2)}, u32[]{:S(2)}) %collective-permute-start.27) | collective-permute-done | bytes 524320 | tf_op jit(solution)/shard_map/ppermute | solution.py:919
  200.9 15.9 %collective-permute-done.29.rest_13_ = bf16[2,1,256,512]{3,2,1,0:T(8,128)(2,1)S(1)} collective-permute-done((bf16[2,1,256,512]{3,2,1,0:T(8,128)(2,1)}, bf16[2,1,256,512]{3,2,1,0:T(8,128)(2,1)S(1)}, u32[]{:S(2)}, u32[]{:S(2)}) %collective-permute-start.29) | collective-permute-done | bytes 524320 | tf_op jit(solution)/shard_map/ppermute | solution.py:919
  227.5 7.2 %collective-permute-done.38.rest_16_ = bf16[2,1,256,512]{3,2,1,0:T(8,128)(2,1)S(1)} collective-permute-done((bf16[2,1,256,512]{3,2,1,0:T(8,128)(2,1)}, bf16[2,1,256,512]{3,2,1,0:T(8,128)(2,1)S(1)}, u32[]{:S(2)}, u32[]{:S(2)}) %collective-permute-start.38) | collective-permute-done | bytes 524320 | tf_op jit(solution)/shard_map/ppermute | solution.py:919
  235.5 49.9 %shard_map.232 = (bf16[4,256,1024]{2,1,0:T(8,128)(2,1)}, bf16[4,256,1024]{2,1,0:T(8,128)(2,1)}, bf16[4,256,1024]{2,1,0:T(8,128)(2,1)}, bf16[4,256,1024]{2,1,0:T(...) custom-call(s32[4]{0:T(128)} %pad_add_fusion.ids.refs_0_, ...), custom_call_target="tpu_custom_call" | custom-call | tf_op jit(solution)/shard_map/pallas_call | solution.py:40
  297.0 25.5 %collective-permute-done.42 = bf16[2,3,256,512]{3,2,1,0:T(8,128)(2,1)S(1)} collective-permute-done((bf16[2,3,256,512]{3,2,1,0:T(8,128)(2,1)}, bf16[2,3,256,512]{3,2,1,0:T(8,128)(2,1)S(1)}, u32[]{:S(2)}, u32[]{:S(2)}) %collective-permute-start.42) | collective-permute-done | bytes 1572896 | tf_op jit(solution)/shard_map/ppermute | solution.py:919
  330.4 19.6 %collective-permute-done.47 = bf16[256,1024]{1,0:T(8,128)(2,1)S(1)} collective-permute-done((bf16[256,1024]{1,0:T(8,128)(2,1)S(1)}, bf16[256,1024]{1,0:T(8,128)(2,1)S(1)}, u32[]{:S(2)}, u32[]{:S(2)}) %collective-permute-start.47) | collective-permute-done | bytes 524320 | tf_op jit(solution)/shard_map/ppermute | solution.py:919
  355.1 6.8 %shard_map.233 = (f32[256,1024]{1,0:T(8,128)}, bf16[256,1024]{1,0:T(8,128)(2,1)}, bf16[4,144,1024]{2,1,0:T(8,128)(2,1)}, bf16[4,144,1024]{2,1,0:T(8,128)(2,1)}) custom-call(s32[4]{0:T(128)} %pad_add_fusion.ids.refs_0_, f32[256,1024]{1,0:T(8,128)} %bitcast.207, f32[256,1024]{1,0:T(8,128)} %get-tuple-element.166.x2_ref, f32[1,1024]{1,0:T(1,128)} %bitcast.247, ...), custom_call_target="tpu_custom_call" | custom-call | tf_op jit(solution)/shard_map/pallas_call | solution.py:40
  371.8 16.1 %shard_map.234 = (bf16[256,1024]{1,0:T(8,128)(2,1)}, bf16[2,1024,512]{2,1,0:T(8,128)(2,1)}, bf16[2,1024,512]{2,1,0:T(8,128)(2,1)}) custom-call(s32[4]{0:T(128)} %pad_add_fusion.ids.refs_0_, bf16[256,1024]{1,0:T(8,128)(2,1)} %get-tuple-element.162.q_ref.refs_1_, bf16[256,1024]{1,0:T(8,128)(2,1)} %get-tuple-element.242.do_ref.refs_2_, ...), custom_call_target="tpu_custom_call" | custom-call | tf_op jit(solution)/shard_map/pallas_call | solution.py:40
  401.2 9.1 %shard_map.235 = bf16[4,256,1024]{2,1,0:T(8,128)(2,1)} custom-call(s32[4]{0:T(128)} %pad_add_fusion.ids.refs_0_, bf16[1024,1024]{1,0:T(8,128)(2,1)} %bitcast.14.own_ref.own_rows, bf16[1024,1024]{1,0:T(8,128)(2,1)} %bitcast.15.other_ref.other_rows, f32[1,1024]{1,0:T(1,128)} %bitcast.243, bf16[256,1024]{1,0:T(8,128)(2,1)} %get-tuple-element.238.dq_ref.refs_11_, ...), custom_call_target="tpu_custom_call" | custom-call | tf_op jit(solution)/shard_map/pallas_call | solution.py:40
  410.2 15.9 %shard_map.236 = (bf16[256,1024]{1,0:T(8,128)(2,1)}, bf16[2,1024,512]{2,1,0:T(8,128)(2,1)}, bf16[2,1024,512]{2,1,0:T(8,128)(2,1)}) custom-call(s32[4]{0:T(128)} %pad_add_fusion.ids.refs_0_, bf16[256,1024]{1,0:T(8,128)(2,1)} %get-tuple-element.162.q_ref.refs_1_, ...), custom_call_target="tpu_custom_call", output_to_operand_aliasing={{0}: (11, {}), {1}: (12, {}), {2}: (13, {})} | custom-call | tf_op jit(solution)/shard_map/pallas_call | solution.py:40
  426.1 10.6 %collective-permute-done.58 = bf16[416,1024]{1,0:T(8,128)(2,1)} collective-permute-done((bf16[416,1024]{1,0:T(8,128)(2,1)S(1)}, bf16[416,1024]{1,0:T(8,128)(2,1)}, u32[]{:S(2)}, u32[]{:S(2)}) %collective-permute-start.58) | collective-permute-done | bytes 852000 | tf_op jit(solution)/shard_map/ppermute | solution.py:919
  436.7 6.4 %collective-permute-done.56 = bf16[2,2,256,512]{3,2,1,0:T(8,128)(2,1)} collective-permute-done((bf16[2,2,256,512]{3,2,1,0:T(8,128)(2,1)}, bf16[2,2,256,512]{3,2,1,0:T(8,128)(2,1)}, u32[]{:S(2)}, u32[]{:S(2)}) %collective-permute-start.56) | collective-permute-done | bytes 1048608 | tf_op jit(solution)/shard_map/ppermute | solution.py:919
  444.3 9.2 %shard_map.237 = bf16[4,256,1024]{2,1,0:T(8,128)(2,1)} custom-call(s32[4]{0:T(128)} %pad_add_fusion.ids.refs_0_, bf16[1024,1024]{1,0:T(8,128)(2,1)} %bitcast.14.own_ref.own_rows, bf16[1024,1024]{1,0:T(8,128)(2,1)} %bitcast.15.other_ref.other_rows, f32[1,1024]{1,0:T(1,128)} %bitcast.244, bf16[256,1024]{1,0:T(8,128)(2,1)} %get-tuple-element.251.dq_ref, ...), custom_call_target="tpu_custom_call" | custom-call | tf_op jit(solution)/shard_map/pallas_call | solution.py:40
  463.8 20.3 %collective-permute-done.64 = bf16[2,256,512]{2,1,0:T(8,128)(2,1)S(1)} collective-permute-done((bf16[2,256,512]{2,1,0:T(8,128)(2,1)S(1)}, bf16[2,256,512]{2,1,0:T(8,128)(2,1)S(1)}, u32[]{:S(2)}, u32[]{:S(2)}) %collective-permute-start.64) | collective-permute-done | bytes 524320 | tf_op jit(solution)/shard_map/ppermute | solution.py:919
  492.6 16.3 %collective-permute-done.66 = bf16[2,256,512]{2,1,0:T(8,128)(2,1)S(1)} collective-permute-done((bf16[2,256,512]{2,1,0:T(8,128)(2,1)S(1)}, bf16[2,256,512]{2,1,0:T(8,128)(2,1)S(1)}, u32[]{:S(2)}, u32[]{:S(2)}) %collective-permute-start.66) | collective-permute-done | bytes 524320 | tf_op jit(solution)/shard_map/ppermute | solution.py:919
  523.2 7.5 %shard_map.238 = f32[256,1024]{1,0:T(8,128)} custom-call(s32[4]{0:T(128)} %pad_add_fusion.ids.refs_0_, bf16[256,1024]{1,0:T(8,128)(2,1)} %get-tuple-element.251.dq_ref, f32[2,256,512]{2,1,0:T(8,128)} %convert_add_fusion.6.dkv_ref, f32[256,1024]{1,0:T(8,128)} %bitcast.201, f32[256,1024]{1,0:T(8,128)} %get-tuple-element.269.dx2_ref, f32[1,1024]{1,0:T(1,128)} %bitcast.245, ...), custom_call_target="tpu_custom_call" | custom-call | tf_op jit(solution)/shard_map/pallas_call | solution.py:40
  (362 shorter events, 211.4 us)
Async XLA Ops:
  7.5 36.7 %collective-permute-start = (bf16[256,1024]{1,0:T(8,128)(2,1)}, bf16[256,1024]{1,0:T(8,128)(2,1)}, u32[]{:S(2)}, u32[]{:S(2)}) collective-permute-start(bf16[256,1024]{1,0:T(8,128)(2,1)} %multiply_convert_fusion), channel_id=1, source_target_pairs={{0,2},{1,3},{2,0},{3,1},{4,6},{5,7},{6,4},{7,5},{8,10},{9,11},{10,... | collective-permute-start | bytes 1572872 | tf_op jit(solution)/shard_map/ppermute | solution.py:919
  44.2 43.5 %collective-permute-start.12 = (bf16[256,1664]{1,0:T(8,128)(2,1)S(1)}, bf16[256,1664]{1,0:T(8,128)(2,1)S(1)}, u32[]{:S(2)}, u32[]{:S(2)}) collective-permute-start(bf16[256,1664]{1,0:T(8,128)(2,1)S(1)} %get-tuple-element.148), channel_id=1, source_target_pairs={{0,24},{8,16},{16,8},{24,0},{1,25},{9,17},{17,9},{25,1},{2,26},{10... | collective-permute-start | bytes 2555912 | tf_op jit(solution)/shard_map/ppermute | solution.py:919
  46.8 40.9 %collective-permute-start.11 = (bf16[256,1664]{1,0:T(8,128)(2,1)S(1)}, bf16[256,1664]{1,0:T(8,128)(2,1)S(1)}, u32[]{:S(2)}, u32[]{:S(2)}) collective-permute-start(bf16[256,1664]{1,0:T(8,128)(2,1)S(1)} %get-tuple-element.148), channel_id=1, source_target_pairs={{0,16},{8,24},{16,0},{24,8},{1,17},{9,25},{17,1},{25,9},{2,18},{10... | collective-permute-start | bytes 2555912 | tf_op jit(solution)/shard_map/ppermute | solution.py:919
  47.3 40.4 %collective-permute-start.9 = (bf16[256,1664]{1,0:T(8,128)(2,1)S(1)}, bf16[256,1664]{1,0:T(8,128)(2,1)S(1)}, u32[]{:S(2)}, u32[]{:S(2)}) collective-permute-start(bf16[256,1664]{1,0:T(8,128)(2,1)S(1)} %get-tuple-element.148), channel_id=1, source_target_pairs={{0,8},{8,0},{16,24},{24,16},{1,9},{9,1},{17,25},{25,17},{2,10},{10... | collective-permute-start | bytes 2555912 | tf_op jit(solution)/shard_map/ppermute | solution.py:919
  61.3 26.4 %collective-permute-start.10 = (bf16[272,1024]{1,0:T(8,128)(2,1)}, bf16[272,1024]{1,0:T(8,128)(2,1)S(1)}, u32[]{:S(2)}, u32[]{:S(2)}) collective-permute-start(bf16[272,1024]{1,0:T(8,128)(2,1)} %get-tuple-element.161), channel_id=1, source_target_pairs={{0,4},{1,5},{2,6},{3,7},{4,0},{5,1},{6,2},{7,3},{8,12},{9,13},{10,... | collective-permute-start | bytes 1671176 | tf_op jit(solution)/shard_map/ppermute | solution.py:919
  98.1 31.3 %collective-permute-start.18 = (bf16[272,1024]{1,0:T(8,128)(2,1)}, bf16[272,1024]{1,0:T(8,128)(2,1)}, u32[]{:S(2)}, u32[]{:S(2)}) collective-permute-start(bf16[272,1024]{1,0:T(8,128)(2,1)} %get-tuple-element.161), channel_id=1, source_target_pairs={{0,24},{8,16},{16,8},{24,0},{1,25},{9,17},{17,9},{25,1},{2,26},{10... | collective-permute-start | bytes 1671176 | tf_op jit(solution)/shard_map/ppermute | solution.py:919
  100.5 28.8 %collective-permute-start.17 = (bf16[272,1024]{1,0:T(8,128)(2,1)}, bf16[272,1024]{1,0:T(8,128)(2,1)}, u32[]{:S(2)}, u32[]{:S(2)}) collective-permute-start(bf16[272,1024]{1,0:T(8,128)(2,1)} %get-tuple-element.161), channel_id=1, source_target_pairs={{0,16},{8,24},{16,0},{24,8},{1,17},{9,25},{17,1},{25,9},{2,18},{10... | collective-permute-start | bytes 1671176 | tf_op jit(solution)/shard_map/ppermute | solution.py:919
  101.0 28.3 %collective-permute-start.16 = (bf16[272,1024]{1,0:T(8,128)(2,1)}, bf16[272,1024]{1,0:T(8,128)(2,1)}, u32[]{:S(2)}, u32[]{:S(2)}) collective-permute-start(bf16[272,1024]{1,0:T(8,128)(2,1)} %get-tuple-element.161), channel_id=1, source_target_pairs={{0,8},{8,0},{16,24},{24,16},{1,9},{9,1},{17,25},{25,17},{2,10},{10... | collective-permute-start | bytes 1671176 | tf_op jit(solution)/shard_map/ppermute | solution.py:919
  129.4 33.5 %collective-permute-start.19 = (bf16[2,2,256,512]{3,2,1,0:T(8,128)(2,1)S(1)}, bf16[2,2,256,512]{3,2,1,0:T(8,128)(2,1)S(1)}, u32[]{:S(2)}, u32[]{:S(2)}) collective-permute-start(bf16[2,2,256,512]{3,2,1,0:T(8,128)(2,1)S(1)} %slice.257), channel_id=1, source_target_pairs={{0,2},{1,3},{2,0},{3,1},{4,6},{5,7},{6,4},{7,5},{8,10},{9,11},{10,... | collective-permute-start | bytes 3145736 | tf_op jit(solution)/shard_map/ppermute | solution.py:919
  129.4 26.9 %collective-permute-start.23 = (bf16[272,1024]{1,0:T(8,128)(2,1)S(1)}, bf16[272,1024]{1,0:T(8,128)(2,1)S(1)}, u32[]{:S(2)}, u32[]{:S(2)}) collective-permute-start(bf16[272,1024]{1,0:T(8,128)(2,1)S(1)} %copy-done.17), channel_id=1, source_target_pairs={{0,24},{8,16},{16,8},{24,0},{1,25},{9,17},{17,9},{25,1},{2,26},{10... | collective-permute-start | bytes 1671176 | tf_op jit(solution)/shard_map/ppermute | solution.py:919
  133.0 28.1 %collective-permute-start.20 = (bf16[2,1,256,512]{3,2,1,0:T(8,128)(2,1)S(1)}, bf16[2,1,256,512]{3,2,1,0:T(8,128)(2,1)S(1)}, u32[]{:S(2)}, u32[]{:S(2)}) collective-permute-start(bf16[2,1,256,512]{3,2,1,0:T(8,128)(2,1)S(1)} %copy-done.30), channel_id=1, source_target_pairs={{0,4},{1,5},{2,6},{3,7},{4,0},{5,1},{6,2},{7,3},{8,12},{9,13},{10,... | collective-permute-start | bytes 1572872 | tf_op jit(solution)/shard_map/ppermute | solution.py:919
  285.9 36.6 %collective-permute-start.42 = (bf16[2,3,256,512]{3,2,1,0:T(8,128)(2,1)}, bf16[2,3,256,512]{3,2,1,0:T(8,128)(2,1)S(1)}, u32[]{:S(2)}, u32[]{:S(2)}) collective-permute-start(bf16[2,3,256,512]{3,2,1,0:T(8,128)(2,1)} %get-tuple-element.209), channel_id=1, source_target_pairs={{0,2},{1,3},{2,0},{3,1},{4,6},{5,7},{6,4},{7,5},{8,10},{9,11},{10,... | collective-permute-start | bytes 4718600 | tf_op jit(solution)/shard_map/ppermute | solution.py:919
  292.5 30.0 %collective-permute-start.44 = (bf16[256,1024]{1,0:T(8,128)(2,1)S(1)}, bf16[256,1024]{1,0:T(8,128)(2,1)S(1)}, u32[]{:S(2)}, u32[]{:S(2)}) collective-permute-start(bf16[256,1024]{1,0:T(8,128)(2,1)S(1)} %get-tuple-element.312), channel_id=1, source_target_pairs={{0,24},{8,16},{16,8},{24,0},{1,25},{9,17},{17,9},{25,1},{2,26},{10... | collective-permute-start | bytes 1572872 | tf_op jit(solution)/shard_map/ppermute | solution.py:919
  293.8 28.7 %collective-permute-start.43 = (bf16[256,1024]{1,0:T(8,128)(2,1)S(1)}, bf16[256,1024]{1,0:T(8,128)(2,1)S(1)}, u32[]{:S(2)}, u32[]{:S(2)}) collective-permute-start(bf16[256,1024]{1,0:T(8,128)(2,1)S(1)} %get-tuple-element.313), channel_id=1, source_target_pairs={{0,16},{8,24},{16,0},{24,8},{1,17},{9,25},{17,1},{25,9},{2,18},{10... | collective-permute-start | bytes 1572872 | tf_op jit(solution)/shard_map/ppermute | solution.py:919
  295.5 27.0 %collective-permute-start.40 = (bf16[256,1024]{1,0:T(8,128)(2,1)S(1)}, bf16[256,1024]{1,0:T(8,128)(2,1)S(1)}, u32[]{:S(2)}, u32[]{:S(2)}) collective-permute-start(bf16[256,1024]{1,0:T(8,128)(2,1)S(1)} %get-tuple-element.311), channel_id=1, source_target_pairs={{0,8},{8,0},{16,24},{24,16},{1,9},{9,1},{17,25},{25,17},{2,10},{10... | collective-permute-start | bytes 1572872 | tf_op jit(solution)/shard_map/ppermute | solution.py:919
  322.9 27.1 %collective-permute-start.45 = (bf16[8,272,1024]{2,1,0:T(8,128)(2,1)S(1)}, bf16[8,272,1024]{2,1,0:T(8,128)(2,1)S(1)}, u32[]{:S(2)}, u32[]{:S(2)}) collective-permute-start(bf16[8,272,1024]{2,1,0:T(8,128)(2,1)S(1)} %copy-done.41), channel_id=1, source_target_pairs={{0,1},{1,0},{2,3},{3,2},{4,5},{5,4},{6,7},{7,6},{8,9},{9,8},{10,11... | collective-permute-start | bytes 13369352 | tf_op jit(solution)/shard_map/ppermute | solution.py:919
  364.2 27.0 %collective-permute-start.52 = (bf16[272,1024]{1,0:T(8,128)(2,1)}, bf16[272,1024]{1,0:T(8,128)(2,1)}, u32[]{:S(2)}, u32[]{:S(2)}) collective-permute-start(bf16[272,1024]{1,0:T(8,128)(2,1)} %get-tuple-element.234), channel_id=1, source_target_pairs={{0,16},{8,24},{16,0},{24,8},{1,17},{9,25},{17,1},{25,9},{2,18},{10... | collective-permute-start | bytes 1671176 | tf_op jit(solution)/shard_map/ppermute | solution.py:919
  395.2 47.8 %collective-permute-start.56 = (bf16[2,2,256,512]{3,2,1,0:T(8,128)(2,1)}, bf16[2,2,256,512]{3,2,1,0:T(8,128)(2,1)}, u32[]{:S(2)}, u32[]{:S(2)}) collective-permute-start(bf16[2,2,256,512]{3,2,1,0:T(8,128)(2,1)} %slice.279), channel_id=1, source_target_pairs={{0,4},{1,5},{2,6},{3,7},{4,0},{5,1},{6,2},{7,3},{8,12},{9,13},{10,... | collective-permute-start | bytes 3145736 | tf_op jit(solution)/shard_map/ppermute | solution.py:919
  396.3 47.4 %collective-permute-start.57 = (bf16[2,2,256,512]{3,2,1,0:T(8,128)(2,1)}, bf16[2,2,256,512]{3,2,1,0:T(8,128)(2,1)}, u32[]{:S(2)}, u32[]{:S(2)}) collective-permute-start(bf16[2,2,256,512]{3,2,1,0:T(8,128)(2,1)} %slice.220), channel_id=1, source_target_pairs={{0,2},{1,3},{2,0},{3,1},{4,6},{5,7},{6,4},{7,5},{8,10},{9,11},{10,... | collective-permute-start | bytes 3145736 | tf_op jit(solution)/shard_map/ppermute | solution.py:919
  397.6 28.5 %collective-permute-start.60 = (bf16[416,1024]{1,0:T(8,128)(2,1)S(1)}, bf16[416,1024]{1,0:T(8,128)(2,1)}, u32[]{:S(2)}, u32[]{:S(2)}) collective-permute-start(bf16[416,1024]{1,0:T(8,128)(2,1)S(1)} %get-tuple-element.294), channel_id=1, source_target_pairs={{0,24},{8,16},{16,8},{24,0},{1,25},{9,17},{17,9},{25,1},{2,26},{10... | collective-permute-start | bytes 2555912 | tf_op jit(solution)/shard_map/ppermute | solution.py:919
  399.0 37.7 %collective-permute-start.58 = (bf16[416,1024]{1,0:T(8,128)(2,1)S(1)}, bf16[416,1024]{1,0:T(8,128)(2,1)}, u32[]{:S(2)}, u32[]{:S(2)}) collective-permute-start(bf16[416,1024]{1,0:T(8,128)(2,1)S(1)} %get-tuple-element.295), channel_id=1, source_target_pairs={{0,8},{8,0},{16,24},{24,16},{1,9},{9,1},{17,25},{25,17},{2,10},{10... | collective-permute-start | bytes 2555912 | tf_op jit(solution)/shard_map/ppermute | solution.py:919
  400.7 36.0 %collective-permute-start.59 = (bf16[416,1024]{1,0:T(8,128)(2,1)S(1)}, bf16[416,1024]{1,0:T(8,128)(2,1)}, u32[]{:S(2)}, u32[]{:S(2)}) collective-permute-start(bf16[416,1024]{1,0:T(8,128)(2,1)S(1)} %get-tuple-element.296), channel_id=1, source_target_pairs={{0,16},{8,24},{16,0},{24,8},{1,17},{9,25},{17,1},{25,9},{2,18},{10... | collective-permute-start | bytes 2555912 | tf_op jit(solution)/shard_map/ppermute | solution.py:919
  453.5 30.8 %collective-permute-start.63 = (bf16[272,1024]{1,0:T(8,128)(2,1)}, bf16[272,1024]{1,0:T(8,128)(2,1)S(1)}, u32[]{:S(2)}, u32[]{:S(2)}) collective-permute-start(bf16[272,1024]{1,0:T(8,128)(2,1)} %fusion.6), channel_id=1, source_target_pairs={{0,4},{1,5},{2,6},{3,7},{4,0},{5,1},{6,2},{7,3},{8,12},{9,13},{10,... | collective-permute-start | bytes 1671176 | tf_op jit(solution)/shard_map/ppermute | solution.py:919
  517.0 26.6 %collective-permute-start.74 = (bf16[4,3,128,512]{3,2,1,0:T(8,128)(2,1)}, bf16[4,3,128,512]{3,2,1,0:T(8,128)(2,1)}, u32[]{:S(2)}, u32[]{:S(2)}) collective-permute-start(bf16[4,3,128,512]{3,2,1,0:T(8,128)(2,1)} %get-tuple-element.298), channel_id=1, source_target_pairs={{0,1},{1,0},{2,3},{3,2},{4,5},{5,4},{6,7},{7,6},{8,9},{9,8},{10,11... | collective-permute-start | bytes 4718600 | tf_op jit(solution)/shard_map/ppermute | solution.py:919
  (95 other events, 1450.2 us)

commit v4 on v3

--- a/solution.py
+++ b/solution.py
@@ -2,6 +2,7 @@
 
 import jax
 import jax.numpy as jnp
+import numpy as np
 from jax import lax
 from jax.experimental import pallas as pl
 from jax.experimental.pallas import tpu as pltpu
@@ -95,15 +96,32 @@
     return on, on + qn, on + qn + kn, on + qn + 2 * kn
 
 
-def qkv_kernel(nr, nh, ids, own_ref, other_ref, gain_ref, cos_ref, sin_ref, *rest):
+def frequencies():
+    return np.tile(10000.0 ** (-np.arange(HD // 2) * 2.0 / HD), 2 * LANES // HD)
+
+
+def place_tables(length):
+    angles = np.arange(length)[:, None] * frequencies()[None, :]
+    return np.cos(angles).astype(np.float32), np.sin(angles).astype(np.float32)
+
+
+def qkv_kernel(nr, nh, ids, own_ref, other_ref, gain_ref, cos_ref, sin_ref, slot_cos, slot_sin, *rest):
     weights = rest[:nh]
-    q_ref, k_ref, v_ref, normed_ref = rest[nh:]
+    q_ref, k_ref, v_ref, cos_out, sin_out, normed_ref = rest[nh:]
     width = own_ref.shape[-1]
     chunk = width // nr
     qn, kn = H * HD // nh, KVH * HD // nh
     at_q, at_k, _, at_end = columns(nh, width)
     normalize(own_ref, other_ref, gain_ref, normed_ref)
-    cosine, sine = cos_ref[...], sin_ref[...]
+    length = cos_ref.shape[0]
+    sign = jnp.where(lane_ids(length) % HD < HD // 2, -1.0, 1.0)
+    for b in range(cos_out.shape[0] // length):
+        slot = pl.ds(pl.program_id(0) * (cos_out.shape[0] // length) + b, 1)
+        c, s = slot_cos[slot], slot_sin[slot]
+        at = slice(b * length, (b + 1) * length)
+        cos_out[at] = cos_ref[...] * c - sin_ref[...] * s
+        sin_out[at] = sign * (sin_ref[...] * c + cos_ref[...] * s)
+    cosine, sine = cos_out[...], sin_out[...]
     for h in range(nh):
         total = None
         for r in range(nr):
@@ -153,27 +171,33 @@
     slots, (length, width) = 2 * rows[0].shape[0], rows[0].shape[1:]
     nr, nh = weights[0].shape[0], len(weights)
     tile, steps = BLOCKS * length, slots // BLOCKS
+    tables = [jnp.asarray(t) for t in place_tables(length)]
     return call(
         functools.partial(qkv_kernel, nr, nh),
         (steps,),
         ids,
-        [*flat_rows(rows), gain, cosine, sine, *weights],
+        [*flat_rows(rows), gain, *tables, cosine, sine, *weights],
         [
             *rows_specs(steps, (tile, width)),
             whole_spec(gain.shape),
-            pl.BlockSpec((tile, LANES), lambda i, _: (i, 0)),
-            pl.BlockSpec((tile, LANES), lambda i, _: (i, 0)),
+            *[whole_spec(t.shape) for t in tables],
+            whole_spec(cosine.shape),
+            whole_spec(sine.shape),
             *[whole_spec(w.shape) for w in weights],
         ],
         [
             jax.ShapeDtypeStruct((length, H * HD), BF),
             jax.ShapeDtypeStruct((slots * length, KVH * HD), BF),
             jax.ShapeDtypeStruct((slots * length, KVH * HD), BF),
+            jax.ShapeDtypeStruct((slots * length, LANES), F32),
+            jax.ShapeDtypeStruct((slots * length, LANES), F32),
         ],
         [
             whole_spec((length, H * HD)),
             pl.BlockSpec((tile, KVH * HD), lambda i, _: (i, 0)),
             pl.BlockSpec((tile, KVH * HD), lambda i, _: (i, 0)),
+            pl.BlockSpec((tile, LANES), lambda i, _: (i, 0)),
+            pl.BlockSpec((tile, LANES), lambda i, _: (i, 0)),
         ],
         [pltpu.VMEM((tile, width), BF)],
     )
@@ -679,7 +703,7 @@
     for g in range(groups):
         c_copy(g).wait()
         n2_copy(g).wait()
-        lax.fori_loop(g * per, (g + 1) * per, gather, 0)
+        lax.fori_loop(g * per, (g + 1) * per, gather, 0, unroll=True)
     for n in range(len(w_parts)):
         w_copy(n).wait()
 
@@ -757,7 +781,7 @@
         )
 
     for g in range(groups):
-        lax.fori_loop(g * per, (g + 1) * per, spread, 0)
+        lax.fori_loop(g * per, (g + 1) * per, spread, 0, unroll=True)
         dn2_copy(g).start()
         y_copy(g).start()
     for g in range(groups):
@@ -787,7 +811,7 @@
     outs += [jax.ShapeDtypeStruct((groups // 2 * per, high, width), BF)] * 2
     outs += [jax.ShapeDtypeStruct(matrices, BF)] * nz
     got = call(
-        functools.partial(mixture_kernel, nz, tuple(w_parts), groups, per, experts, 256),
+        functools.partial(mixture_kernel, nz, tuple(w_parts), groups, per, experts, 640),
         (1,),
         ids,
         [slots, gates, *n2_groups, *c_groups, *flat],
@@ -1016,12 +1040,8 @@
     def positions(start):
         s_late = after(s, start)
         owners = jnp.stack([s_late ^ (2 * r + k) for k in range(2) for r in range(chips)])
-        places = (owners[:, None] * length + jnp.arange(length)[None, :]).reshape(n_shard * length)
-        freqs = 10000.0 ** (-(jnp.arange(HD // 2, dtype=F32) * 2.0 / HD))
-        angles = places.astype(F32)[:, None] * freqs[None, :]
+        angles = (owners * length).astype(F32)[:, None] * jnp.asarray(frequencies(), F32)[None, :]
         cosine, sine = jnp.cos(angles), jnp.sin(angles)
-        cosine = jnp.concatenate([cosine] * 4, axis=1)
-        sine = jnp.concatenate([-sine, sine] * 2, axis=1)
         every = block_ids[0].reshape(n_shard, length)
         key_blocks = jnp.concatenate(
             [pick(every, s_late ^ (2 * r + k)) for k in range(2) for r in range(chips)]
@@ -1057,14 +1077,14 @@
 
     if fast:
         w_near, w_far = swap(chip, "shard", 2), swap(chip, "shard", 4)
-        x_near = swap(scaled_rows, "shard", 2)
-        x_far = swap(after(scaled_rows, w_far), "shard", 4)
         stacked = jnp.stack([chip, w_near, w_far, swap(w_far, "shard", 2)])
         block = jnp.concatenate([pick(stacked, z ^ i) for i in range(chips)], axis=0)
         c_pack = cotangent_rows(chip)
         w_mine, w_other = own_experts(chip)
         cosine, sine, key_extra, query_extra = positions(chip)
-        w_got = over_columns(after(block, x_near, w_other))
+        w_got = over_columns(after(block, w_other))
+        x_late = after(scaled_rows, block)
+        x_near, x_far = swap(x_late, "shard", 2), swap(x_late, "shard", 4)
         x_cross = swap(x_far, "shard", 2)
         c_far = swap(after(c_pack, x_far), "shard", 4)
         chip_w = in_order(after(w_mine, x_cross), w_other, core, 2)
@@ -1077,11 +1097,18 @@
         early = (own_core, c_far, cosine, sine, key_extra, query_extra)
         w_got = [after(got, *early) for got in w_got]
         blocks = jnp.stack([block] + w_got)
-        attn_w = [blocks, swap(blocks, "shard", 1)]
         gain_cols = blocks[:, :, at_end:]
         gain_cols = jnp.concatenate([pick(gain_cols, e ^ i) for i in range(n_expert)], axis=0)
-        near_a = swap(after(here[:, :1], blocks), "shard", 2)
-        far_a = swap(after(there[0], blocks), "shard", 4)
+        attn_other, near_a, far_a, gain_one, gain_two, ids = together(
+            swap(blocks, "shard", 1),
+            here[:, :1],
+            there[0],
+            gain_cols[:, 0].astype(F32)[None],
+            gain_cols[:, LANES // 2].astype(F32)[None],
+            ids,
+        )
+        attn_w = [blocks, attn_other]
+        near_a, far_a = swap(near_a, "shard", 2), swap(far_a, "shard", 4)
         c_own_got = over_columns(after(c_pack, attn_w[1]))
     else:
         c_pack = cotangent_rows(packed)
@@ -1092,11 +1119,11 @@
         attn_w = [blocks[None]]
         gain_cols = blocks[:, at_end:]
         expert_w = gather_z(in_order(*own_experts(packed), core, 2))
-    gain_one = gain_cols[:, 0].astype(F32)[None]
-    gain_two = gain_cols[:, LANES // 2].astype(F32)[None]
+        gain_one = gain_cols[:, 0].astype(F32)[None]
+        gain_two = gain_cols[:, LANES // 2].astype(F32)[None]
     nr = attn_w[0].shape[0]
 
-    q, k, v = project(ids, rows, gain_one, cosine, sine, attn_w)
+    q, k, v, cosine, sine = project(ids, rows, gain_one, cosine, sine, attn_w)
     if fast:
         c_far_got = over_columns(after(c_far, q))
         q, near_a, far_a, *c_own_got = together(q, near_a, far_a, *c_own_got)

time: 557 us -> 549 us (0.986)
  other arithmetic: 73.5 us -> 63.8 us
  starting transfers between devices: 70.3 us -> 78.6 us
    ppermute x75, starting transfers between devices: 70.3 us -> 78.6 us  [swap(): return lax.ppermute(value, axis, [(i, i ^ distance) for i in range(count)])]
  transfers between devices with their start and end apart: 75 -> 75, of which waited for: 37 -> 34; matrix products, arithmetic and copies ran while one was open for 15% -> 13% of each run, Pallas kernels for 17% -> 17%
where the time goes in v4:
time: 549 us; the launch traced here: 544 us
  waiting for transfers between devices  224 us (41%)
  Pallas kernels  146 us (27%)
  starting transfers between devices  78.6 us (14%)
  other arithmetic  63.8 us (12%)
  local copies, waits for them, and re-layouts  29.6 us (5%)
    ppermute x75, waiting for transfers between devices, swap(): return lax.ppermute(value, axis, [(i, i ^ distance) for i in range(count)])  224 us
    pallas_call x10, Pallas kernels, call(): pl.pallas_call(kernel, grid_spec=pltpu.PrefetchScalarGridSpec(num_scalar_...  146 us
    ppermute x75, starting transfers between devices, swap(): return lax.ppermute(value, axis, [(i, i ^ distance) for i in range(count)])  78.6 us
    convert_element_type x12, other arithmetic, add_low(): return total.astype(BF)  15.1 us
  transfers between devices with their start and end apart: 75, of which 34 were waited for; matrix products, arithmetic and copies ran while one was open for 13% of the time, Pallas kernels for 17%

profile of v4, /device:TPU:0, one launch (start us, length us, event | category | flops | bytes accessed | tf_op | source)
XLA Modules:
  0.0 544.3 jit_solution(4172348460835113968)
XLA Ops:
  26.3 5.8 %collective-permute-done.3 = bf16[64,1664]{1,0:T(8,128)(2,1)S(1)} collective-permute-done((bf16[64,1664]{1,0:T(8,128)(2,1)}, bf16[64,1664]{1,0:T(8,128)(2,1)S(1)}, u32[]{:S(2)}, u32[]{:S(2)}) %collective-permute-start.3) | collective-permute-done | bytes 213024 | tf_op jit(solution)/shard_map/ppermute | solution.py:943
  42.9 17.0 %collective-permute-done.7 = bf16[256,1024]{1,0:T(8,128)(2,1)S(1)} collective-permute-done((bf16[256,1024]{1,0:T(8,128)(2,1)S(1)}, bf16[256,1024]{1,0:T(8,128)(2,1)S(1)}, u32[]{:S(2)}, u32[]{:S(2)}) %collective-permute-start.7) | collective-permute-done | bytes 524320 | tf_op jit(solution)/shard_map/ppermute | solution.py:943
  65.1 18.6 %collective-permute-done.8 = bf16[256,1024]{1,0:T(8,128)(2,1)S(1)} collective-permute-done((bf16[256,1024]{1,0:T(8,128)(2,1)S(1)}, bf16[256,1024]{1,0:T(8,128)(2,1)S(1)}, u32[]{:S(2)}, u32[]{:S(2)}) %collective-permute-start.8) | collective-permute-done | bytes 524320 | tf_op jit(solution)/shard_map/ppermute | solution.py:943
  105.3 14.6 %shard_map.256 = (bf16[256,1024]{1,0:T(8,128)(2,1)}, bf16[2048,512]{1,0:T(8,128)(2,1)}, bf16[2048,512]{1,0:T(8,128)(2,1)}, f32[2048,128]{1,0:T(8,128)}, f32[2048,128]{1,0:T(8,128)}) custom-call(s32[4]{0:T(128)} %pad_add_fusion.ids.refs_0_, bf16[1024,1024]{1,0:T(8,128)(2,1)} %bitcast.58.own_ref.own_rows, bf16[1024,1024]{1,0:T(8,128)(2,1)} %bitcast.59.other_ref.other_rows, ...), custom_call_target="tpu_custom_call" | custom-call | tf_op jit(solution)/shard_map/pallas_call | solution.py:41
  119.9 6.7 %collective-permute-done.14.rest_9_ = bf16[2,1,256,512]{3,2,1,0:T(8,128)(2,1)S(1)} collective-permute-done((bf16[2,1,256,512]{3,2,1,0:T(8,128)(2,1)}, bf16[2,1,256,512]{3,2,1,0:T(8,128)(2,1)S(1)}, u32[]{:S(2)}, u32[]{:S(2)}) %collective-permute-start.14) | collective-permute-done | bytes 524320 | tf_op jit(solution)/shard_map/ppermute | solution.py:943
  134.3 16.8 %shard_map.257 = (f32[256,1024]{1,0:T(8,128)}, bf16[256,1024]{1,0:T(8,128)(2,1)}, f32[4,256,128]{2,1,0:T(8,128)}) custom-call(s32[4]{0:T(128)} %pad_add_fusion.ids.refs_0_, bf16[256,1024]{1,0:T(8,128)(2,1)} %get-tuple-element.171.q_ref.refs_1_, bf16[2048,512]{1,0:T(8,128)(2,1)} %get-tuple-element.172.k_ref.refs_5_, ...), custom_call_target="tpu_custom_call" | custom-call | tf_op jit(solution)/shard_map/pallas_call | solution.py:41
  155.9 4.8 collective-permute-done.20.rest_12_
  169.0 12.6 %collective-permute-done.25.rest_14_ = bf16[2,1,256,512]{3,2,1,0:T(8,128)(2,1)S(1)} collective-permute-done((bf16[2,1,256,512]{3,2,1,0:T(8,128)(2,1)S(1)}, bf16[2,1,256,512]{3,2,1,0:T(8,128)(2,1)S(1)}, u32[]{:S(2)}, u32[]{:S(2)}) %collective-permute-start.25) | collective-permute-done | bytes 524320 | tf_op jit(solution)/shard_map/ppermute | solution.py:943
  181.6 6.0 %collective-permute-done.27 = bf16[256,1024]{1,0:T(8,128)(2,1)S(1)} collective-permute-done((bf16[256,1024]{1,0:T(8,128)(2,1)}, bf16[256,1024]{1,0:T(8,128)(2,1)S(1)}, u32[]{:S(2)}, u32[]{:S(2)}) %collective-permute-start.27) | collective-permute-done | bytes 524320 | tf_op jit(solution)/shard_map/ppermute | solution.py:943
  200.4 16.1 %collective-permute-done.29.rest_13_ = bf16[2,1,256,512]{3,2,1,0:T(8,128)(2,1)S(1)} collective-permute-done((bf16[2,1,256,512]{3,2,1,0:T(8,128)(2,1)}, bf16[2,1,256,512]{3,2,1,0:T(8,128)(2,1)S(1)}, u32[]{:S(2)}, u32[]{:S(2)}) %collective-permute-start.29) | collective-permute-done | bytes 524320 | tf_op jit(solution)/shard_map/ppermute | solution.py:943
  228.6 6.2 %collective-permute-done.38.rest_16_ = bf16[2,1,256,512]{3,2,1,0:T(8,128)(2,1)S(1)} collective-permute-done((bf16[2,1,256,512]{3,2,1,0:T(8,128)(2,1)S(1)}, bf16[2,1,256,512]{3,2,1,0:T(8,128)(2,1)S(1)}, u32[]{:S(2)}, u32[]{:S(2)}) %collective-permute-start.38) | collective-permute-done | bytes 524320 | tf_op jit(solution)/shard_map/ppermute | solution.py:943
  235.6 45.4 %shard_map.259 = (bf16[4,256,1024]{2,1,0:T(8,128)(2,1)}, bf16[4,256,1024]{2,1,0:T(8,128)(2,1)}, bf16[4,256,1024]{2,1,0:T(8,128)(2,1)}, bf16[4,256,1024]{2,1,0:T(...) custom-call(s32[4]{0:T(128)} %pad_add_fusion.ids.refs_0_, ...), custom_call_target="tpu_custom_call" | custom-call | tf_op jit(solution)/shard_map/pallas_call | solution.py:41
  292.7 25.5 %collective-permute-done.42 = bf16[2,3,256,512]{3,2,1,0:T(8,128)(2,1)S(1)} collective-permute-done((bf16[2,3,256,512]{3,2,1,0:T(8,128)(2,1)}, bf16[2,3,256,512]{3,2,1,0:T(8,128)(2,1)S(1)}, u32[]{:S(2)}, u32[]{:S(2)}) %collective-permute-start.42) | collective-permute-done | bytes 1572896 | tf_op jit(solution)/shard_map/ppermute | solution.py:943
  325.9 19.7 %collective-permute-done.47 = bf16[256,1024]{1,0:T(8,128)(2,1)S(1)} collective-permute-done((bf16[256,1024]{1,0:T(8,128)(2,1)S(1)}, bf16[256,1024]{1,0:T(8,128)(2,1)S(1)}, u32[]{:S(2)}, u32[]{:S(2)}) %collective-permute-start.47) | collective-permute-done | bytes 524320 | tf_op jit(solution)/shard_map/ppermute | solution.py:943
  350.6 6.9 %shard_map.260 = (f32[256,1024]{1,0:T(8,128)}, bf16[256,1024]{1,0:T(8,128)(2,1)}, bf16[4,144,1024]{2,1,0:T(8,128)(2,1)}, bf16[4,144,1024]{2,1,0:T(8,128)(2,1)}) custom-call(s32[4]{0:T(128)} %pad_add_fusion.ids.refs_0_, f32[256,1024]{1,0:T(8,128)} %bitcast.204, f32[256,1024]{1,0:T(8,128)} %get-tuple-element.176.x2_ref, f32[1,1024]{1,0:T(1,128)} %bitcast.249, ...), custom_call_target="tpu_custom_call" | custom-call | tf_op jit(solution)/shard_map/pallas_call | solution.py:41
  367.5 15.7 %shard_map.261 = (bf16[256,1024]{1,0:T(8,128)(2,1)}, bf16[2,1024,512]{2,1,0:T(8,128)(2,1)}, bf16[2,1024,512]{2,1,0:T(8,128)(2,1)}) custom-call(s32[4]{0:T(128)} %pad_add_fusion.ids.refs_0_, bf16[256,1024]{1,0:T(8,128)(2,1)} %get-tuple-element.171.q_ref.refs_1_, bf16[256,1024]{1,0:T(8,128)(2,1)} %get-tuple-element.254.do_ref.refs_2_, ...), custom_call_target="tpu_custom_call" | custom-call | tf_op jit(solution)/shard_map/pallas_call | solution.py:41
  396.9 9.1 %shard_map.262 = bf16[4,256,1024]{2,1,0:T(8,128)(2,1)} custom-call(s32[4]{0:T(128)} %pad_add_fusion.ids.refs_0_, bf16[1024,1024]{1,0:T(8,128)(2,1)} %bitcast.58.own_ref.own_rows, bf16[1024,1024]{1,0:T(8,128)(2,1)} %bitcast.59.other_ref.other_rows, f32[1,1024]{1,0:T(1,128)} %bitcast.245, bf16[256,1024]{1,0:T(8,128)(2,1)} %get-tuple-element.250.dq_ref.refs_11_, ...), custom_call_target="tpu_custom_call" | custom-call | tf_op jit(solution)/shard_map/pallas_call | solution.py:41
  406.0 15.9 %shard_map.263 = (bf16[256,1024]{1,0:T(8,128)(2,1)}, bf16[2,1024,512]{2,1,0:T(8,128)(2,1)}, bf16[2,1024,512]{2,1,0:T(8,128)(2,1)}) custom-call(s32[4]{0:T(128)} %pad_add_fusion.ids.refs_0_, bf16[256,1024]{1,0:T(8,128)(2,1)} %get-tuple-element.171.q_ref.refs_1_, ...), custom_call_target="tpu_custom_call", output_to_operand_aliasing={{0}: (11, {}), {1}: (12, {}), {2}: (13, {})} | custom-call | tf_op jit(solution)/shard_map/pallas_call | solution.py:41
  421.9 10.6 %collective-permute-done.58 = bf16[416,1024]{1,0:T(8,128)(2,1)} collective-permute-done((bf16[416,1024]{1,0:T(8,128)(2,1)S(1)}, bf16[416,1024]{1,0:T(8,128)(2,1)}, u32[]{:S(2)}, u32[]{:S(2)}) %collective-permute-start.58) | collective-permute-done | bytes 852000 | tf_op jit(solution)/shard_map/ppermute | solution.py:943
  432.5 5.8 %collective-permute-done.56 = bf16[2,2,256,512]{3,2,1,0:T(8,128)(2,1)} collective-permute-done((bf16[2,2,256,512]{3,2,1,0:T(8,128)(2,1)}, bf16[2,2,256,512]{3,2,1,0:T(8,128)(2,1)}, u32[]{:S(2)}, u32[]{:S(2)}) %collective-permute-start.56) | collective-permute-done | bytes 1048608 | tf_op jit(solution)/shard_map/ppermute | solution.py:943
  438.8 9.3 %shard_map.264 = bf16[4,256,1024]{2,1,0:T(8,128)(2,1)} custom-call(s32[4]{0:T(128)} %pad_add_fusion.ids.refs_0_, bf16[1024,1024]{1,0:T(8,128)(2,1)} %bitcast.58.own_ref.own_rows, bf16[1024,1024]{1,0:T(8,128)(2,1)} %bitcast.59.other_ref.other_rows, f32[1,1024]{1,0:T(1,128)} %bitcast.246, bf16[256,1024]{1,0:T(8,128)(2,1)} %get-tuple-element.263.dq_ref, ...), custom_call_target="tpu_custom_call" | custom-call | tf_op jit(solution)/shard_map/pallas_call | solution.py:41
  459.6 19.4 %collective-permute-done.64 = bf16[2,256,512]{2,1,0:T(8,128)(2,1)S(1)} collective-permute-done((bf16[2,256,512]{2,1,0:T(8,128)(2,1)S(1)}, bf16[2,256,512]{2,1,0:T(8,128)(2,1)S(1)}, u32[]{:S(2)}, u32[]{:S(2)}) %collective-permute-start.64) | collective-permute-done | bytes 524320 | tf_op jit(solution)/shard_map/ppermute | solution.py:943
  488.1 16.1 %collective-permute-done.66 = bf16[2,256,512]{2,1,0:T(8,128)(2,1)S(1)} collective-permute-done((bf16[2,256,512]{2,1,0:T(8,128)(2,1)S(1)}, bf16[2,256,512]{2,1,0:T(8,128)(2,1)S(1)}, u32[]{:S(2)}, u32[]{:S(2)}) %collective-permute-start.66) | collective-permute-done | bytes 524320 | tf_op jit(solution)/shard_map/ppermute | solution.py:943
  518.2 7.5 %shard_map.265 = f32[256,1024]{1,0:T(8,128)} custom-call(s32[4]{0:T(128)} %pad_add_fusion.ids.refs_0_, bf16[256,1024]{1,0:T(8,128)(2,1)} %get-tuple-element.263.dq_ref, f32[2,256,512]{2,1,0:T(8,128)} %convert_add_fusion.6.dkv_ref, f32[256,1024]{1,0:T(8,128)} %bitcast.198, f32[256,1024]{1,0:T(8,128)} %get-tuple-element.281.dx2_ref, f32[1,1024]{1,0:T(1,128)} %bitcast.247, ...), custom_call_target="tpu_custom_call" | custom-call | tf_op jit(solution)/shard_map/pallas_call | solution.py:41
  (385 shorter events, 210.3 us)
Async XLA Ops:
  39.4 49.0 %collective-permute-start.11 = (bf16[256,1664]{1,0:T(8,128)(2,1)S(1)}, bf16[256,1664]{1,0:T(8,128)(2,1)S(1)}, u32[]{:S(2)}, u32[]{:S(2)}) collective-permute-start(bf16[256,1664]{1,0:T(8,128)(2,1)S(1)} %get-tuple-element.153), channel_id=1, source_target_pairs={{0,24},{8,16},{16,8},{24,0},{1,25},{9,17},{17,9},{25,1},{2,26},{10... | collective-permute-start | bytes 2555912 | tf_op jit(solution)/shard_map/ppermute | solution.py:943
  41.8 46.5 %collective-permute-start.10 = (bf16[256,1664]{1,0:T(8,128)(2,1)S(1)}, bf16[256,1664]{1,0:T(8,128)(2,1)S(1)}, u32[]{:S(2)}, u32[]{:S(2)}) collective-permute-start(bf16[256,1664]{1,0:T(8,128)(2,1)S(1)} %get-tuple-element.153), channel_id=1, source_target_pairs={{0,16},{8,24},{16,0},{24,8},{1,17},{9,25},{17,1},{25,9},{2,18},{10... | collective-permute-start | bytes 2555912 | tf_op jit(solution)/shard_map/ppermute | solution.py:943
  42.4 46.0 %collective-permute-start.5 = (bf16[256,1664]{1,0:T(8,128)(2,1)S(1)}, bf16[256,1664]{1,0:T(8,128)(2,1)S(1)}, u32[]{:S(2)}, u32[]{:S(2)}) collective-permute-start(bf16[256,1664]{1,0:T(8,128)(2,1)S(1)} %get-tuple-element.153), channel_id=1, source_target_pairs={{0,8},{8,0},{16,24},{24,16},{1,9},{9,1},{17,25},{25,17},{2,10},{10... | collective-permute-start | bytes 2555912 | tf_op jit(solution)/shard_map/ppermute | solution.py:943
  60.5 27.9 %collective-permute-start.9 = (bf16[272,1024]{1,0:T(8,128)(2,1)S(1)}, bf16[272,1024]{1,0:T(8,128)(2,1)S(1)}, u32[]{:S(2)}, u32[]{:S(2)}) collective-permute-start(bf16[272,1024]{1,0:T(8,128)(2,1)S(1)} %get-tuple-element.170), channel_id=1, source_target_pairs={{0,4},{1,5},{2,6},{3,7},{4,0},{5,1},{6,2},{7,3},{8,12},{9,13},{10,... | collective-permute-start | bytes 1671176 | tf_op jit(solution)/shard_map/ppermute | solution.py:943
  98.8 29.0 %collective-permute-start.18 = (bf16[272,1024]{1,0:T(8,128)(2,1)S(1)}, bf16[272,1024]{1,0:T(8,128)(2,1)S(1)}, u32[]{:S(2)}, u32[]{:S(2)}) collective-permute-start(bf16[272,1024]{1,0:T(8,128)(2,1)S(1)} %copy-done.26), channel_id=1, source_target_pairs={{0,24},{8,16},{16,8},{24,0},{1,25},{9,17},{17,9},{25,1},{2,26},{10... | collective-permute-start | bytes 1671176 | tf_op jit(solution)/shard_map/ppermute | solution.py:943
  101.2 26.6 %collective-permute-start.17 = (bf16[272,1024]{1,0:T(8,128)(2,1)S(1)}, bf16[272,1024]{1,0:T(8,128)(2,1)S(1)}, u32[]{:S(2)}, u32[]{:S(2)}) collective-permute-start(bf16[272,1024]{1,0:T(8,128)(2,1)S(1)} %copy-done.26), channel_id=1, source_target_pairs={{0,16},{8,24},{16,0},{24,8},{1,17},{9,25},{17,1},{25,9},{2,18},{10... | collective-permute-start | bytes 1671176 | tf_op jit(solution)/shard_map/ppermute | solution.py:943
  127.8 34.9 %collective-permute-start.19 = (bf16[2,2,256,512]{3,2,1,0:T(8,128)(2,1)S(1)}, bf16[2,2,256,512]{3,2,1,0:T(8,128)(2,1)S(1)}, u32[]{:S(2)}, u32[]{:S(2)}) collective-permute-start(bf16[2,2,256,512]{3,2,1,0:T(8,128)(2,1)S(1)} %slice.257), channel_id=1, source_target_pairs={{0,2},{1,3},{2,0},{3,1},{4,6},{5,7},{6,4},{7,5},{8,10},{9,11},{10,... | collective-permute-start | bytes 3145736 | tf_op jit(solution)/shard_map/ppermute | solution.py:943
  128.2 27.6 %collective-permute-start.23 = (bf16[272,1024]{1,0:T(8,128)(2,1)S(1)}, bf16[272,1024]{1,0:T(8,128)(2,1)S(1)}, u32[]{:S(2)}, u32[]{:S(2)}) collective-permute-start(bf16[272,1024]{1,0:T(8,128)(2,1)S(1)} %copy-done.20), channel_id=1, source_target_pairs={{0,24},{8,16},{16,8},{24,0},{1,25},{9,17},{17,9},{25,1},{2,26},{10... | collective-permute-start | bytes 1671176 | tf_op jit(solution)/shard_map/ppermute | solution.py:943
  131.7 28.9 %collective-permute-start.20 = (bf16[2,1,256,512]{3,2,1,0:T(8,128)(2,1)S(1)}, bf16[2,1,256,512]{3,2,1,0:T(8,128)(2,1)}, u32[]{:S(2)}, u32[]{:S(2)}) collective-permute-start(bf16[2,1,256,512]{3,2,1,0:T(8,128)(2,1)S(1)} %copy-done.42), channel_id=1, source_target_pairs={{0,4},{1,5},{2,6},{3,7},{4,0},{5,1},{6,2},{7,3},{8,12},{9,13},{10,... | collective-permute-start | bytes 1572872 | tf_op jit(solution)/shard_map/ppermute | solution.py:943
  190.3 26.2 %collective-permute-start.33 = (bf16[256,1024]{1,0:T(8,128)(2,1)S(1)}, bf16[256,1024]{1,0:T(8,128)(2,1)S(1)}, u32[]{:S(2)}, u32[]{:S(2)}) collective-permute-start(bf16[256,1024]{1,0:T(8,128)(2,1)S(1)} %collective-permute-done.24), channel_id=1, source_target_pairs={{0,24},{8,16},{16,8},{24,0},{1,25},{9,17},{17,9},{25,1},{2,26},{10... | collective-permute-start | bytes 1572872 | tf_op jit(solution)/shard_map/ppermute | solution.py:943
  281.6 36.6 %collective-permute-start.42 = (bf16[2,3,256,512]{3,2,1,0:T(8,128)(2,1)}, bf16[2,3,256,512]{3,2,1,0:T(8,128)(2,1)S(1)}, u32[]{:S(2)}, u32[]{:S(2)}) collective-permute-start(bf16[2,3,256,512]{3,2,1,0:T(8,128)(2,1)} %get-tuple-element.219), channel_id=1, source_target_pairs={{0,2},{1,3},{2,0},{3,1},{4,6},{5,7},{6,4},{7,5},{8,10},{9,11},{10,... | collective-permute-start | bytes 4718600 | tf_op jit(solution)/shard_map/ppermute | solution.py:943
  288.1 30.0 %collective-permute-start.44 = (bf16[256,1024]{1,0:T(8,128)(2,1)S(1)}, bf16[256,1024]{1,0:T(8,128)(2,1)S(1)}, u32[]{:S(2)}, u32[]{:S(2)}) collective-permute-start(bf16[256,1024]{1,0:T(8,128)(2,1)S(1)} %get-tuple-element.324), channel_id=1, source_target_pairs={{0,24},{8,16},{16,8},{24,0},{1,25},{9,17},{17,9},{25,1},{2,26},{10... | collective-permute-start | bytes 1572872 | tf_op jit(solution)/shard_map/ppermute | solution.py:943
  289.6 28.6 %collective-permute-start.43 = (bf16[256,1024]{1,0:T(8,128)(2,1)S(1)}, bf16[256,1024]{1,0:T(8,128)(2,1)S(1)}, u32[]{:S(2)}, u32[]{:S(2)}) collective-permute-start(bf16[256,1024]{1,0:T(8,128)(2,1)S(1)} %get-tuple-element.325), channel_id=1, source_target_pairs={{0,16},{8,24},{16,0},{24,8},{1,17},{9,25},{17,1},{25,9},{2,18},{10... | collective-permute-start | bytes 1572872 | tf_op jit(solution)/shard_map/ppermute | solution.py:943
  291.1 27.0 %collective-permute-start.40 = (bf16[256,1024]{1,0:T(8,128)(2,1)S(1)}, bf16[256,1024]{1,0:T(8,128)(2,1)S(1)}, u32[]{:S(2)}, u32[]{:S(2)}) collective-permute-start(bf16[256,1024]{1,0:T(8,128)(2,1)S(1)} %get-tuple-element.323), channel_id=1, source_target_pairs={{0,8},{8,0},{16,24},{24,16},{1,9},{9,1},{17,25},{25,17},{2,10},{10... | collective-permute-start | bytes 1572872 | tf_op jit(solution)/shard_map/ppermute | solution.py:943
  318.6 27.1 %collective-permute-start.45 = (bf16[8,272,1024]{2,1,0:T(8,128)(2,1)S(1)}, bf16[8,272,1024]{2,1,0:T(8,128)(2,1)S(1)}, u32[]{:S(2)}, u32[]{:S(2)}) collective-permute-start(bf16[8,272,1024]{2,1,0:T(8,128)(2,1)S(1)} %copy-done.55), channel_id=1, source_target_pairs={{0,1},{1,0},{2,3},{3,2},{4,5},{5,4},{6,7},{7,6},{8,9},{9,8},{10,11... | collective-permute-start | bytes 13369352 | tf_op jit(solution)/shard_map/ppermute | solution.py:943
  319.5 26.2 %collective-permute-start.47 = (bf16[256,1024]{1,0:T(8,128)(2,1)S(1)}, bf16[256,1024]{1,0:T(8,128)(2,1)S(1)}, u32[]{:S(2)}, u32[]{:S(2)}) collective-permute-start(bf16[256,1024]{1,0:T(8,128)(2,1)S(1)} %fusion.16), channel_id=1, source_target_pairs={{0,4},{1,5},{2,6},{3,7},{4,0},{5,1},{6,2},{7,3},{8,12},{9,13},{10,... | collective-permute-start | bytes 1572872 | tf_op jit(solution)/shard_map/ppermute | solution.py:943
  360.0 26.8 %collective-permute-start.52 = (bf16[272,1024]{1,0:T(8,128)(2,1)}, bf16[272,1024]{1,0:T(8,128)(2,1)}, u32[]{:S(2)}, u32[]{:S(2)}) collective-permute-start(bf16[272,1024]{1,0:T(8,128)(2,1)} %get-tuple-element.246), channel_id=1, source_target_pairs={{0,16},{8,24},{16,0},{24,8},{1,17},{9,25},{17,1},{25,9},{2,18},{10... | collective-permute-start | bytes 1671176 | tf_op jit(solution)/shard_map/ppermute | solution.py:943
  390.1 48.1 %collective-permute-start.56 = (bf16[2,2,256,512]{3,2,1,0:T(8,128)(2,1)}, bf16[2,2,256,512]{3,2,1,0:T(8,128)(2,1)}, u32[]{:S(2)}, u32[]{:S(2)}) collective-permute-start(bf16[2,2,256,512]{3,2,1,0:T(8,128)(2,1)} %slice.279), channel_id=1, source_target_pairs={{0,4},{1,5},{2,6},{3,7},{4,0},{5,1},{6,2},{7,3},{8,12},{9,13},{10,... | collective-permute-start | bytes 3145736 | tf_op jit(solution)/shard_map/ppermute | solution.py:943
  392.0 46.2 %collective-permute-start.57 = (bf16[2,2,256,512]{3,2,1,0:T(8,128)(2,1)}, bf16[2,2,256,512]{3,2,1,0:T(8,128)(2,1)}, u32[]{:S(2)}, u32[]{:S(2)}) collective-permute-start(bf16[2,2,256,512]{3,2,1,0:T(8,128)(2,1)} %slice.220), channel_id=1, source_target_pairs={{0,2},{1,3},{2,0},{3,1},{4,6},{5,7},{6,4},{7,5},{8,10},{9,11},{10,... | collective-permute-start | bytes 3145736 | tf_op jit(solution)/shard_map/ppermute | solution.py:943
  393.3 28.5 %collective-permute-start.60 = (bf16[416,1024]{1,0:T(8,128)(2,1)S(1)}, bf16[416,1024]{1,0:T(8,128)(2,1)}, u32[]{:S(2)}, u32[]{:S(2)}) collective-permute-start(bf16[416,1024]{1,0:T(8,128)(2,1)S(1)} %get-tuple-element.306), channel_id=1, source_target_pairs={{0,24},{8,16},{16,8},{24,0},{1,25},{9,17},{17,9},{25,1},{2,26},{10... | collective-permute-start | bytes 2555912 | tf_op jit(solution)/shard_map/ppermute | solution.py:943
  394.8 37.7 %collective-permute-start.58 = (bf16[416,1024]{1,0:T(8,128)(2,1)S(1)}, bf16[416,1024]{1,0:T(8,128)(2,1)}, u32[]{:S(2)}, u32[]{:S(2)}) collective-permute-start(bf16[416,1024]{1,0:T(8,128)(2,1)S(1)} %get-tuple-element.307), channel_id=1, source_target_pairs={{0,8},{8,0},{16,24},{24,16},{1,9},{9,1},{17,25},{25,17},{2,10},{10... | collective-permute-start | bytes 2555912 | tf_op jit(solution)/shard_map/ppermute | solution.py:943
  396.4 36.1 %collective-permute-start.59 = (bf16[416,1024]{1,0:T(8,128)(2,1)S(1)}, bf16[416,1024]{1,0:T(8,128)(2,1)}, u32[]{:S(2)}, u32[]{:S(2)}) collective-permute-start(bf16[416,1024]{1,0:T(8,128)(2,1)S(1)} %get-tuple-element.308), channel_id=1, source_target_pairs={{0,16},{8,24},{16,0},{24,8},{1,17},{9,25},{17,1},{25,9},{2,18},{10... | collective-permute-start | bytes 2555912 | tf_op jit(solution)/shard_map/ppermute | solution.py:943
  448.1 31.1 %collective-permute-start.63 = (bf16[272,1024]{1,0:T(8,128)(2,1)}, bf16[272,1024]{1,0:T(8,128)(2,1)S(1)}, u32[]{:S(2)}, u32[]{:S(2)}) collective-permute-start(bf16[272,1024]{1,0:T(8,128)(2,1)} %fusion.6), channel_id=1, source_target_pairs={{0,4},{1,5},{2,6},{3,7},{4,0},{5,1},{6,2},{7,3},{8,12},{9,13},{10,... | collective-permute-start | bytes 1671176 | tf_op jit(solution)/shard_map/ppermute | solution.py:943
  512.5 26.5 %collective-permute-start.74 = (bf16[4,3,128,512]{3,2,1,0:T(8,128)(2,1)}, bf16[4,3,128,512]{3,2,1,0:T(8,128)(2,1)}, u32[]{:S(2)}, u32[]{:S(2)}) collective-permute-start(bf16[4,3,128,512]{3,2,1,0:T(8,128)(2,1)} %get-tuple-element.310), channel_id=1, source_target_pairs={{0,1},{1,0},{2,3},{3,2},{4,5},{5,4},{6,7},{7,6},{8,9},{9,8},{10,11... | collective-permute-start | bytes 4718600 | tf_op jit(solution)/shard_map/ppermute | solution.py:943
  (109 other events, 1663.5 us)

commit v5 on v4

--- a/solution.py
+++ b/solution.py
@@ -983,6 +983,15 @@
     for value in values[1:]:
         total = total + value.astype(F32)
     return total.astype(BF)
+
+
+def sum_start(blocks, first):
+    return swap(jnp.stack([blocks[first], blocks[3]]), "expert", first)
+
+
+def sum_next(blocks, got, first):
+    mine = blocks[0].astype(F32) + got[0].astype(F32)
+    return mine, swap(add_low(blocks[3 - first], got[1]), "expert", 3 - first)
 
 
 def body(
@@ -1210,40 +1219,45 @@
     if fast:
         d_out_sums = add_low(d_out_w[0], swap(d_out_w[1], "shard", 1))
         far_a, near_a = swap(far_early, "shard", 4), swap(near_early, "shard", 2)
-        y_got = [swap(after(y_sum[1, r], dn2), "expert", r) for r in range(1, n_expert)]
+        y_sum = after(y_sum, dn2)
+        got_a, got_b = sum_start(y_sum[1], 1), sum_start(y_sum[0], 2)
         done = attend_back(ids, q, after(d_mixed, d_out_sums), *args, 1)
-        y_across = add_low(y_sum[1, 0], *[after(g, done[0]) for g in y_got])
-        dq = after(done[0], y_across, far_a, near_a)
+        dq, far_a, near_a, got_a, got_b, *done = together(done[0], far_a, near_a, got_a, got_b, *done)
         far_b = swap(after(d_far[:, 1:], dq), "shard", 4)
         near_b = swap(after(d_experts[1][:, 1:], dq), "shard", 2)
-        both = jnp.concatenate([y_sum[0], after(d_out_sums, dq)], axis=1)
-        both_got = [swap(both[r], "expert", r) for r in range(1, n_expert)]
+        y_across, got_a = sum_next(y_sum[1], got_a, 1)
+        y_out, got_b = sum_next(y_sum[0], got_b, 2)
+        got_c = sum_start(after(d_out_sums, dq), 1)
         d_other = half_grads(ids, rows, gain_one, dq, done[1:], 1, nr, nh)
         dq, *dkv = attend_back(ids, q, after(d_mixed, d_other), *args, 0, done)
-        dq, far_b, near_b, *parts = together(dq, far_b, near_b, *dkv, *both_got)
-        dkv, both_got = parts[:2], parts[2:]
+        dq, far_b, near_b, got_a, got_b, got_c, *dkv = together(
+            dq, far_b, near_b, got_a, got_b, got_c, *dkv
+        )
+        y_across = (y_across + got_a.astype(F32)).astype(BF)
+        y_far = swap(y_across, "shard", 4)
         d_other = swap(after(d_other, dq), "shard", 1)
-        y_far = swap(after(y_across, dq), "shard", 4)
+        d_out_total, got_c = sum_next(d_out_sums, got_c, 1)
     else:
         dq, *dkv = attend_back(ids, q, d_mixed, *args)
         y_got = [swap(y_sum[0, r], "expert", r) for r in range(1, n_expert)]
     dkv_core = swap(dkv[1], "shard", 1)
+    dkv_sums = add_low(dkv[0], dkv_core)
+    if fast:
+        dq = after(dq, dkv_sums, y_across)
     d_own = half_grads(ids, rows, gain_one, dq, dkv, 0, nr, nh)
     if fast:
-        d_own, d_other, dkv_core = together(d_own, d_other, dkv_core)
-    dkv_sums = add_low(dkv[0], dkv_core)
+        d_own, d_other, got_c = together(d_own, d_other, got_c)
     dkv_parts = [dkv_sums[:, r * length : (r + 1) * length] for r in range(chips)]
     if fast:
         sums = add_low(d_own, d_other)
         dkv_step = swap(dkv_parts[3], "shard", 2)
         dkv_far = add_low(dkv_parts[2], dkv_step)
-        sums, y_far, dkv_far = together(sums, y_far, dkv_far)
         got = [swap(sums[r], "expert", r) for r in range(1, n_expert)]
-        dkv_far = swap(dkv_far, "shard", 4)
-        dkv_near = swap(after(dkv_parts[1], dkv_step), "shard", 2)
-        dkv_near, dkv_far, *got = together(dkv_near, dkv_far, *got)
-        both = sum([g.astype(F32) for g in both_got], both[0].astype(F32))
-        y_out, d_out_total = both[: y_sum.shape[2]], both[y_sum.shape[2] :].astype(BF)
+        dkv_far, y_far = together(dkv_far, y_far)
+        got = [after(g, dkv_far) for g in got]
+        dkv_far, dkv_near = swap(dkv_far, "shard", 4), swap(after(dkv_parts[1], dkv_far), "shard", 2)
+        d_out_total = (d_out_total + got_c.astype(F32)).astype(BF)
+        y_out = y_out + got_b.astype(F32)
         cols = width // nh
         high = d_out_total.shape[0] - GATE_ROWS
         gain_grad = d_out_total[high, : width // n_expert]
@@ -1252,12 +1266,13 @@
         )
         gain_grad = jnp.broadcast_to(gain_grad[:, None], (gain_grad.shape[0], LANES))
         d_out_total = jnp.concatenate([d_out_total, gain_grad], axis=1)
-        dkv_own = sum([g.astype(F32) for g in (dkv_near, dkv_far)], dkv_parts[0].astype(F32))
         d_total = add_low(sums[0], *got)
         total = jnp.concatenate([d_out_total, d_total], axis=1)
         total = total.reshape(chips, total.shape[0] // chips, total.shape[1])
         total = [pick(total, z ^ r) for r in range(chips)]
         step, near = swap(total[3], "shard", 2), swap(total[1], "shard", 2)
+        dkv_far, dkv_near, step, near = together(dkv_far, dkv_near, step, near)
+        dkv_own = sum([g.astype(F32) for g in (dkv_near, dkv_far)], dkv_parts[0].astype(F32))
         far = swap(add_low(total[2], step), "shard", 4)
         token_grad = rows_back(ids, dq, dkv_own, x, dx2, gain_one, attn_w)
         summed = total[0].astype(F32) + near.astype(F32) + after(far, token_grad).astype(F32)

time: 549 us -> 545 us (level)
    convert_element_type x12 -> x13, other arithmetic: 15.1 us -> 15.8 us  [add_low(): return total.astype(BF)]
  transfers between devices with their start and end apart: 75 -> 75, of which waited for: 34 -> 32; matrix products, arithmetic and copies ran while one was open for 13% -> 14% of each run, Pallas kernels for 17% -> 17%
where the time goes in v5:
time: 545 us; the launch traced here: 540 us
  waiting for transfers between devices  221 us (41%)
  Pallas kernels  146 us (27%)
  starting transfers between devices  77.8 us (14%)
  other arithmetic  68.1 us (12%)
  local copies, waits for them, and re-layouts  24.8 us (5%)
    ppermute x75, waiting for transfers between devices, swap(): return lax.ppermute(value, axis, [(i, i ^ distance) for i in range(count)])  221 us
    pallas_call x10, Pallas kernels, call(): pl.pallas_call(kernel, grid_spec=pltpu.PrefetchScalarGridSpec(num_scalar_...  146 us
    ppermute x75, starting transfers between devices, swap(): return lax.ppermute(value, axis, [(i, i ^ distance) for i in range(count)])  77.8 us
    convert_element_type x13, other arithmetic, add_low(): return total.astype(BF)  15.8 us
  transfers between devices with their start and end apart: 75, of which 32 were waited for; matrix products, arithmetic and copies ran while one was open for 14% of the time, Pallas kernels for 17%

profile of v5, /device:TPU:0, one launch (start us, length us, event | category | flops | bytes accessed | tf_op | source)
XLA Modules:
  0.0 540.0 jit_solution(5248064564427382368)
XLA Ops:
  26.3 5.8 %collective-permute-done.3 = bf16[64,1664]{1,0:T(8,128)(2,1)S(1)} collective-permute-done((bf16[64,1664]{1,0:T(8,128)(2,1)}, bf16[64,1664]{1,0:T(8,128)(2,1)S(1)}, u32[]{:S(2)}, u32[]{:S(2)}) %collective-permute-start.3) | collective-permute-done | bytes 213024 | tf_op jit(solution)/shard_map/ppermute | solution.py:943
  42.9 17.0 %collective-permute-done.7 = bf16[256,1024]{1,0:T(8,128)(2,1)S(1)} collective-permute-done((bf16[256,1024]{1,0:T(8,128)(2,1)S(1)}, bf16[256,1024]{1,0:T(8,128)(2,1)S(1)}, u32[]{:S(2)}, u32[]{:S(2)}) %collective-permute-start.7) | collective-permute-done | bytes 524320 | tf_op jit(solution)/shard_map/ppermute | solution.py:943
  65.1 18.6 %collective-permute-done.8 = bf16[256,1024]{1,0:T(8,128)(2,1)S(1)} collective-permute-done((bf16[256,1024]{1,0:T(8,128)(2,1)S(1)}, bf16[256,1024]{1,0:T(8,128)(2,1)S(1)}, u32[]{:S(2)}, u32[]{:S(2)}) %collective-permute-start.8) | collective-permute-done | bytes 524320 | tf_op jit(solution)/shard_map/ppermute | solution.py:943
  105.3 14.6 %shard_map.256 = (bf16[256,1024]{1,0:T(8,128)(2,1)}, bf16[2048,512]{1,0:T(8,128)(2,1)}, bf16[2048,512]{1,0:T(8,128)(2,1)}, f32[2048,128]{1,0:T(8,128)}, f32[2048,128]{1,0:T(8,128)}) custom-call(s32[4]{0:T(128)} %pad_add_fusion.ids.refs_0_, bf16[1024,1024]{1,0:T(8,128)(2,1)} %bitcast.58.own_ref.own_rows, bf16[1024,1024]{1,0:T(8,128)(2,1)} %bitcast.59.other_ref.other_rows, ...), custom_call_target="tpu_custom_call" | custom-call | tf_op jit(solution)/shard_map/pallas_call | solution.py:41
  119.9 6.7 %collective-permute-done.14.rest_9_ = bf16[2,1,256,512]{3,2,1,0:T(8,128)(2,1)S(1)} collective-permute-done((bf16[2,1,256,512]{3,2,1,0:T(8,128)(2,1)}, bf16[2,1,256,512]{3,2,1,0:T(8,128)(2,1)S(1)}, u32[]{:S(2)}, u32[]{:S(2)}) %collective-permute-start.14) | collective-permute-done | bytes 524320 | tf_op jit(solution)/shard_map/ppermute | solution.py:943
  134.3 16.7 %shard_map.257 = (f32[256,1024]{1,0:T(8,128)}, bf16[256,1024]{1,0:T(8,128)(2,1)}, f32[4,256,128]{2,1,0:T(8,128)}) custom-call(s32[4]{0:T(128)} %pad_add_fusion.ids.refs_0_, bf16[256,1024]{1,0:T(8,128)(2,1)} %get-tuple-element.174.q_ref.refs_1_, bf16[2048,512]{1,0:T(8,128)(2,1)} %get-tuple-element.175.k_ref.refs_5_, ...), custom_call_target="tpu_custom_call" | custom-call | tf_op jit(solution)/shard_map/pallas_call | solution.py:41
  155.9 4.8 collective-permute-done.20.rest_12_
  169.0 12.6 %collective-permute-done.25.rest_14_ = bf16[2,1,256,512]{3,2,1,0:T(8,128)(2,1)S(1)} collective-permute-done((bf16[2,1,256,512]{3,2,1,0:T(8,128)(2,1)S(1)}, bf16[2,1,256,512]{3,2,1,0:T(8,128)(2,1)S(1)}, u32[]{:S(2)}, u32[]{:S(2)}) %collective-permute-start.25) | collective-permute-done | bytes 524320 | tf_op jit(solution)/shard_map/ppermute | solution.py:943
  181.6 6.0 %collective-permute-done.27 = bf16[256,1024]{1,0:T(8,128)(2,1)S(1)} collective-permute-done((bf16[256,1024]{1,0:T(8,128)(2,1)}, bf16[256,1024]{1,0:T(8,128)(2,1)S(1)}, u32[]{:S(2)}, u32[]{:S(2)}) %collective-permute-start.27) | collective-permute-done | bytes 524320 | tf_op jit(solution)/shard_map/ppermute | solution.py:943
  200.4 16.1 %collective-permute-done.29.rest_13_ = bf16[2,1,256,512]{3,2,1,0:T(8,128)(2,1)S(1)} collective-permute-done((bf16[2,1,256,512]{3,2,1,0:T(8,128)(2,1)}, bf16[2,1,256,512]{3,2,1,0:T(8,128)(2,1)S(1)}, u32[]{:S(2)}, u32[]{:S(2)}) %collective-permute-start.29) | collective-permute-done | bytes 524320 | tf_op jit(solution)/shard_map/ppermute | solution.py:943
  227.2 7.2 %collective-permute-done.38.rest_16_ = bf16[2,1,256,512]{3,2,1,0:T(8,128)(2,1)S(1)} collective-permute-done((bf16[2,1,256,512]{3,2,1,0:T(8,128)(2,1)}, bf16[2,1,256,512]{3,2,1,0:T(8,128)(2,1)S(1)}, u32[]{:S(2)}, u32[]{:S(2)}) %collective-permute-start.38) | collective-permute-done | bytes 524320 | tf_op jit(solution)/shard_map/ppermute | solution.py:943
  235.1 45.4 %shard_map.259 = (bf16[4,256,1024]{2,1,0:T(8,128)(2,1)}, bf16[4,256,1024]{2,1,0:T(8,128)(2,1)}, bf16[4,256,1024]{2,1,0:T(8,128)(2,1)}, bf16[4,256,1024]{2,1,0:T(...) custom-call(s32[4]{0:T(128)} %pad_add_fusion.ids.refs_0_, ...), custom_call_target="tpu_custom_call" | custom-call | tf_op jit(solution)/shard_map/pallas_call | solution.py:41
  292.2 25.5 %collective-permute-done.42 = bf16[2,3,256,512]{3,2,1,0:T(8,128)(2,1)S(1)} collective-permute-done((bf16[2,3,256,512]{3,2,1,0:T(8,128)(2,1)}, bf16[2,3,256,512]{3,2,1,0:T(8,128)(2,1)S(1)}, u32[]{:S(2)}, u32[]{:S(2)}) %collective-permute-start.42) | collective-permute-done | bytes 1572896 | tf_op jit(solution)/shard_map/ppermute | solution.py:943
  325.8 19.6 %collective-permute-done.47 = bf16[256,1024]{1,0:T(8,128)(2,1)S(1)} collective-permute-done((bf16[256,1024]{1,0:T(8,128)(2,1)S(1)}, bf16[256,1024]{1,0:T(8,128)(2,1)S(1)}, u32[]{:S(2)}, u32[]{:S(2)}) %collective-permute-start.47) | collective-permute-done | bytes 524320 | tf_op jit(solution)/shard_map/ppermute | solution.py:943
  350.4 6.9 %shard_map.260 = (f32[256,1024]{1,0:T(8,128)}, bf16[256,1024]{1,0:T(8,128)(2,1)}, bf16[4,144,1024]{2,1,0:T(8,128)(2,1)}, bf16[4,144,1024]{2,1,0:T(8,128)(2,1)}) custom-call(s32[4]{0:T(128)} %pad_add_fusion.ids.refs_0_, f32[256,1024]{1,0:T(8,128)} %bitcast.223, f32[256,1024]{1,0:T(8,128)} %get-tuple-element.179.x2_ref, f32[1,1024]{1,0:T(1,128)} %bitcast.268, ...), custom_call_target="tpu_custom_call" | custom-call | tf_op jit(solution)/shard_map/pallas_call | solution.py:41
  367.2 15.7 %shard_map.261 = (bf16[256,1024]{1,0:T(8,128)(2,1)}, bf16[2,1024,512]{2,1,0:T(8,128)(2,1)}, bf16[2,1024,512]{2,1,0:T(8,128)(2,1)}) custom-call(s32[4]{0:T(128)} %pad_add_fusion.ids.refs_0_, bf16[256,1024]{1,0:T(8,128)(2,1)} %get-tuple-element.174.q_ref.refs_1_, bf16[256,1024]{1,0:T(8,128)(2,1)} %get-tuple-element.254.do_ref.refs_2_, ...), custom_call_target="tpu_custom_call" | custom-call | tf_op jit(solution)/shard_map/pallas_call | solution.py:41
  382.9 5.2 collective-permute-done.51
  397.7 9.1 %shard_map.262 = bf16[4,256,1024]{2,1,0:T(8,128)(2,1)} custom-call(s32[4]{0:T(128)} %pad_add_fusion.ids.refs_0_, bf16[1024,1024]{1,0:T(8,128)(2,1)} %bitcast.58.own_ref.own_rows, bf16[1024,1024]{1,0:T(8,128)(2,1)} %bitcast.59.other_ref.other_rows, f32[1,1024]{1,0:T(1,128)} %bitcast.264, bf16[256,1024]{1,0:T(8,128)(2,1)} %get-tuple-element.255.dq_ref.refs_11_, ...), custom_call_target="tpu_custom_call" | custom-call | tf_op jit(solution)/shard_map/pallas_call | solution.py:41
  406.8 15.9 %shard_map.263 = (bf16[256,1024]{1,0:T(8,128)(2,1)}, bf16[2,1024,512]{2,1,0:T(8,128)(2,1)}, bf16[2,1024,512]{2,1,0:T(8,128)(2,1)}) custom-call(s32[4]{0:T(128)} %pad_add_fusion.ids.refs_0_, bf16[256,1024]{1,0:T(8,128)(2,1)} %get-tuple-element.174.q_ref.refs_1_, ...), custom_call_target="tpu_custom_call", output_to_operand_aliasing={{0}: (11, {}), {1}: (12, {}), {2}: (13, {})} | custom-call | tf_op jit(solution)/shard_map/pallas_call | solution.py:41
  422.8 13.6 %collective-permute-done.55 = bf16[2,2,256,512]{3,2,1,0:T(8,128)(2,1)S(1)} collective-permute-done((bf16[2,2,256,512]{3,2,1,0:T(8,128)(2,1)}, bf16[2,2,256,512]{3,2,1,0:T(8,128)(2,1)S(1)}, u32[]{:S(2)}, u32[]{:S(2)}) %collective-permute-start.55) | collective-permute-done | bytes 1048608 | tf_op jit(solution)/shard_map/ppermute | solution.py:943
  447.9 9.3 %shard_map.264 = bf16[4,256,1024]{2,1,0:T(8,128)(2,1)} custom-call(s32[4]{0:T(128)} %pad_add_fusion.ids.refs_0_, bf16[1024,1024]{1,0:T(8,128)(2,1)} %bitcast.58.own_ref.own_rows, bf16[1024,1024]{1,0:T(8,128)(2,1)} %bitcast.59.other_ref.other_rows, f32[1,1024]{1,0:T(1,128)} %bitcast.265, bf16[256,1024]{1,0:T(8,128)(2,1)} %get-tuple-element.270.dq_ref, ...), custom_call_target="tpu_custom_call" | custom-call | tf_op jit(solution)/shard_map/pallas_call | solution.py:41
  466.3 13.5 %collective-permute-done.61 = bf16[2,256,512]{2,1,0:T(8,128)(2,1)S(1)} collective-permute-done((bf16[2,256,512]{2,1,0:T(8,128)(2,1)S(1)}, bf16[2,256,512]{2,1,0:T(8,128)(2,1)S(1)}, u32[]{:S(2)}, u32[]{:S(2)}) %collective-permute-start.61) | collective-permute-done | bytes 524320 | tf_op jit(solution)/shard_map/ppermute | solution.py:943
  492.7 18.4 %collective-permute-done.71 = bf16[64,1664]{1,0:T(8,128)(2,1)S(1)} collective-permute-done((bf16[64,1664]{1,0:T(8,128)(2,1)S(1)}, bf16[64,1664]{1,0:T(8,128)(2,1)S(1)}, u32[]{:S(2)}, u32[]{:S(2)}) %collective-permute-start.71) | collective-permute-done | bytes 213024 | tf_op jit(solution)/shard_map/ppermute | solution.py:943
  516.4 7.5 %shard_map.265 = f32[256,1024]{1,0:T(8,128)} custom-call(s32[4]{0:T(128)} %pad_add_fusion.ids.refs_0_, bf16[256,1024]{1,0:T(8,128)(2,1)} %get-tuple-element.270.dq_ref, f32[2,256,512]{2,1,0:T(8,128)} %convert_add_fusion.8.dkv_ref, f32[256,1024]{1,0:T(8,128)} %bitcast.215, f32[256,1024]{1,0:T(8,128)} %get-tuple-element.284.dx2_ref, f32[1,1024]{1,0:T(1,128)} %bitcast.266, ...), custom_call_target="tpu_custom_call" | custom-call | tf_op jit(solution)/shard_map/pallas_call | solution.py:41
  (383 shorter events, 206.3 us)
Async XLA Ops:
  39.4 49.0 %collective-permute-start.11 = (bf16[256,1664]{1,0:T(8,128)(2,1)S(1)}, bf16[256,1664]{1,0:T(8,128)(2,1)S(1)}, u32[]{:S(2)}, u32[]{:S(2)}) collective-permute-start(bf16[256,1664]{1,0:T(8,128)(2,1)S(1)} %get-tuple-element.156), channel_id=1, source_target_pairs={{0,24},{8,16},{16,8},{24,0},{1,25},{9,17},{17,9},{25,1},{2,26},{10... | collective-permute-start | bytes 2555912 | tf_op jit(solution)/shard_map/ppermute | solution.py:943
  41.8 46.5 %collective-permute-start.10 = (bf16[256,1664]{1,0:T(8,128)(2,1)S(1)}, bf16[256,1664]{1,0:T(8,128)(2,1)S(1)}, u32[]{:S(2)}, u32[]{:S(2)}) collective-permute-start(bf16[256,1664]{1,0:T(8,128)(2,1)S(1)} %get-tuple-element.156), channel_id=1, source_target_pairs={{0,16},{8,24},{16,0},{24,8},{1,17},{9,25},{17,1},{25,9},{2,18},{10... | collective-permute-start | bytes 2555912 | tf_op jit(solution)/shard_map/ppermute | solution.py:943
  42.4 46.0 %collective-permute-start.5 = (bf16[256,1664]{1,0:T(8,128)(2,1)S(1)}, bf16[256,1664]{1,0:T(8,128)(2,1)S(1)}, u32[]{:S(2)}, u32[]{:S(2)}) collective-permute-start(bf16[256,1664]{1,0:T(8,128)(2,1)S(1)} %get-tuple-element.156), channel_id=1, source_target_pairs={{0,8},{8,0},{16,24},{24,16},{1,9},{9,1},{17,25},{25,17},{2,10},{10... | collective-permute-start | bytes 2555912 | tf_op jit(solution)/shard_map/ppermute | solution.py:943
  60.5 27.9 %collective-permute-start.9 = (bf16[272,1024]{1,0:T(8,128)(2,1)S(1)}, bf16[272,1024]{1,0:T(8,128)(2,1)S(1)}, u32[]{:S(2)}, u32[]{:S(2)}) collective-permute-start(bf16[272,1024]{1,0:T(8,128)(2,1)S(1)} %get-tuple-element.173), channel_id=1, source_target_pairs={{0,4},{1,5},{2,6},{3,7},{4,0},{5,1},{6,2},{7,3},{8,12},{9,13},{10,... | collective-permute-start | bytes 1671176 | tf_op jit(solution)/shard_map/ppermute | solution.py:943
  98.8 29.0 %collective-permute-start.18 = (bf16[272,1024]{1,0:T(8,128)(2,1)S(1)}, bf16[272,1024]{1,0:T(8,128)(2,1)S(1)}, u32[]{:S(2)}, u32[]{:S(2)}) collective-permute-start(bf16[272,1024]{1,0:T(8,128)(2,1)S(1)} %copy-done.30), channel_id=1, source_target_pairs={{0,24},{8,16},{16,8},{24,0},{1,25},{9,17},{17,9},{25,1},{2,26},{10... | collective-permute-start | bytes 1671176 | tf_op jit(solution)/shard_map/ppermute | solution.py:943
  101.2 26.6 %collective-permute-start.17 = (bf16[272,1024]{1,0:T(8,128)(2,1)S(1)}, bf16[272,1024]{1,0:T(8,128)(2,1)S(1)}, u32[]{:S(2)}, u32[]{:S(2)}) collective-permute-start(bf16[272,1024]{1,0:T(8,128)(2,1)S(1)} %copy-done.30), channel_id=1, source_target_pairs={{0,16},{8,24},{16,0},{24,8},{1,17},{9,25},{17,1},{25,9},{2,18},{10... | collective-permute-start | bytes 1671176 | tf_op jit(solution)/shard_map/ppermute | solution.py:943
  127.8 34.9 %collective-permute-start.19 = (bf16[2,2,256,512]{3,2,1,0:T(8,128)(2,1)S(1)}, bf16[2,2,256,512]{3,2,1,0:T(8,128)(2,1)S(1)}, u32[]{:S(2)}, u32[]{:S(2)}) collective-permute-start(bf16[2,2,256,512]{3,2,1,0:T(8,128)(2,1)S(1)} %slice.315), channel_id=1, source_target_pairs={{0,2},{1,3},{2,0},{3,1},{4,6},{5,7},{6,4},{7,5},{8,10},{9,11},{10,... | collective-permute-start | bytes 3145736 | tf_op jit(solution)/shard_map/ppermute | solution.py:943
  128.2 27.6 %collective-permute-start.23 = (bf16[272,1024]{1,0:T(8,128)(2,1)S(1)}, bf16[272,1024]{1,0:T(8,128)(2,1)S(1)}, u32[]{:S(2)}, u32[]{:S(2)}) collective-permute-start(bf16[272,1024]{1,0:T(8,128)(2,1)S(1)} %copy-done.22), channel_id=1, source_target_pairs={{0,24},{8,16},{16,8},{24,0},{1,25},{9,17},{17,9},{25,1},{2,26},{10... | collective-permute-start | bytes 1671176 | tf_op jit(solution)/shard_map/ppermute | solution.py:943
  131.7 28.9 %collective-permute-start.20 = (bf16[2,1,256,512]{3,2,1,0:T(8,128)(2,1)S(1)}, bf16[2,1,256,512]{3,2,1,0:T(8,128)(2,1)}, u32[]{:S(2)}, u32[]{:S(2)}) collective-permute-start(bf16[2,1,256,512]{3,2,1,0:T(8,128)(2,1)S(1)} %copy-done.42), channel_id=1, source_target_pairs={{0,4},{1,5},{2,6},{3,7},{4,0},{5,1},{6,2},{7,3},{8,12},{9,13},{10,... | collective-permute-start | bytes 1572872 | tf_op jit(solution)/shard_map/ppermute | solution.py:943
  281.1 36.6 %collective-permute-start.42 = (bf16[2,3,256,512]{3,2,1,0:T(8,128)(2,1)}, bf16[2,3,256,512]{3,2,1,0:T(8,128)(2,1)S(1)}, u32[]{:S(2)}, u32[]{:S(2)}) collective-permute-start(bf16[2,3,256,512]{3,2,1,0:T(8,128)(2,1)} %get-tuple-element.222), channel_id=1, source_target_pairs={{0,2},{1,3},{2,0},{3,1},{4,6},{5,7},{6,4},{7,5},{8,10},{9,11},{10,... | collective-permute-start | bytes 4718600 | tf_op jit(solution)/shard_map/ppermute | solution.py:943
  287.7 30.0 %collective-permute-start.44 = (bf16[256,1024]{1,0:T(8,128)(2,1)S(1)}, bf16[256,1024]{1,0:T(8,128)(2,1)S(1)}, u32[]{:S(2)}, u32[]{:S(2)}) collective-permute-start(bf16[256,1024]{1,0:T(8,128)(2,1)S(1)} %get-tuple-element.328), channel_id=1, source_target_pairs={{0,24},{8,16},{16,8},{24,0},{1,25},{9,17},{17,9},{25,1},{2,26},{10... | collective-permute-start | bytes 1572872 | tf_op jit(solution)/shard_map/ppermute | solution.py:943
  289.5 28.3 %collective-permute-start.43 = (bf16[256,1024]{1,0:T(8,128)(2,1)S(1)}, bf16[256,1024]{1,0:T(8,128)(2,1)S(1)}, u32[]{:S(2)}, u32[]{:S(2)}) collective-permute-start(bf16[256,1024]{1,0:T(8,128)(2,1)S(1)} %get-tuple-element.329), channel_id=1, source_target_pairs={{0,16},{8,24},{16,0},{24,8},{1,17},{9,25},{17,1},{25,9},{2,18},{10... | collective-permute-start | bytes 1572872 | tf_op jit(solution)/shard_map/ppermute | solution.py:943
  290.7 27.0 %collective-permute-start.40 = (bf16[256,1024]{1,0:T(8,128)(2,1)S(1)}, bf16[256,1024]{1,0:T(8,128)(2,1)S(1)}, u32[]{:S(2)}, u32[]{:S(2)}) collective-permute-start(bf16[256,1024]{1,0:T(8,128)(2,1)S(1)} %get-tuple-element.327), channel_id=1, source_target_pairs={{0,8},{8,0},{16,24},{24,16},{1,9},{9,1},{17,25},{25,17},{2,10},{10... | collective-permute-start | bytes 1572872 | tf_op jit(solution)/shard_map/ppermute | solution.py:943
  318.1 27.2 %collective-permute-start.45 = (bf16[8,272,1024]{2,1,0:T(8,128)(2,1)S(1)}, bf16[8,272,1024]{2,1,0:T(8,128)(2,1)S(1)}, u32[]{:S(2)}, u32[]{:S(2)}) collective-permute-start(bf16[8,272,1024]{2,1,0:T(8,128)(2,1)S(1)} %copy-done.52), channel_id=1, source_target_pairs={{0,1},{1,0},{2,3},{3,2},{4,5},{5,4},{6,7},{7,6},{8,9},{9,8},{10,11... | collective-permute-start | bytes 13369352 | tf_op jit(solution)/shard_map/ppermute | solution.py:943
  358.6 29.6 %collective-permute-start.53 = (bf16[2,272,1024]{2,1,0:T(8,128)(2,1)}, bf16[2,272,1024]{2,1,0:T(8,128)(2,1)}, u32[]{:S(2)}, u32[]{:S(2)}) collective-permute-start(bf16[2,272,1024]{2,1,0:T(8,128)(2,1)} %pad_maximum_fusion.7), channel_id=1, source_target_pairs={{0,8},{8,0},{16,24},{24,16},{1,9},{9,1},{17,25},{25,17},{2,10},{10... | collective-permute-start | bytes 3342344 | tf_op jit(solution)/shard_map/ppermute | solution.py:943
  361.2 27.0 %collective-permute-start.54 = (bf16[2,272,1024]{2,1,0:T(8,128)(2,1)}, bf16[2,272,1024]{2,1,0:T(8,128)(2,1)}, u32[]{:S(2)}, u32[]{:S(2)}) collective-permute-start(bf16[2,272,1024]{2,1,0:T(8,128)(2,1)} %pad_maximum_fusion.8), channel_id=1, source_target_pairs={{0,16},{8,24},{16,0},{24,8},{1,17},{9,25},{17,1},{25,9},{2,18},{10... | collective-permute-start | bytes 3342344 | tf_op jit(solution)/shard_map/ppermute | solution.py:943
  388.2 48.1 %collective-permute-start.55 = (bf16[2,2,256,512]{3,2,1,0:T(8,128)(2,1)}, bf16[2,2,256,512]{3,2,1,0:T(8,128)(2,1)S(1)}, u32[]{:S(2)}, u32[]{:S(2)}) collective-permute-start(bf16[2,2,256,512]{3,2,1,0:T(8,128)(2,1)} %slice.330), channel_id=1, source_target_pairs={{0,4},{1,5},{2,6},{3,7},{4,0},{5,1},{6,2},{7,3},{8,12},{9,13},{10,... | collective-permute-start | bytes 3145736 | tf_op jit(solution)/shard_map/ppermute | solution.py:943
  390.5 45.9 %collective-permute-start.56 = (bf16[2,2,256,512]{3,2,1,0:T(8,128)(2,1)}, bf16[2,2,256,512]{3,2,1,0:T(8,128)(2,1)}, u32[]{:S(2)}, u32[]{:S(2)}) collective-permute-start(bf16[2,2,256,512]{3,2,1,0:T(8,128)(2,1)} %slice.270), channel_id=1, source_target_pairs={{0,2},{1,3},{2,0},{3,1},{4,6},{5,7},{6,4},{7,5},{8,10},{9,11},{10,... | collective-permute-start | bytes 3145736 | tf_op jit(solution)/shard_map/ppermute | solution.py:943
  391.9 30.9 %collective-permute-start.59 = (bf16[2,144,1024]{2,1,0:T(8,128)(2,1)}, bf16[2,144,1024]{2,1,0:T(8,128)(2,1)S(1)}, u32[]{:S(2)}, u32[]{:S(2)}) collective-permute-start(bf16[2,144,1024]{2,1,0:T(8,128)(2,1)} %pad_maximum_fusion.12), channel_id=1, source_target_pairs={{0,8},{8,0},{16,24},{24,16},{1,9},{9,1},{17,25},{25,17},{2,10},{10... | collective-permute-start | bytes 1769480 | tf_op jit(solution)/shard_map/ppermute | solution.py:943
  395.7 27.0 %collective-permute-start.58 = (bf16[272,1024]{1,0:T(8,128)(2,1)}, bf16[272,1024]{1,0:T(8,128)(2,1)S(1)}, u32[]{:S(2)}, u32[]{:S(2)}) collective-permute-start(bf16[272,1024]{1,0:T(8,128)(2,1)} %get-tuple-element.307), channel_id=1, source_target_pairs={{0,8},{8,0},{16,24},{24,16},{1,9},{9,1},{17,25},{25,17},{2,10},{10... | collective-permute-start | bytes 1671176 | tf_op jit(solution)/shard_map/ppermute | solution.py:943
  441.2 38.8 %collective-permute-start.62 = (bf16[272,1024]{1,0:T(8,128)(2,1)}, bf16[272,1024]{1,0:T(8,128)(2,1)}, u32[]{:S(2)}, u32[]{:S(2)}) collective-permute-start(bf16[272,1024]{1,0:T(8,128)(2,1)} %fusion.3), channel_id=1, source_target_pairs={{0,4},{1,5},{2,6},{3,7},{4,0},{5,1},{6,2},{7,3},{8,12},{9,13},{10,... | collective-permute-start | bytes 1671176 | tf_op jit(solution)/shard_map/ppermute | solution.py:943
  479.9 34.9 %collective-permute-start.68 = (bf16[2,256,512]{2,1,0:T(8,128)(2,1)S(1)}, bf16[2,256,512]{2,1,0:T(8,128)(2,1)S(1)}, u32[]{:S(2)}, u32[]{:S(2)}) collective-permute-start(bf16[2,256,512]{2,1,0:T(8,128)(2,1)S(1)} %add_convert_fusion.7), channel_id=1, source_target_pairs={{0,4},{1,5},{2,6},{3,7},{4,0},{5,1},{6,2},{7,3},{8,12},{9,13},{10,... | collective-permute-start | bytes 1572872 | tf_op jit(solution)/shard_map/ppermute | solution.py:943
  480.2 34.7 %collective-permute-start.69 = (bf16[2,256,512]{2,1,0:T(8,128)(2,1)S(1)}, bf16[2,256,512]{2,1,0:T(8,128)(2,1)S(1)}, u32[]{:S(2)}, u32[]{:S(2)}) collective-permute-start(bf16[2,256,512]{2,1,0:T(8,128)(2,1)S(1)} %get-tuple-element.279), channel_id=1, source_target_pairs={{0,2},{1,3},{2,0},{3,1},{4,6},{5,7},{6,4},{7,5},{8,10},{9,11},{10,... | collective-permute-start | bytes 1572872 | tf_op jit(solution)/shard_map/ppermute | solution.py:943
  492.7 42.0 %collective-permute-start.74 = (bf16[4,3,128,512]{3,2,1,0:T(8,128)(2,1)}, bf16[4,3,128,512]{3,2,1,0:T(8,128)(2,1)}, u32[]{:S(2)}, u32[]{:S(2)}) collective-permute-start(bf16[4,3,128,512]{3,2,1,0:T(8,128)(2,1)} %get-tuple-element.314), channel_id=1, source_target_pairs={{0,1},{1,0},{2,3},{3,2},{4,5},{5,4},{6,7},{7,6},{8,9},{9,8},{10,11... | collective-permute-start | bytes 4718600 | tf_op jit(solution)/shard_map/ppermute | solution.py:943
  (106 other events, 1721.7 us)

commit v6 on v5

--- a/solution.py
+++ b/solution.py
@@ -655,8 +655,10 @@
     dn2_out, rest = rest[:groups], rest[groups:]
     y_out, rest = rest[: groups // 2], rest[groups // 2 :]
     dw_out, rest = rest[:nz], rest[nz:]
-    n2_ref, c_ref, w_ref, x_rows, c_rows, gate_rows, grad_rows, inner_ref, dw_ref = rest[:9]
-    n2_sem, c_sem, w_sem, dn2_sem, y_sem, dw_sem = rest[9:]
+    n2_ref, c_ref, wide_ref, down_ref, x_rows, c_rows, gate_rows, grad_rows = rest[:8]
+    inner_ref, hg_ref, dwide_ref, ddown_ref = rest[8:12]
+    n2_sem, c_sem, w_sem, dn2_sem, y_sem, dw_sem = rest[12:]
+    hidden_size = down_ref.shape[-1]
     length = slot_ref.shape[-1]
     width = n2_ref.shape[-1]
     chunk = width // nz
@@ -668,16 +670,23 @@
     def c_copy(g):
         return pltpu.make_async_copy(c_in[g], c_ref.at[pl.ds(g * per, per)], c_sem.at[g])
 
-    def w_copy(n):
-        r, first, count = w_parts[n]
-        to = w_ref.at[:, pl.ds(first, count), span(z_chunk(ids, r, nz), chunk)]
-        return pltpu.make_async_copy(w_in[n], to, w_sem.at[n])
+    def matrix_of(k, wide, down, rows):
+        if k == 2:
+            return down.at[rows]
+        return wide.at[rows + (pl.ds(k * hidden_size, hidden_size),)]
+
+    def w_copy(n, i):
+        r, first, _ = w_parts[n]
+        rows = (slice(None), span(z_chunk(ids, r, nz), chunk))
+        to = matrix_of(first + i, wide_ref, down_ref, rows)
+        return pltpu.make_async_copy(w_in[n].at[:, i], to, w_sem.at[n, i])
 
     for g in range(groups):
         c_copy(g).start()
         n2_copy(g).start()
-    for n in range(len(w_parts)):
-        w_copy(n).start()
+    for n, (_, _, count) in enumerate(w_parts):
+        for i in range(count):
+            w_copy(n, i).start()
 
     def chosen_rows(i):
         places = lax.broadcasted_iota(jnp.int32, (CAP, length), 0).astype(F32)
@@ -704,19 +713,22 @@
         c_copy(g).wait()
         n2_copy(g).wait()
         lax.fori_loop(g * per, (g + 1) * per, gather, 0, unroll=True)
-    for n in range(len(w_parts)):
-        w_copy(n).wait()
-
-    def dw_copy(j, r):
-        rows = span(z_chunk(ids, r, nz), chunk)
-        return pltpu.make_async_copy(dw_ref.at[j, :, rows], dw_out[r].at[j], dw_sem.at[j, r])
+    for n, (_, _, count) in enumerate(w_parts):
+        for i in range(count):
+            w_copy(n, i).wait()
+
+    def dw_copy(j, r, k):
+        rows = (j, span(z_chunk(ids, r, nz), chunk))
+        source = matrix_of(k, dwide_ref, ddown_ref, rows)
+        return pltpu.make_async_copy(source, dw_out[r].at[j, k], dw_sem.at[j, r, k])
 
     for j in range(experts):
 
         def one_tile(i, _, j=j):
             at = pl.ds(pl.multiple_of(i * tile, tile), tile)
             x, c = x_rows[j, at], c_rows[j, at]
-            a, b, ch = dot(x, w_ref[j, 0]), dot(x, w_ref[j, 1]), dot(c, w_ref[j, 2])
+            wide, ch = dot(x, wide_ref[j]), dot(c, down_ref[j])
+            a, b = wide[:, :hidden_size], wide[:, hidden_size:]
             gate = gate_rows[j, at][:, :1]
             sig = 1.0 / (1.0 + jnp.exp(-a))
             act = a * sig
@@ -727,23 +739,23 @@
             dh = ch * gate
             da = (dh * b * sig * (1.0 + a * (1.0 - sig))).astype(BF)
             db = (dh * act).astype(BF)
-            inner_ref[0, at], inner_ref[1, at], inner_ref[2, at] = da, db, hg
+            inner_ref[at, :hidden_size], inner_ref[at, hidden_size:] = da, db
+            hg_ref[at] = hg
             return 0
 
         lax.fori_loop(0, blocks * CAP // tile, one_tile, 0)
         for part in range(width // chunk):
             cols = slice(part * chunk, (part + 1) * chunk)
+            dwide_ref[j, cols] = dot_tn(x_rows[j, :, cols], inner_ref[...]).astype(BF)
+            ddown_ref[j, cols] = dot_tn(c_rows[j, :, cols], hg_ref[...]).astype(BF)
+        for r in range(nz):
             for k in range(3):
-                x = (c_rows if k == 2 else x_rows)[j, :, cols]
-                dw_ref[j, k, cols] = dot_tn(x, inner_ref[k]).astype(BF)
-        for r in range(nz):
-            dw_copy(j, r).start()
+                dw_copy(j, r, k).start()
 
         def back_tile(i, _, j=j):
             at = pl.ds(pl.multiple_of(i * tile, tile), tile)
-            da, db, hg = inner_ref[0, at], inner_ref[1, at], inner_ref[2, at]
-            c_rows[j, at] = dot_nt(hg, w_ref[j, 2]).astype(BF)
-            x_rows[j, at] = (dot_nt(da, w_ref[j, 0]) + dot_nt(db, w_ref[j, 1])).astype(BF)
+            c_rows[j, at] = dot_nt(hg_ref[at], down_ref[j]).astype(BF)
+            x_rows[j, at] = dot_nt(inner_ref[at], wide_ref[j]).astype(BF)
             return 0
 
         lax.fori_loop(0, blocks * CAP // tile, back_tile, 0)
@@ -789,7 +801,8 @@
         y_copy(g).wait()
     for j in range(experts):
         for r in range(nz):
-            dw_copy(j, r).wait()
+            for k in range(3):
+                dw_copy(j, r, k).wait()
 
 
 def mixture(ids, slots, gates, n2_groups, c_groups, weights):
@@ -821,19 +834,22 @@
         [
             pltpu.VMEM((blocks, length, width), BF),
             pltpu.VMEM((blocks, high, width), BF),
-            pltpu.VMEM(matrices[:2] + (width,) + matrices[3:], BF),
+            pltpu.VMEM((experts, width, 2 * part[-1]), BF),
+            pltpu.VMEM((experts, width, part[-1]), BF),
             pltpu.VMEM((experts, rows, width), BF),
             pltpu.VMEM((experts, rows, width), BF),
             pltpu.VMEM((experts, rows, LANES), F32),
             pltpu.VMEM((experts, rows, LANES), F32),
-            pltpu.VMEM((3, rows, part[-1]), BF),
-            pltpu.VMEM(matrices[:2] + (width,) + matrices[3:], BF),
+            pltpu.VMEM((rows, 2 * part[-1]), BF),
+            pltpu.VMEM((rows, part[-1]), BF),
+            pltpu.VMEM((experts, width, 2 * part[-1]), BF),
+            pltpu.VMEM((experts, width, part[-1]), BF),
             pltpu.SemaphoreType.DMA((groups,)),
             pltpu.SemaphoreType.DMA((groups,)),
-            pltpu.SemaphoreType.DMA((len(flat),)),
+            pltpu.SemaphoreType.DMA((len(flat), 3)),
             pltpu.SemaphoreType.DMA((groups,)),
             pltpu.SemaphoreType.DMA((groups,)),
-            pltpu.SemaphoreType.DMA((experts, nz)),
+            pltpu.SemaphoreType.DMA((experts, nz, 3)),
         ],
     )
     return got[:groups], got[groups : groups + 2], got[groups + 2 :]

time: 545 us -> 545 us (level)
  no operation moved by 1% of the time
where the time goes in v6:
time: 545 us; the launch traced here: 540 us
  waiting for transfers between devices  221 us (41%)
  Pallas kernels  146 us (27%)
  starting transfers between devices  77.8 us (14%)
  other arithmetic  68.1 us (12%)
  local copies, waits for them, and re-layouts  24.8 us (5%)
    ppermute x75, waiting for transfers between devices, swap(): return lax.ppermute(value, axis, [(i, i ^ distance) for i in range(count)])  221 us
    pallas_call x10, Pallas kernels, call(): pl.pallas_call(kernel, grid_spec=pltpu.PrefetchScalarGridSpec(num_scalar_...  146 us
    ppermute x75, starting transfers between devices, swap(): return lax.ppermute(value, axis, [(i, i ^ distance) for i in range(count)])  77.8 us
    convert_element_type x13, other arithmetic, add_low(): return total.astype(BF)  15.8 us
  transfers between devices with their start and end apart: 75, of which 32 were waited for; matrix products, arithmetic and copies ran while one was open for 14% of the time, Pallas kernels for 17%

profile of v6, /device:TPU:0, one launch (start us, length us, event | category | flops | bytes accessed | tf_op | source)
XLA Modules:
  0.0 540.4 jit_solution(14619928817254336889)
XLA Ops:
  26.3 5.8 %collective-permute-done.3 = bf16[64,1664]{1,0:T(8,128)(2,1)S(1)} collective-permute-done((bf16[64,1664]{1,0:T(8,128)(2,1)}, bf16[64,1664]{1,0:T(8,128)(2,1)S(1)}, u32[]{:S(2)}, u32[]{:S(2)}) %collective-permute-start.3) | collective-permute-done | bytes 213024 | tf_op jit(solution)/shard_map/ppermute | solution.py:959
  42.9 17.0 %collective-permute-done.7 = bf16[256,1024]{1,0:T(8,128)(2,1)S(1)} collective-permute-done((bf16[256,1024]{1,0:T(8,128)(2,1)S(1)}, bf16[256,1024]{1,0:T(8,128)(2,1)S(1)}, u32[]{:S(2)}, u32[]{:S(2)}) %collective-permute-start.7) | collective-permute-done | bytes 524320 | tf_op jit(solution)/shard_map/ppermute | solution.py:959
  65.1 18.6 %collective-permute-done.8 = bf16[256,1024]{1,0:T(8,128)(2,1)S(1)} collective-permute-done((bf16[256,1024]{1,0:T(8,128)(2,1)S(1)}, bf16[256,1024]{1,0:T(8,128)(2,1)S(1)}, u32[]{:S(2)}, u32[]{:S(2)}) %collective-permute-start.8) | collective-permute-done | bytes 524320 | tf_op jit(solution)/shard_map/ppermute | solution.py:959
  105.3 14.6 %shard_map.256 = (bf16[256,1024]{1,0:T(8,128)(2,1)}, bf16[2048,512]{1,0:T(8,128)(2,1)}, bf16[2048,512]{1,0:T(8,128)(2,1)}, f32[2048,128]{1,0:T(8,128)}, f32[2048,128]{1,0:T(8,128)}) custom-call(s32[4]{0:T(128)} %pad_add_fusion.ids.refs_0_, bf16[1024,1024]{1,0:T(8,128)(2,1)} %bitcast.58.own_ref.own_rows, bf16[1024,1024]{1,0:T(8,128)(2,1)} %bitcast.59.other_ref.other_rows, ...), custom_call_target="tpu_custom_call" | custom-call | tf_op jit(solution)/shard_map/pallas_call | solution.py:41
  119.9 6.7 %collective-permute-done.14.rest_9_ = bf16[2,1,256,512]{3,2,1,0:T(8,128)(2,1)S(1)} collective-permute-done((bf16[2,1,256,512]{3,2,1,0:T(8,128)(2,1)}, bf16[2,1,256,512]{3,2,1,0:T(8,128)(2,1)S(1)}, u32[]{:S(2)}, u32[]{:S(2)}) %collective-permute-start.14) | collective-permute-done | bytes 524320 | tf_op jit(solution)/shard_map/ppermute | solution.py:959
  134.3 16.7 %shard_map.257 = (f32[256,1024]{1,0:T(8,128)}, bf16[256,1024]{1,0:T(8,128)(2,1)}, f32[4,256,128]{2,1,0:T(8,128)}) custom-call(s32[4]{0:T(128)} %pad_add_fusion.ids.refs_0_, bf16[256,1024]{1,0:T(8,128)(2,1)} %get-tuple-element.174.q_ref.refs_1_, bf16[2048,512]{1,0:T(8,128)(2,1)} %get-tuple-element.175.k_ref.refs_5_, ...), custom_call_target="tpu_custom_call" | custom-call | tf_op jit(solution)/shard_map/pallas_call | solution.py:41
  155.9 4.8 collective-permute-done.20.rest_12_
  169.0 12.6 %collective-permute-done.25.rest_14_ = bf16[2,1,256,512]{3,2,1,0:T(8,128)(2,1)S(1)} collective-permute-done((bf16[2,1,256,512]{3,2,1,0:T(8,128)(2,1)S(1)}, bf16[2,1,256,512]{3,2,1,0:T(8,128)(2,1)S(1)}, u32[]{:S(2)}, u32[]{:S(2)}) %collective-permute-start.25) | collective-permute-done | bytes 524320 | tf_op jit(solution)/shard_map/ppermute | solution.py:959
  181.6 6.0 %collective-permute-done.27 = bf16[256,1024]{1,0:T(8,128)(2,1)S(1)} collective-permute-done((bf16[256,1024]{1,0:T(8,128)(2,1)}, bf16[256,1024]{1,0:T(8,128)(2,1)S(1)}, u32[]{:S(2)}, u32[]{:S(2)}) %collective-permute-start.27) | collective-permute-done | bytes 524320 | tf_op jit(solution)/shard_map/ppermute | solution.py:959
  200.4 16.1 %collective-permute-done.29.rest_13_ = bf16[2,1,256,512]{3,2,1,0:T(8,128)(2,1)S(1)} collective-permute-done((bf16[2,1,256,512]{3,2,1,0:T(8,128)(2,1)}, bf16[2,1,256,512]{3,2,1,0:T(8,128)(2,1)S(1)}, u32[]{:S(2)}, u32[]{:S(2)}) %collective-permute-start.29) | collective-permute-done | bytes 524320 | tf_op jit(solution)/shard_map/ppermute | solution.py:959
  227.2 7.2 %collective-permute-done.38.rest_16_ = bf16[2,1,256,512]{3,2,1,0:T(8,128)(2,1)S(1)} collective-permute-done((bf16[2,1,256,512]{3,2,1,0:T(8,128)(2,1)}, bf16[2,1,256,512]{3,2,1,0:T(8,128)(2,1)S(1)}, u32[]{:S(2)}, u32[]{:S(2)}) %collective-permute-start.38) | collective-permute-done | bytes 524320 | tf_op jit(solution)/shard_map/ppermute | solution.py:959
  235.1 45.8 %shard_map.259 = (bf16[4,256,1024]{2,1,0:T(8,128)(2,1)}, bf16[4,256,1024]{2,1,0:T(8,128)(2,1)}, bf16[4,256,1024]{2,1,0:T(8,128)(2,1)}, bf16[4,256,1024]{2,1,0:T(...) custom-call(s32[4]{0:T(128)} %pad_add_fusion.ids.refs_0_, ...), custom_call_target="tpu_custom_call" | custom-call | tf_op jit(solution)/shard_map/pallas_call | solution.py:41
  292.6 25.5 %collective-permute-done.42 = bf16[2,3,256,512]{3,2,1,0:T(8,128)(2,1)S(1)} collective-permute-done((bf16[2,3,256,512]{3,2,1,0:T(8,128)(2,1)}, bf16[2,3,256,512]{3,2,1,0:T(8,128)(2,1)S(1)}, u32[]{:S(2)}, u32[]{:S(2)}) %collective-permute-start.42) | collective-permute-done | bytes 1572896 | tf_op jit(solution)/shard_map/ppermute | solution.py:959
  326.1 19.6 %collective-permute-done.47 = bf16[256,1024]{1,0:T(8,128)(2,1)S(1)} collective-permute-done((bf16[256,1024]{1,0:T(8,128)(2,1)S(1)}, bf16[256,1024]{1,0:T(8,128)(2,1)S(1)}, u32[]{:S(2)}, u32[]{:S(2)}) %collective-permute-start.47) | collective-permute-done | bytes 524320 | tf_op jit(solution)/shard_map/ppermute | solution.py:959
  350.8 6.9 %shard_map.260 = (f32[256,1024]{1,0:T(8,128)}, bf16[256,1024]{1,0:T(8,128)(2,1)}, bf16[4,144,1024]{2,1,0:T(8,128)(2,1)}, bf16[4,144,1024]{2,1,0:T(8,128)(2,1)}) custom-call(s32[4]{0:T(128)} %pad_add_fusion.ids.refs_0_, f32[256,1024]{1,0:T(8,128)} %bitcast.223, f32[256,1024]{1,0:T(8,128)} %get-tuple-element.179.x2_ref, f32[1,1024]{1,0:T(1,128)} %bitcast.268, ...), custom_call_target="tpu_custom_call" | custom-call | tf_op jit(solution)/shard_map/pallas_call | solution.py:41
  367.6 15.7 %shard_map.261 = (bf16[256,1024]{1,0:T(8,128)(2,1)}, bf16[2,1024,512]{2,1,0:T(8,128)(2,1)}, bf16[2,1024,512]{2,1,0:T(8,128)(2,1)}) custom-call(s32[4]{0:T(128)} %pad_add_fusion.ids.refs_0_, bf16[256,1024]{1,0:T(8,128)(2,1)} %get-tuple-element.174.q_ref.refs_1_, bf16[256,1024]{1,0:T(8,128)(2,1)} %get-tuple-element.254.do_ref.refs_2_, ...), custom_call_target="tpu_custom_call" | custom-call | tf_op jit(solution)/shard_map/pallas_call | solution.py:41
  383.2 5.2 collective-permute-done.51
  398.0 9.1 %shard_map.262 = bf16[4,256,1024]{2,1,0:T(8,128)(2,1)} custom-call(s32[4]{0:T(128)} %pad_add_fusion.ids.refs_0_, bf16[1024,1024]{1,0:T(8,128)(2,1)} %bitcast.58.own_ref.own_rows, bf16[1024,1024]{1,0:T(8,128)(2,1)} %bitcast.59.other_ref.other_rows, f32[1,1024]{1,0:T(1,128)} %bitcast.264, bf16[256,1024]{1,0:T(8,128)(2,1)} %get-tuple-element.255.dq_ref.refs_11_, ...), custom_call_target="tpu_custom_call" | custom-call | tf_op jit(solution)/shard_map/pallas_call | solution.py:41
  407.1 15.9 %shard_map.263 = (bf16[256,1024]{1,0:T(8,128)(2,1)}, bf16[2,1024,512]{2,1,0:T(8,128)(2,1)}, bf16[2,1024,512]{2,1,0:T(8,128)(2,1)}) custom-call(s32[4]{0:T(128)} %pad_add_fusion.ids.refs_0_, bf16[256,1024]{1,0:T(8,128)(2,1)} %get-tuple-element.174.q_ref.refs_1_, ...), custom_call_target="tpu_custom_call", output_to_operand_aliasing={{0}: (11, {}), {1}: (12, {}), {2}: (13, {})} | custom-call | tf_op jit(solution)/shard_map/pallas_call | solution.py:41
  423.1 13.6 %collective-permute-done.55 = bf16[2,2,256,512]{3,2,1,0:T(8,128)(2,1)S(1)} collective-permute-done((bf16[2,2,256,512]{3,2,1,0:T(8,128)(2,1)}, bf16[2,2,256,512]{3,2,1,0:T(8,128)(2,1)S(1)}, u32[]{:S(2)}, u32[]{:S(2)}) %collective-permute-start.55) | collective-permute-done | bytes 1048608 | tf_op jit(solution)/shard_map/ppermute | solution.py:959
  448.3 9.3 %shard_map.264 = bf16[4,256,1024]{2,1,0:T(8,128)(2,1)} custom-call(s32[4]{0:T(128)} %pad_add_fusion.ids.refs_0_, bf16[1024,1024]{1,0:T(8,128)(2,1)} %bitcast.58.own_ref.own_rows, bf16[1024,1024]{1,0:T(8,128)(2,1)} %bitcast.59.other_ref.other_rows, f32[1,1024]{1,0:T(1,128)} %bitcast.265, bf16[256,1024]{1,0:T(8,128)(2,1)} %get-tuple-element.270.dq_ref, ...), custom_call_target="tpu_custom_call" | custom-call | tf_op jit(solution)/shard_map/pallas_call | solution.py:41
  466.6 13.5 %collective-permute-done.61 = bf16[2,256,512]{2,1,0:T(8,128)(2,1)S(1)} collective-permute-done((bf16[2,256,512]{2,1,0:T(8,128)(2,1)S(1)}, bf16[2,256,512]{2,1,0:T(8,128)(2,1)S(1)}, u32[]{:S(2)}, u32[]{:S(2)}) %collective-permute-start.61) | collective-permute-done | bytes 524320 | tf_op jit(solution)/shard_map/ppermute | solution.py:959
  493.0 18.4 %collective-permute-done.71 = bf16[64,1664]{1,0:T(8,128)(2,1)S(1)} collective-permute-done((bf16[64,1664]{1,0:T(8,128)(2,1)S(1)}, bf16[64,1664]{1,0:T(8,128)(2,1)S(1)}, u32[]{:S(2)}, u32[]{:S(2)}) %collective-permute-start.71) | collective-permute-done | bytes 213024 | tf_op jit(solution)/shard_map/ppermute | solution.py:959
  516.8 7.5 %shard_map.265 = f32[256,1024]{1,0:T(8,128)} custom-call(s32[4]{0:T(128)} %pad_add_fusion.ids.refs_0_, bf16[256,1024]{1,0:T(8,128)(2,1)} %get-tuple-element.270.dq_ref, f32[2,256,512]{2,1,0:T(8,128)} %convert_add_fusion.8.dkv_ref, f32[256,1024]{1,0:T(8,128)} %bitcast.215, f32[256,1024]{1,0:T(8,128)} %get-tuple-element.284.dx2_ref, f32[1,1024]{1,0:T(1,128)} %bitcast.266, ...), custom_call_target="tpu_custom_call" | custom-call | tf_op jit(solution)/shard_map/pallas_call | solution.py:41
  (383 shorter events, 206.3 us)
Async XLA Ops:
  39.4 49.0 %collective-permute-start.11 = (bf16[256,1664]{1,0:T(8,128)(2,1)S(1)}, bf16[256,1664]{1,0:T(8,128)(2,1)S(1)}, u32[]{:S(2)}, u32[]{:S(2)}) collective-permute-start(bf16[256,1664]{1,0:T(8,128)(2,1)S(1)} %get-tuple-element.156), channel_id=1, source_target_pairs={{0,24},{8,16},{16,8},{24,0},{1,25},{9,17},{17,9},{25,1},{2,26},{10... | collective-permute-start | bytes 2555912 | tf_op jit(solution)/shard_map/ppermute | solution.py:959
  41.8 46.5 %collective-permute-start.10 = (bf16[256,1664]{1,0:T(8,128)(2,1)S(1)}, bf16[256,1664]{1,0:T(8,128)(2,1)S(1)}, u32[]{:S(2)}, u32[]{:S(2)}) collective-permute-start(bf16[256,1664]{1,0:T(8,128)(2,1)S(1)} %get-tuple-element.156), channel_id=1, source_target_pairs={{0,16},{8,24},{16,0},{24,8},{1,17},{9,25},{17,1},{25,9},{2,18},{10... | collective-permute-start | bytes 2555912 | tf_op jit(solution)/shard_map/ppermute | solution.py:959
  42.4 46.0 %collective-permute-start.5 = (bf16[256,1664]{1,0:T(8,128)(2,1)S(1)}, bf16[256,1664]{1,0:T(8,128)(2,1)S(1)}, u32[]{:S(2)}, u32[]{:S(2)}) collective-permute-start(bf16[256,1664]{1,0:T(8,128)(2,1)S(1)} %get-tuple-element.156), channel_id=1, source_target_pairs={{0,8},{8,0},{16,24},{24,16},{1,9},{9,1},{17,25},{25,17},{2,10},{10... | collective-permute-start | bytes 2555912 | tf_op jit(solution)/shard_map/ppermute | solution.py:959
  60.5 27.9 %collective-permute-start.9 = (bf16[272,1024]{1,0:T(8,128)(2,1)S(1)}, bf16[272,1024]{1,0:T(8,128)(2,1)S(1)}, u32[]{:S(2)}, u32[]{:S(2)}) collective-permute-start(bf16[272,1024]{1,0:T(8,128)(2,1)S(1)} %get-tuple-element.173), channel_id=1, source_target_pairs={{0,4},{1,5},{2,6},{3,7},{4,0},{5,1},{6,2},{7,3},{8,12},{9,13},{10,... | collective-permute-start | bytes 1671176 | tf_op jit(solution)/shard_map/ppermute | solution.py:959
  98.8 29.0 %collective-permute-start.18 = (bf16[272,1024]{1,0:T(8,128)(2,1)S(1)}, bf16[272,1024]{1,0:T(8,128)(2,1)S(1)}, u32[]{:S(2)}, u32[]{:S(2)}) collective-permute-start(bf16[272,1024]{1,0:T(8,128)(2,1)S(1)} %copy-done.30), channel_id=1, source_target_pairs={{0,24},{8,16},{16,8},{24,0},{1,25},{9,17},{17,9},{25,1},{2,26},{10... | collective-permute-start | bytes 1671176 | tf_op jit(solution)/shard_map/ppermute | solution.py:959
  101.2 26.6 %collective-permute-start.17 = (bf16[272,1024]{1,0:T(8,128)(2,1)S(1)}, bf16[272,1024]{1,0:T(8,128)(2,1)S(1)}, u32[]{:S(2)}, u32[]{:S(2)}) collective-permute-start(bf16[272,1024]{1,0:T(8,128)(2,1)S(1)} %copy-done.30), channel_id=1, source_target_pairs={{0,16},{8,24},{16,0},{24,8},{1,17},{9,25},{17,1},{25,9},{2,18},{10... | collective-permute-start | bytes 1671176 | tf_op jit(solution)/shard_map/ppermute | solution.py:959
  127.8 34.9 %collective-permute-start.19 = (bf16[2,2,256,512]{3,2,1,0:T(8,128)(2,1)S(1)}, bf16[2,2,256,512]{3,2,1,0:T(8,128)(2,1)S(1)}, u32[]{:S(2)}, u32[]{:S(2)}) collective-permute-start(bf16[2,2,256,512]{3,2,1,0:T(8,128)(2,1)S(1)} %slice.315), channel_id=1, source_target_pairs={{0,2},{1,3},{2,0},{3,1},{4,6},{5,7},{6,4},{7,5},{8,10},{9,11},{10,... | collective-permute-start | bytes 3145736 | tf_op jit(solution)/shard_map/ppermute | solution.py:959
  128.2 27.6 %collective-permute-start.23 = (bf16[272,1024]{1,0:T(8,128)(2,1)S(1)}, bf16[272,1024]{1,0:T(8,128)(2,1)S(1)}, u32[]{:S(2)}, u32[]{:S(2)}) collective-permute-start(bf16[272,1024]{1,0:T(8,128)(2,1)S(1)} %copy-done.22), channel_id=1, source_target_pairs={{0,24},{8,16},{16,8},{24,0},{1,25},{9,17},{17,9},{25,1},{2,26},{10... | collective-permute-start | bytes 1671176 | tf_op jit(solution)/shard_map/ppermute | solution.py:959
  131.7 28.9 %collective-permute-start.20 = (bf16[2,1,256,512]{3,2,1,0:T(8,128)(2,1)S(1)}, bf16[2,1,256,512]{3,2,1,0:T(8,128)(2,1)}, u32[]{:S(2)}, u32[]{:S(2)}) collective-permute-start(bf16[2,1,256,512]{3,2,1,0:T(8,128)(2,1)S(1)} %copy-done.42), channel_id=1, source_target_pairs={{0,4},{1,5},{2,6},{3,7},{4,0},{5,1},{6,2},{7,3},{8,12},{9,13},{10,... | collective-permute-start | bytes 1572872 | tf_op jit(solution)/shard_map/ppermute | solution.py:959
  281.5 36.6 %collective-permute-start.42 = (bf16[2,3,256,512]{3,2,1,0:T(8,128)(2,1)}, bf16[2,3,256,512]{3,2,1,0:T(8,128)(2,1)S(1)}, u32[]{:S(2)}, u32[]{:S(2)}) collective-permute-start(bf16[2,3,256,512]{3,2,1,0:T(8,128)(2,1)} %get-tuple-element.222), channel_id=1, source_target_pairs={{0,2},{1,3},{2,0},{3,1},{4,6},{5,7},{6,4},{7,5},{8,10},{9,11},{10,... | collective-permute-start | bytes 4718600 | tf_op jit(solution)/shard_map/ppermute | solution.py:959
  288.0 30.0 %collective-permute-start.44 = (bf16[256,1024]{1,0:T(8,128)(2,1)S(1)}, bf16[256,1024]{1,0:T(8,128)(2,1)S(1)}, u32[]{:S(2)}, u32[]{:S(2)}) collective-permute-start(bf16[256,1024]{1,0:T(8,128)(2,1)S(1)} %get-tuple-element.328), channel_id=1, source_target_pairs={{0,24},{8,16},{16,8},{24,0},{1,25},{9,17},{17,9},{25,1},{2,26},{10... | collective-permute-start | bytes 1572872 | tf_op jit(solution)/shard_map/ppermute | solution.py:959
  289.8 28.3 %collective-permute-start.43 = (bf16[256,1024]{1,0:T(8,128)(2,1)S(1)}, bf16[256,1024]{1,0:T(8,128)(2,1)S(1)}, u32[]{:S(2)}, u32[]{:S(2)}) collective-permute-start(bf16[256,1024]{1,0:T(8,128)(2,1)S(1)} %get-tuple-element.329), channel_id=1, source_target_pairs={{0,16},{8,24},{16,0},{24,8},{1,17},{9,25},{17,1},{25,9},{2,18},{10... | collective-permute-start | bytes 1572872 | tf_op jit(solution)/shard_map/ppermute | solution.py:959
  291.0 27.0 %collective-permute-start.40 = (bf16[256,1024]{1,0:T(8,128)(2,1)S(1)}, bf16[256,1024]{1,0:T(8,128)(2,1)S(1)}, u32[]{:S(2)}, u32[]{:S(2)}) collective-permute-start(bf16[256,1024]{1,0:T(8,128)(2,1)S(1)} %get-tuple-element.327), channel_id=1, source_target_pairs={{0,8},{8,0},{16,24},{24,16},{1,9},{9,1},{17,25},{25,17},{2,10},{10... | collective-permute-start | bytes 1572872 | tf_op jit(solution)/shard_map/ppermute | solution.py:959
  318.5 27.2 %collective-permute-start.45 = (bf16[8,272,1024]{2,1,0:T(8,128)(2,1)S(1)}, bf16[8,272,1024]{2,1,0:T(8,128)(2,1)S(1)}, u32[]{:S(2)}, u32[]{:S(2)}) collective-permute-start(bf16[8,272,1024]{2,1,0:T(8,128)(2,1)S(1)} %copy-done.52), channel_id=1, source_target_pairs={{0,1},{1,0},{2,3},{3,2},{4,5},{5,4},{6,7},{7,6},{8,9},{9,8},{10,11... | collective-permute-start | bytes 13369352 | tf_op jit(solution)/shard_map/ppermute | solution.py:959
  359.0 29.6 %collective-permute-start.53 = (bf16[2,272,1024]{2,1,0:T(8,128)(2,1)}, bf16[2,272,1024]{2,1,0:T(8,128)(2,1)}, u32[]{:S(2)}, u32[]{:S(2)}) collective-permute-start(bf16[2,272,1024]{2,1,0:T(8,128)(2,1)} %pad_maximum_fusion.7), channel_id=1, source_target_pairs={{0,8},{8,0},{16,24},{24,16},{1,9},{9,1},{17,25},{25,17},{2,10},{10... | collective-permute-start | bytes 3342344 | tf_op jit(solution)/shard_map/ppermute | solution.py:959
  361.6 27.0 %collective-permute-start.54 = (bf16[2,272,1024]{2,1,0:T(8,128)(2,1)}, bf16[2,272,1024]{2,1,0:T(8,128)(2,1)}, u32[]{:S(2)}, u32[]{:S(2)}) collective-permute-start(bf16[2,272,1024]{2,1,0:T(8,128)(2,1)} %pad_maximum_fusion.8), channel_id=1, source_target_pairs={{0,16},{8,24},{16,0},{24,8},{1,17},{9,25},{17,1},{25,9},{2,18},{10... | collective-permute-start | bytes 3342344 | tf_op jit(solution)/shard_map/ppermute | solution.py:959
  388.6 48.1 %collective-permute-start.55 = (bf16[2,2,256,512]{3,2,1,0:T(8,128)(2,1)}, bf16[2,2,256,512]{3,2,1,0:T(8,128)(2,1)S(1)}, u32[]{:S(2)}, u32[]{:S(2)}) collective-permute-start(bf16[2,2,256,512]{3,2,1,0:T(8,128)(2,1)} %slice.330), channel_id=1, source_target_pairs={{0,4},{1,5},{2,6},{3,7},{4,0},{5,1},{6,2},{7,3},{8,12},{9,13},{10,... | collective-permute-start | bytes 3145736 | tf_op jit(solution)/shard_map/ppermute | solution.py:959
  390.8 45.9 %collective-permute-start.56 = (bf16[2,2,256,512]{3,2,1,0:T(8,128)(2,1)}, bf16[2,2,256,512]{3,2,1,0:T(8,128)(2,1)}, u32[]{:S(2)}, u32[]{:S(2)}) collective-permute-start(bf16[2,2,256,512]{3,2,1,0:T(8,128)(2,1)} %slice.270), channel_id=1, source_target_pairs={{0,2},{1,3},{2,0},{3,1},{4,6},{5,7},{6,4},{7,5},{8,10},{9,11},{10,... | collective-permute-start | bytes 3145736 | tf_op jit(solution)/shard_map/ppermute | solution.py:959
  392.2 30.9 %collective-permute-start.59 = (bf16[2,144,1024]{2,1,0:T(8,128)(2,1)}, bf16[2,144,1024]{2,1,0:T(8,128)(2,1)S(1)}, u32[]{:S(2)}, u32[]{:S(2)}) collective-permute-start(bf16[2,144,1024]{2,1,0:T(8,128)(2,1)} %pad_maximum_fusion.12), channel_id=1, source_target_pairs={{0,8},{8,0},{16,24},{24,16},{1,9},{9,1},{17,25},{25,17},{2,10},{10... | collective-permute-start | bytes 1769480 | tf_op jit(solution)/shard_map/ppermute | solution.py:959
  396.0 27.0 %collective-permute-start.58 = (bf16[272,1024]{1,0:T(8,128)(2,1)}, bf16[272,1024]{1,0:T(8,128)(2,1)S(1)}, u32[]{:S(2)}, u32[]{:S(2)}) collective-permute-start(bf16[272,1024]{1,0:T(8,128)(2,1)} %get-tuple-element.307), channel_id=1, source_target_pairs={{0,8},{8,0},{16,24},{24,16},{1,9},{9,1},{17,25},{25,17},{2,10},{10... | collective-permute-start | bytes 1671176 | tf_op jit(solution)/shard_map/ppermute | solution.py:959
  441.5 38.8 %collective-permute-start.62 = (bf16[272,1024]{1,0:T(8,128)(2,1)}, bf16[272,1024]{1,0:T(8,128)(2,1)}, u32[]{:S(2)}, u32[]{:S(2)}) collective-permute-start(bf16[272,1024]{1,0:T(8,128)(2,1)} %fusion.3), channel_id=1, source_target_pairs={{0,4},{1,5},{2,6},{3,7},{4,0},{5,1},{6,2},{7,3},{8,12},{9,13},{10,... | collective-permute-start | bytes 1671176 | tf_op jit(solution)/shard_map/ppermute | solution.py:959
  480.3 34.9 %collective-permute-start.68 = (bf16[2,256,512]{2,1,0:T(8,128)(2,1)S(1)}, bf16[2,256,512]{2,1,0:T(8,128)(2,1)S(1)}, u32[]{:S(2)}, u32[]{:S(2)}) collective-permute-start(bf16[2,256,512]{2,1,0:T(8,128)(2,1)S(1)} %add_convert_fusion.7), channel_id=1, source_target_pairs={{0,4},{1,5},{2,6},{3,7},{4,0},{5,1},{6,2},{7,3},{8,12},{9,13},{10,... | collective-permute-start | bytes 1572872 | tf_op jit(solution)/shard_map/ppermute | solution.py:959
  480.5 34.7 %collective-permute-start.69 = (bf16[2,256,512]{2,1,0:T(8,128)(2,1)S(1)}, bf16[2,256,512]{2,1,0:T(8,128)(2,1)S(1)}, u32[]{:S(2)}, u32[]{:S(2)}) collective-permute-start(bf16[2,256,512]{2,1,0:T(8,128)(2,1)S(1)} %get-tuple-element.279), channel_id=1, source_target_pairs={{0,2},{1,3},{2,0},{3,1},{4,6},{5,7},{6,4},{7,5},{8,10},{9,11},{10,... | collective-permute-start | bytes 1572872 | tf_op jit(solution)/shard_map/ppermute | solution.py:959
  493.0 42.0 %collective-permute-start.74 = (bf16[4,3,128,512]{3,2,1,0:T(8,128)(2,1)}, bf16[4,3,128,512]{3,2,1,0:T(8,128)(2,1)}, u32[]{:S(2)}, u32[]{:S(2)}) collective-permute-start(bf16[4,3,128,512]{3,2,1,0:T(8,128)(2,1)} %get-tuple-element.314), channel_id=1, source_target_pairs={{0,1},{1,0},{2,3},{3,2},{4,5},{5,4},{6,7},{7,6},{8,9},{9,8},{10,11... | collective-permute-start | bytes 4718600 | tf_op jit(solution)/shard_map/ppermute | solution.py:959
  (106 other events, 1721.8 us)
